TPU v7x, 128 devices: a whole 4x4x4 slice. The times are simulated.
128 devices in a mesh: ctx: 64 (over x, z, y), wa: 2 (over core).
Axes of the slice: x: 4, y: 4, z: 4, core: 2. Of those that a mesh axis runs over, the one named last changes fastest.
Arguments:
- tokens: bfloat16 [8192, 1600], P('ctx'), may hold values from -6 to 6
- norm_gain: float32 [1600], replicated, may hold values from 0.25 to 1.75
- qkv_weight: bfloat16 [1600, 2240], P('ctx'), may hold values from -0.15625 to 0.15625
- heads_gain: float32 [1600], replicated, may hold values from 0.25 to 1.75
- mamba_in: bfloat16 [1600, 2, 3200], P('ctx', None, 'wa'), may hold values from -0.15625 to 0.15625
- conv_weight: bfloat16 [4, 3200], P(None, 'wa'), may hold values from -3 to 3
- conv_bias: float32 [3200], P('wa'), may hold values from -4 to 4
- state_proj: bfloat16 [3200, 132], P('wa'), may hold values from -0.109375 to 0.109375
- step_proj: bfloat16 [100, 3200], P(None, 'wa'), may hold values from -0.625 to 0.625
- step_bias: float32 [3200], P('wa'), may hold values from -4 to 0
- decay_log: float32 [3200, 16], P('wa'), may hold values from -9 to 0
- skip_gain: float32 [3200], P('wa'), may hold values from 0.5 to 3
- mamba_gain: float32 [3200], P('wa'), may hold values from 0.25 to 1.75
- heads_out: bfloat16 [1600, 1600], P('ctx', 'wa'), may hold values from -0.15625 to 0.15625
- mamba_out: bfloat16 [1600, 3200], P('ctx', 'wa'), may hold values from -0.109375 to 0.109375
- mlp_gain: float32 [1600], replicated, may hold values from 0.25 to 1.75
- gate_up: bfloat16 [1600, 2, 5504], P('ctx', None, 'wa'), may hold values from -0.15625 to 0.15625
- down_proj: bfloat16 [1600, 5504], P('ctx', 'wa'), may hold values from -0.078125 to 0.078125
- cotangent: bfloat16 [8192, 1600], P('ctx'), may hold values from -16 to 16
Outputs:
- layer_out: bfloat16 [8192, 1600], P('ctx')
- tokens_grad: float32 [8192, 1600], P('ctx')
- norm_gain_grad: float32 [1600], replicated
- qkv_weight_grad: float32 [1600, 2240], P('ctx')
- heads_gain_grad: float32 [1600], replicated
- mamba_in_grad: float32 [1600, 2, 3200], P('ctx', None, 'wa')
- conv_weight_grad: float32 [4, 3200], P(None, 'wa')
- conv_bias_grad: float32 [3200], P('wa')
- state_proj_grad: float32 [3200, 132], P('wa')
- step_proj_grad: float32 [100, 3200], P(None, 'wa')
- step_bias_grad: float32 [3200], P('wa')
- decay_log_grad: float32 [3200, 16], P('wa')
- skip_gain_grad: float32 [3200], P('wa')
- mamba_gain_grad: float32 [3200], P('wa')
- heads_out_grad: float32 [1600, 1600], P('ctx', 'wa')
- mamba_out_grad: float32 [1600, 3200], P('ctx', 'wa')
- mlp_gain_grad: float32 [1600], replicated
- gate_up_grad: float32 [1600, 2, 5504], P('ctx', None, 'wa')
- down_proj_grad: float32 [1600, 5504], P('ctx', 'wa')
All inputs are finite; a program needn't handle non-finite values.
Results may differ from a plain program's by a relative error of at most 0.014.
Values may be sent and summed in bfloat16 or wider, within the bound.
No kernel may reach another device: no remote copies, remote signals or barrier semaphores. Data moves between devices by JAX's collectives and lax.ppermute only.
A program may use at most 576 MiB of HBM per device.

v0:
```python
import jax
import jax.numpy as jnp
from jax import lax
from jax.sharding import PartitionSpec as P

KV_HEADS = 5
GROUP = 5
HEAD = 64
INNER = 3200
STATE = 16
CONV = 4
WINDOW = 1024


epsilon = 1e-06


def shortened(shard):

    def short(part):
        return part.astype(jnp.bfloat16) if part.dtype == jnp.float32 else part

    return jax.tree.map(short, shard)


def from_behind(block, axis, distance):
    devices = range(lax.axis_size(axis))
    route = [(i - distance, i) for i in devices if i - distance in devices]
    return lax.ppermute(block, axis, route)


def entering(value, axis, join, neutral, backward):
    count, mine = (lax.axis_size(axis), lax.axis_index(axis))
    pieces = jax.tree.map(lambda part: lax.all_gather(part, axis), value)
    if backward:
        pieces = jax.tree.map(lambda part: part[::-1], pieces)
        mine = count - 1 - mine
    subtotal = jax.tree.map(
        lambda part, zero: jnp.full_like(part, 0) + jnp.asarray(zero, part.dtype), value, neutral
    )

    def step(position, subtotal):
        longer = join(subtotal, jax.tree.map(lambda part: part[position], pieces))
        return jax.tree.map(lambda new, old: jnp.where(position < mine, new, old), longer, subtotal)

    return lax.fori_loop(0, count - 1, step, subtotal)


def norm_apply(values, gain):
    return values * lax.rsqrt(jnp.mean(values * values, -1, keepdims=True) + epsilon) * gain


def swiglu_gate(gate_part, up_part):
    return jax.nn.silu(gate_part) * up_part


def pair_sum(terms):
    return lax.psum(terms, "wa")


def fetch_rows(arrays):
    return jax.tree.map(
        lambda part, own: part.astype(own.dtype),
        lax.all_gather(shortened(arrays), "ctx", axis=0, tiled=True),
        arrays,
    )


def settle(gradients):
    return lax.psum_scatter(gradients, "ctx", scatter_dimension=0, tiled=True)


def halo_each(own_pair, halo_count):
    pieces = [from_behind(own_pair, "ctx", amount) for amount in range(halo_count, 0, -1)]
    return jnp.concatenate(pieces, 0)


def halo_each_back(gradient, halo_count, tok_rows):
    summed = jnp.zeros((tok_rows, gradient.shape[1]), jnp.float32)
    for amount in range(halo_count, 0, -1):
        slot_index = halo_count - amount
        block_grad = gradient[slot_index * tok_rows : (slot_index + 1) * tok_rows]
        summed = summed + from_behind(block_grad.astype(jnp.bfloat16), "ctx", -amount).astype(
            block_grad.dtype
        )
    return summed


def visible_mask(query_rows, key_rows, first_pos, key_first):
    query_pos = first_pos + jnp.arange(query_rows, dtype=jnp.int32)
    key_pos = key_first + jnp.arange(key_rows, dtype=jnp.int32)
    earlier = key_pos[None, :] <= query_pos[:, None]
    nearby = key_pos[None, :] > query_pos[:, None] - WINDOW
    return earlier & nearby & (key_pos[None, :] >= 0)


def head_scores(queries, keys_all, visible, score_scale):
    scores = (
        jnp.einsum("tkgd,skd->kgts", queries, keys_all, preferred_element_type=jnp.float32)
        * score_scale
    )
    return jnp.where(visible, scores, -1e30)


def attend_forward(queries, keys_all, values_all, visible, score_scale):
    scores = head_scores(queries, keys_all, visible, score_scale)
    row_max = jnp.max(scores, -1, keepdims=True)
    lifted = jnp.exp(scores - row_max)
    row_total = jnp.sum(lifted, -1, keepdims=True)
    probability = (lifted / row_total).astype(jnp.bfloat16)
    mixed_heads = jnp.einsum(
        "kgts,skd->tkgd", probability, values_all, preferred_element_type=jnp.float32
    )
    return (mixed_heads.reshape(mixed_heads.shape[0], -1), row_max + jnp.log(row_total))


def attend_backward(queries, keys_all, values_all, visible, score_scale, log_total, heads_grad):
    scores = head_scores(queries, keys_all, visible, score_scale)
    probability = jnp.where(visible, jnp.exp(scores - log_total), 0.0)
    prob_grad = jnp.einsum(
        "tkgd,skd->kgts", heads_grad, values_all, preferred_element_type=jnp.float32
    )
    row_delta = jnp.sum(probability * prob_grad, -1, keepdims=True)
    score_grad = (probability * (prob_grad - row_delta)).astype(jnp.bfloat16)
    query_grad = (
        jnp.einsum("kgts,skd->tkgd", score_grad, keys_all, preferred_element_type=jnp.float32)
        * score_scale
    )
    key_grad = (
        jnp.einsum("kgts,tkgd->skd", score_grad, queries, preferred_element_type=jnp.float32)
        * score_scale
    )
    value_grad = jnp.einsum(
        "kgts,tkgd->skd",
        probability.astype(jnp.bfloat16),
        heads_grad,
        preferred_element_type=jnp.float32,
    )
    return (query_grad, key_grad, value_grad)


def conv_apply(extended, conv_taps, conv_bias):
    tap_count = conv_taps.shape[0]
    out_rows = extended.shape[0] - tap_count + 1
    summed = conv_bias + conv_taps[0] * extended[0:out_rows]
    for offset in range(1, tap_count):
        summed = summed + conv_taps[offset] * extended[offset : offset + out_rows]
    return jax.nn.silu(summed)


def chain_link(earlier, later):
    return (earlier[0] * later[0], later[0] * earlier[1] + later[1])


def local_scan(acted, step_sizes, input_mat, decay_log):
    decay_rates = -jnp.exp(decay_log).T
    decay_step = jnp.exp(step_sizes[:, None, :] * decay_rates[None])
    drive_term = (step_sizes * acted)[:, None, :] * input_mat[:, :, None]
    return lax.associative_scan(chain_link, (decay_step, drive_term), axis=0)


def mamba_core(acted, step_sizes, input_mat, output_mat, decay_log, skip_gain, carry_in):
    cum_decay, local_state = local_scan(acted, step_sizes, input_mat, decay_log)
    states = local_state + cum_decay * carry_in[None]
    ssm_value = jnp.sum(states * output_mat[:, :, None], 1) + skip_gain * acted
    return (ssm_value, states[-1])


def shards(
    tokens,
    norm_gain,
    qkv_weight,
    heads_gain,
    mamba_in,
    conv_weight,
    conv_bias,
    state_proj,
    step_proj,
    step_bias,
    decay_log,
    skip_gain,
    mamba_gain,
    heads_out,
    mamba_out,
    mlp_gain,
    gate_up,
    down_proj,
    cotangent,
):
    tok_rows = tokens.shape[0]
    model_width = tokens.shape[1]
    inner_width = conv_weight.shape[1]
    hidden_width = gate_up.shape[2]
    heads_width = KV_HEADS * GROUP * HEAD
    kv_width = KV_HEADS * HEAD
    half_width = heads_width // lax.axis_size("wa")
    halo_count = WINDOW // tok_rows
    score_scale = HEAD ** (-0.5)
    first_pos = lax.axis_index("ctx") * tok_rows
    wa_pos = lax.axis_index("wa")
    qkv_full, in_full, hout_full, mout_full = fetch_rows(
        (qkv_weight, mamba_in, heads_out, mamba_out)
    )
    residual = tokens.astype(jnp.float32)
    normed = norm_apply(residual, norm_gain).astype(jnp.bfloat16)
    projected = jnp.dot(normed, qkv_full, preferred_element_type=jnp.float32).astype(jnp.bfloat16)
    queries = projected[:, :heads_width].reshape(tok_rows, KV_HEADS, GROUP, HEAD)
    own_pair = projected[:, heads_width:]
    halo_pair = halo_each(own_pair, halo_count)
    pair_all = jnp.concatenate((halo_pair, own_pair), 0)
    keys_all = pair_all[:, :kv_width].reshape(-1, KV_HEADS, HEAD)
    values_all = pair_all[:, kv_width:].reshape(-1, KV_HEADS, HEAD)
    visible = visible_mask(
        tok_rows, pair_all.shape[0], first_pos, first_pos - halo_count * tok_rows
    )
    heads_value, log_total = attend_forward(queries, keys_all, values_all, visible, score_scale)
    heads_normed = norm_apply(heads_value, heads_gain)
    heads_half = lax.dynamic_slice_in_dim(heads_normed, wa_pos * half_width, half_width, 1).astype(
        jnp.bfloat16
    )
    mixed_in = jnp.dot(
        normed, in_full.reshape(model_width, 2 * inner_width), preferred_element_type=jnp.float32
    ).astype(jnp.bfloat16)
    conv_in = mixed_in[:, :inner_width]
    gate_float = mixed_in[:, inner_width:].astype(jnp.float32)
    conv_tail_rows = from_behind(conv_in[tok_rows - (CONV - 1) :], "ctx", 1)
    extended = jnp.concatenate((conv_tail_rows, conv_in), 0).astype(jnp.float32)
    conv_taps = conv_weight.astype(jnp.float32)
    acted_b = conv_apply(extended, conv_taps, conv_bias).astype(jnp.bfloat16)
    acted = acted_b.astype(jnp.float32)
    rank_width = step_proj.shape[0]
    state_in = pair_sum(jnp.dot(acted_b, state_proj, preferred_element_type=jnp.float32))
    low_rank = state_in[:, :rank_width].astype(jnp.bfloat16)
    input_mat = state_in[:, rank_width : rank_width + STATE]
    output_mat = state_in[:, rank_width + STATE :]
    step_pre = jnp.dot(low_rank, step_proj, preferred_element_type=jnp.float32) + step_bias
    step_sizes = jax.nn.softplus(step_pre)
    cum_decay, local_state = local_scan(acted, step_sizes, input_mat, decay_log)
    carried = entering(
        (cum_decay[-1], local_state[-1]),
        "ctx",
        chain_link,
        (jnp.ones_like(cum_decay[-1]), jnp.zeros_like(local_state[-1])),
        False,
    )
    carry_in = carried[1]
    states = local_state + cum_decay * carry_in[None]
    ssm_value = jnp.sum(states * output_mat[:, :, None], 1) + skip_gain * acted
    gate_act = jax.nn.silu(gate_float)
    gated = ssm_value * gate_act
    square_total = pair_sum(jnp.sum(gated * gated, -1))
    mamba_scale = lax.rsqrt(square_total / INNER + epsilon)[:, None]
    mamba_normed = (gated * mamba_scale * mamba_gain).astype(jnp.bfloat16)
    mix_part = jnp.einsum("ti,oi->to", heads_half, hout_full, preferred_element_type=jnp.float32)
    mix_part = mix_part + jnp.einsum(
        "ti,oi->to", mamba_normed, mout_full, preferred_element_type=jnp.float32
    )
    mixer = pair_sum(mix_part) * 0.5
    middle = residual + mixer
    gu_full, down_full = fetch_rows((gate_up, down_proj))
    normed_mid = norm_apply(middle, mlp_gain).astype(jnp.bfloat16)
    gate_values = jnp.dot(
        normed_mid,
        gu_full.reshape(model_width, 2 * hidden_width),
        preferred_element_type=jnp.float32,
    )
    hidden_b = swiglu_gate(gate_values[:, :hidden_width], gate_values[:, hidden_width:]).astype(
        jnp.bfloat16
    )
    mlp_total = pair_sum(
        jnp.einsum("tf,of->to", hidden_b, down_full, preferred_element_type=jnp.float32)
    )
    layer_out = (middle + mlp_total).astype(jnp.bfloat16)
    gu_back, down_back = fetch_rows((gate_up, down_proj))
    down_grad = jnp.einsum("to,tf->of", cotangent, hidden_b, preferred_element_type=jnp.float32)
    hidden_grad = jnp.einsum("to,of->tf", cotangent, down_back, preferred_element_type=jnp.float32)
    gate_grad, up_grad = jax.vjp(
        swiglu_gate, gate_values[:, :hidden_width], gate_values[:, hidden_width:]
    )[1](hidden_grad)
    gate_values_grad = jnp.concatenate((gate_grad, up_grad), 1).astype(jnp.bfloat16)
    gu_grad = jnp.einsum(
        "td,tj->dj", normed_mid, gate_values_grad, preferred_element_type=jnp.float32
    ).reshape(model_width, 2, hidden_width)
    normed_mid_grad = pair_sum(
        jnp.einsum(
            "tj,dj->td",
            gate_values_grad,
            gu_back.reshape(model_width, 2 * hidden_width),
            preferred_element_type=jnp.float32,
        )
    )
    middle_norm_grad, mlp_gain_grad = jax.vjp(norm_apply, middle, mlp_gain)[1](normed_mid_grad)
    middle_grad = cotangent.astype(jnp.float32) + middle_norm_grad
    gu_settled, down_settled = settle((gu_grad, down_grad))
    qkv_back, in_back, hout_back, mout_back = fetch_rows(
        (qkv_weight, mamba_in, heads_out, mamba_out)
    )
    mixer_grad = middle_grad.astype(jnp.bfloat16)
    hout_grad = 0.5 * jnp.einsum(
        "to,ti->oi", mixer_grad, heads_half, preferred_element_type=jnp.float32
    )
    mout_grad = 0.5 * jnp.einsum(
        "to,ti->oi", mixer_grad, mamba_normed, preferred_element_type=jnp.float32
    )
    half_grad = 0.5 * jnp.einsum(
        "to,oi->ti", mixer_grad, hout_back, preferred_element_type=jnp.float32
    )
    mamba_normed_grad = 0.5 * jnp.einsum(
        "to,oi->ti", mixer_grad, mout_back, preferred_element_type=jnp.float32
    )
    padded_grad = lax.dynamic_update_slice_in_dim(
        jnp.zeros((tok_rows, heads_width), jnp.float32), half_grad, wa_pos * half_width, 1
    )
    row_term = jnp.sum(mamba_normed_grad * mamba_gain * gated, -1)
    heads_normed_grad, row_total = pair_sum((padded_grad, row_term))
    gated_grad = (
        mamba_normed_grad * mamba_gain * mamba_scale
        - gated * mamba_scale**3 * row_total[:, None] / INNER
    )
    mamba_gain_grad = jnp.sum(mamba_normed_grad * gated * mamba_scale, 0)
    ssm_grad = gated_grad * gate_act
    gate_in_grad = jax.vjp(jax.nn.silu, gate_float)[1](gated_grad * ssm_value)[0]
    state_push = jnp.sum(cum_decay * output_mat[:, :, None] * ssm_grad[:, None, :], 0)
    pushed = entering(
        (cum_decay[-1], state_push),
        "ctx",
        chain_link,
        (jnp.ones_like(state_push), jnp.zeros_like(state_push)),
        True,
    )
    future_grad = pushed[1]
    core_grads = jax.vjp(
        mamba_core, acted, step_sizes, input_mat, output_mat, decay_log, skip_gain, carry_in
    )[1]((ssm_grad, future_grad))
    (
        acted_core_grad,
        step_grad,
        input_grad,
        output_grad,
        decay_log_grad,
        skip_gain_grad,
        unused_carry,
    ) = core_grads
    step_pre_grad = step_grad * jax.nn.sigmoid(step_pre)
    step_bias_grad = jnp.sum(step_pre_grad, 0)
    step_pre_b = step_pre_grad.astype(jnp.bfloat16)
    step_proj_grad = jnp.einsum(
        "tr,tc->rc", low_rank, step_pre_b, preferred_element_type=jnp.float32
    )
    low_rank_grad = jnp.einsum(
        "tc,rc->tr", step_pre_b, step_proj, preferred_element_type=jnp.float32
    )
    state_in_grad = pair_sum(jnp.concatenate((low_rank_grad, input_grad, output_grad), 1)).astype(
        jnp.bfloat16
    )
    state_proj_grad = jnp.einsum(
        "tc,tj->cj", acted_b, state_in_grad, preferred_element_type=jnp.float32
    )
    acted_grad = acted_core_grad + jnp.einsum(
        "tj,cj->tc", state_in_grad, state_proj, preferred_element_type=jnp.float32
    )
    extended_grad, conv_weight_grad, conv_bias_grad = jax.vjp(
        conv_apply, extended, conv_taps, conv_bias
    )[1](acted_grad)
    returned = from_behind(extended_grad[: CONV - 1], "ctx", -1)
    conv_in_grad = jnp.concatenate(
        (extended_grad[CONV - 1 : tok_rows], extended_grad[tok_rows:] + returned), 0
    )
    mixed_in_grad = jnp.concatenate((conv_in_grad, gate_in_grad), 1).astype(jnp.bfloat16)
    in_grad = jnp.einsum(
        "td,tj->dj", normed, mixed_in_grad, preferred_element_type=jnp.float32
    ).reshape(model_width, 2, inner_width)
    normed_mamba_grad = jnp.einsum(
        "tj,dj->td",
        mixed_in_grad,
        in_back.reshape(model_width, 2 * inner_width),
        preferred_element_type=jnp.float32,
    )
    heads_value_grad, heads_gain_grad = jax.vjp(norm_apply, heads_value, heads_gain)[1](
        heads_normed_grad
    )
    heads_grad = heads_value_grad.astype(jnp.bfloat16).reshape(tok_rows, KV_HEADS, GROUP, HEAD)
    query_grad, key_grad, value_grad = attend_backward(
        queries, keys_all, values_all, visible, score_scale, log_total, heads_grad
    )
    pair_grad = jnp.concatenate(
        (key_grad.reshape(-1, kv_width), value_grad.reshape(-1, kv_width)), 1
    )
    halo_grad = pair_grad[: halo_count * tok_rows]
    returned_pair = halo_each_back(halo_grad, halo_count, tok_rows)
    own_pair_grad = pair_grad[halo_count * tok_rows :] + returned_pair
    projected_grad = jnp.concatenate(
        (query_grad.reshape(tok_rows, heads_width), own_pair_grad), 1
    ).astype(jnp.bfloat16)
    qkv_grad = jnp.einsum("td,tj->dj", normed, projected_grad, preferred_element_type=jnp.float32)
    normed_heads_grad = jnp.einsum(
        "tj,dj->td", projected_grad, qkv_back, preferred_element_type=jnp.float32
    )
    normed_grad = normed_heads_grad + pair_sum(normed_mamba_grad)
    residual_norm_grad, norm_gain_grad = jax.vjp(norm_apply, residual, norm_gain)[1](normed_grad)
    tokens_grad = middle_grad + residual_norm_grad
    qkv_settled, in_settled, hout_settled, mout_settled = settle(
        (qkv_grad, in_grad, hout_grad, mout_grad)
    )
    small_sums = lax.psum(
        (
            norm_gain_grad,
            heads_gain_grad,
            conv_weight_grad,
            conv_bias_grad,
            state_proj_grad,
            step_proj_grad,
            step_bias_grad,
            decay_log_grad,
            skip_gain_grad,
            mamba_gain_grad,
            mlp_gain_grad,
        ),
        "ctx",
    )
    return (
        layer_out,
        tokens_grad,
        small_sums[0],
        qkv_settled,
        small_sums[1],
        in_settled,
        small_sums[2],
        small_sums[3],
        small_sums[4],
        small_sums[5],
        small_sums[6],
        small_sums[7],
        small_sums[8],
        small_sums[9],
        hout_settled,
        mout_settled,
        small_sums[10],
        gu_settled,
        down_settled,
    )


def solution(mesh):
    placed = (
        P("ctx", None),
        P(),
        P("ctx", None),
        P(),
        P("ctx", None, "wa"),
        P(None, "wa"),
        P("wa"),
        P("wa", None),
        P(None, "wa"),
        P("wa"),
        P("wa", None),
        P("wa"),
        P("wa"),
        P("ctx", "wa"),
        P("ctx", "wa"),
        P(),
        P("ctx", None, "wa"),
        P("ctx", "wa"),
        P("ctx", None),
    )
    return jax.shard_map(
        shards,
        mesh=mesh,
        in_specs=placed,
        out_specs=(
            P("ctx", None),
            P("ctx", None),
            P(),
            P("ctx", None),
            P(),
            P("ctx", None, "wa"),
            P(None, "wa"),
            P("wa"),
            P("wa", None),
            P(None, "wa"),
            P("wa"),
            P("wa", None),
            P("wa"),
            P("wa"),
            P("ctx", "wa"),
            P("ctx", "wa"),
            P(),
            P("ctx", None, "wa"),
            P("ctx", "wa"),
        ),
        check_vma=False,
    )
```

profile of v0, /device:TPU:1, one launch (start us, length us, event | category | flops | bytes accessed | tf_op | source)
XLA Modules:
  0.0 3762.3 jit_solution(14623076712917112061)
XLA Ops:
  10.7 89.2 %all-gather.15.cloned.1.call-done = bf16[1600,2,1600]{2,1,0:T(2,128)(2,1)} async-done(((bf16[25,2,1600]{2,1,0:T(2,128)(2,1)}), bf16[1600,2,1600]{2,1,0:T(2,128)(2,1)}) %all-gather.15.cloned.1.call-update) | async-done | bytes 10240016 | tf_op jit(solution)/shard_map/all_gather | solution.py:64
  99.9 21.0 reshape.225
  136.0 24.0 all-reduce.123.cloned.1.call-done
  376.4 39.1 %pad.478 = f32[128,16,1600]{2,1,0:T(8,128)} pad(f32[64,16,1600]{2,1,0:T(8,128)} %add.653, f32[]{:T(128)} %constant.101.clone.1), padding=1_0_1x0_0_0x0_0_0 | pad | bytes 19660804 | tf_op jit(solution)/shard_map/pad | solution.py:159
  485.0 38.9 %pad.477 = f32[128,16,1600]{2,1,0:T(8,128)} pad(f32[64,16,1600]{2,1,0:T(8,128)} %pad_maximum_fusion.1, f32[]{:T(128)} %constant.101.clone.1), padding=0_1_1x0_0_0x0_0_0 | pad | bytes 19660804 | tf_op jit(solution)/shard_map/pad | solution.py:159
  535.3 39.1 %pad.464 = f32[128,16,1600]{2,1,0:T(8,128)} pad(f32[64,16,1600]{2,1,0:T(8,128)} %add.645, f32[]{:T(128)} %constant.101.clone.1), padding=1_0_1x0_0_0x0_0_0 | pad | bytes 19660804 | tf_op jit(solution)/shard_map/pad | solution.py:159
  580.5 39.0 %pad.463 = f32[128,16,1600]{2,1,0:T(8,128)} pad(f32[64,16,1600]{2,1,0:T(8,128)} %pad_maximum_fusion, f32[]{:T(128)} %constant.101.clone.1), padding=0_1_1x0_0_0x0_0_0 | pad | bytes 19660804 | tf_op jit(solution)/shard_map/pad | solution.py:159
  724.2 66.6 %while.28 = (s32[]{:T(128)}, f32[16,1600]{1,0:T(8,128)S(1)}, s32[]{:T(128)}, f32[64,16,1600]{2,1,0:T(8,128)}, f32[64,16,1600]{2,1,0:T(8,128)}, /*index=5*/s32[]{:T(128)}, s32[]{:T(128)}) while((s32[]{:T(128)}, f32[16,1600]{1,0:T(8,128)S(1)}, s32[]{:T(128)}, f32[64,16,1600]{2,1,0:T(8,128)}, f32[64,16,1600]{2,1,0:T(8,128)}, ...), condition=%wide.region_6.7_spmd.clone, body=%wide.region_5.6_spmd.clone.sunk | while | flops 102404 | bytes 409709 | solution.py:46
  790.8 24.0 multiply_reduce_fusion.7
  855.0 110.5 %all-gather.21.cloned.1.call-done = bf16[1600,2,2752]{2,1,0:T(2,128)(2,1)} async-done(((bf16[25,2,2752]{2,1,0:T(2,128)(2,1)}), bf16[1600,2,2752]{2,1,0:T(2,128)(2,1)}) %all-gather.21.cloned.1.call-update) | async-done | bytes 17612816 | tf_op jit(solution)/shard_map/all_gather | solution.py:64
  965.5 37.9 %reshape.226 = bf16[1600,5504]{1,0:T(8,128)(2,1)} reshape(bf16[1600,2,2752]{2,1,0:T(2,128)(2,1)} %all-gather.21.cloned.1.call-done) | data formatting | bytes 35225600 | tf_op jit(solution)/shard_map/reshape | solution.py:264
  1033.8 23.5 all-reduce.127.cloned.1.call-done
  1109.8 52.1 %all-gather.23.cloned.1.call-done = f32[1024,1600]{1,0:T(8,128)} async-done(((f32[16,1600]{1,0:T(8,128)}), f32[1024,1600]{1,0:T(8,128)}) %all-gather.23.cloned.1.call-update) | async-done | bytes 6553616 | tf_op jit(solution)/shard_map/all_gather | solution.py:34
  1168.1 66.4 %while.29 = (s32[]{:T(128)}, f32[16,1600]{1,0:T(8,128)S(1)}, s32[]{:T(128)}, f32[64,16,1600]{2,1,0:T(8,128)}, f32[64,16,1600]{2,1,0:T(8,128)}, /*index=5*/s32[]{:T(128)}, s32[]{:T(128)}) while((s32[]{:T(128)}, f32[16,1600]{1,0:T(8,128)S(1)}, s32[]{:T(128)}, f32[64,16,1600]{2,1,0:T(8,128)}, f32[64,16,1600]{2,1,0:T(8,128)}, ...), condition=%wide.region_22.23_spmd.clone, body=%wide.region_21.22_spmd.clone.sunk | while | flops 102404 | bytes 409709 | solution.py:46
  1268.4 23.1 slice_multiply_fusion.4
  1641.9 24.9 multiply_add_fusion.2
  1666.7 39.0 %pad.524 = f32[128,16,1600]{2,1,0:T(8,128)} pad(f32[64,16,1600]{2,1,0:T(8,128)} %get-tuple-element.353, f32[]{:T(128)} %constant.101.clone.1), padding=1_0_1x0_0_0x0_0_0 | pad | bytes 19660804 | tf_op jit(solution)/shard_map/transpose(jvp())/pad | solution.py:159
  1718.8 39.0 %pad.525 = f32[128,16,1600]{2,1,0:T(8,128)} pad(f32[64,16,1600]{2,1,0:T(8,128)} %get-tuple-element.376, f32[]{:T(128)} %constant.101.clone.1), padding=0_1_1x0_0_0x0_0_0 | pad | bytes 19660804 | tf_op jit(solution)/shard_map/transpose(jvp())/pad | solution.py:159
  1757.8 38.4 %pad.482 = f32[128,16,1600]{2,1,0:T(8,128)} pad(f32[63,16,1600]{2,1,0:T(8,128)} %get-tuple-element.388, f32[]{:T(128)} %constant.101.clone.1), padding=2_1_1x0_0_0x0_0_0 | pad | bytes 19558404 | tf_op jit(solution)/shard_map/transpose(jvp())/pad | solution.py:159
  1811.4 39.1 %pad.571 = f32[128,16,1600]{2,1,0:T(8,128)} pad(f32[64,16,1600]{2,1,0:T(8,128)} %get-tuple-element.375, f32[]{:T(128)} %constant.101.clone.1), padding=0_1_1x0_0_0x0_0_0 | pad | bytes 19660804 | tf_op jit(solution)/shard_map/transpose(jvp())/pad | solution.py:159
  1850.5 39.0 %pad.570 = f32[128,16,1600]{2,1,0:T(8,128)} pad(f32[64,16,1600]{2,1,0:T(8,128)} %get-tuple-element.351, f32[]{:T(128)} %constant.101.clone.1), padding=1_0_1x0_0_0x0_0_0 | pad | bytes 19660804 | tf_op jit(solution)/shard_map/transpose(jvp())/pad | solution.py:159
  1889.5 38.4 %pad.528 = f32[128,16,1600]{2,1,0:T(8,128)} pad(f32[63,16,1600]{2,1,0:T(8,128)} %get-tuple-element.381, f32[]{:T(128)} %constant.101.clone.1), padding=2_1_1x0_0_0x0_0_0 | pad | bytes 19558404 | tf_op jit(solution)/shard_map/transpose(jvp())/pad | solution.py:159
  1982.0 46.4 %reshape.236 = f32[1600,2,2752]{2,1,0:T(2,128)} reshape(f32[1600,5504]{1,0:T(8,128)} %fusion.23) | data formatting | bytes 70451200 | tf_op jit(solution)/shard_map/reshape | solution.py:283
  2038.4 351.0 %fusion.3 = f32[32,2752]{1,0:T(8,128)} fusion(f32[1600,2752]{1,0:T(8,128)} %convolution_bitcast_fusion.1), kind=kCustom, calls=%all-reduce-scatter.3 | all-reduce-scatter fusion | flops 5636097 | bytes 17965568
  2459.9 26.0 reshape.231
  2606.7 442.2 %fusion.88 = (f32[32,2240]{1,0:T(8,128)S(1)}, f32[32,800]{1,0:T(8,128)S(1)}, f32[32,1600]{1,0:T(8,128)S(1)}) fusion(f32[1600,2240]{1,0:T(8,128)} %fusion.50, f32[1600,800]{1,0:T(8,128)} %convolution_multiply_fusion.2, f32[1600,1600]{1,0:T(8,128)} %convolution_multiply_fusion.1), kind=kCustom, calls=%all-reduce-scatter.4 | all-reduce-scatter fusion | flops 9502721 | bytes 30290432
  3128.8 47.1 %concatenate.99 = f32[473,2752]{1,0:T(8,128)} concatenate(f32[25,2752]{1,0:T(8,128)} %collective-permute-done.73, f32[32,2752]{1,0:T(8,128)} %collective-permute-done.72, f32[32,2752]{1,0:T(8,128)} %collective-permute-done.71, f32[32,2752]{1,0:T(8,128)} %collective-permute-done.70, f32[32,2752]{1,0:T(8,128)S(1)} %copy-done.154, f32[32,2752]{1,0:T(8,128)} %copy-done.155, ...), dimensions={0} | concatenate | bytes 10413568
  3264.3 21.3 collective-permute-start.31
  3364.1 25.8 concatenate.98
  3391.6 38.8 %concatenate.96 = f32[473,2240]{1,0:T(8,128)} concatenate(f32[25,2240]{1,0:T(8,128)} %copy-done.164, f32[32,2240]{1,0:T(8,128)S(1)} %copy-done.160, f32[32,2240]{1,0:T(8,128)S(1)} %copy-done.162, f32[32,2240]{1,0:T(8,128)} %copy-done.163, f32[32,2240]{1,0:T(8,128)} %collective-permute-done.27, f32[32,2240]{1,0:T(8,128)} %collective-permute-done.26, ...), dimensions={0} | concatenate | bytes 8476160
  3434.0 174.1 %all-reduce.133.cloned.1.call-done = (f32[1600,2,1600]{2,1,0:T(2,128)}, f32[1600,132]{0,1:T(8,128)}, f32[100,1600]{1,0:T(8,128)}, f32[1600,16]{0,1:T(8,128)}) async-done(((f32[1600,2,1600]{2,1,0:T(2,128)}, f32[1600,132]{0,1:T(8,128)}, f32[100,1600]{1,0:T(8,128)}, f32[1600,16]{0,1:T(8,128)}), (f32[1600,2,1600]{2,1,0:T(2,128)}, f32[1600,132]{0,1:T(8,128)}, f32[100,1600]{1,0:T(8,128)}, ...) | async-done | bytes 22067216
  3609.9 130.1 %all-reduce.131.cloned.1.call-done = (f32[1600]{0:T(1024)}, f32[1600]{0:T(1024)}, f32[4,1600]{1,0:T(4,128)}, f32[1600]{0:T(1024)}, f32[1600]{0:T(1024)}, /*index...) async-done(((f32[1600]{0:T(1024)}, f32[1600]{0:T(1024)}, f32[4,1600]{1,0:T(4,128)}, f32[1600]{0:T(1024)}, f32[1600]{0:T(1024)}, /*index=5*/f32[1600]{0:T(1024)}, f32[1600]{0:T(1024)}, ...) | async-done | bytes 70416 | tf_op jit(solution)/shard_map/psum | solution.py:405
  (1137 shorter events, 1617.7 us)
Async XLA Ops:
  7.2 92.7 %all-gather.15.cloned.1.call-start = ((), (), s32[]{:S(2)}) async-start(), calls=%async_computation | async-start | bytes 10816000 | tf_op jit(solution)/shard_map/all_gather | solution.py:64
  7.9 152.1 %all-reduce.123.cloned.1.call-start = ((), (), s32[]{:S(2)}) async-start(), calls=%async_computation.1 | async-start | bytes 139264 | tf_op jit(solution)/shard_map/psum | solution.py:58
  134.0 488.0 %all-gather.25.cloned.1.call-start = ((), (), s32[]{:S(2)}) async-start(), calls=%async_computation.8 | async-start | bytes 9584640 | tf_op jit(solution)/shard_map/all_gather | solution.py:64
  134.8 515.2 %all-gather.27.cloned.1.call-start = ((), (), s32[]{:S(2)}) async-start(), calls=%async_computation.9 | async-start | bytes 3727360 | tf_op jit(solution)/shard_map/all_gather | solution.py:64
  135.4 519.5 %all-gather.29.cloned.1.call-start = ((), (), s32[]{:S(2)}) async-start(), calls=%async_computation.10 | async-start | bytes 6922240 | tf_op jit(solution)/shard_map/all_gather | solution.py:64
  135.9 588.2 %all-gather.17.cloned.1.call-start = ((), (), s32[]{:S(2)}) async-start(), calls=%async_computation.2 | async-start | bytes 6922240 | tf_op jit(solution)/shard_map/all_gather | solution.py:34
  525.5 198.6 %all-gather.19.cloned.1.call-start = ((), (), s32[]{:S(2)}) async-start(), calls=%async_computation.3 | async-start | bytes 6922240 | tf_op jit(solution)/shard_map/all_gather | solution.py:34
  621.1 205.3 %all-gather.31.cloned.1.call-start = ((), (), s32[]{:S(2)}) async-start(), calls=%async_computation.11 | async-start | bytes 11714560 | tf_op jit(solution)/shard_map/all_gather | solution.py:64
  621.9 231.7 %all-reduce.125.cloned.1.call-start = ((), (), s32[]{:S(2)}) async-start(), calls=%async_computation.4 | async-start | bytes 1703936 | tf_op jit(solution)/shard_map/psum | solution.py:58
  825.8 139.7 %all-gather.21.cloned.1.call-start = ((), (), s32[]{:S(2)}) async-start(), calls=%async_computation.5 | async-start | bytes 18304000 | tf_op jit(solution)/shard_map/all_gather | solution.py:64
  826.4 230.9 %all-reduce.127.cloned.1.call-start = ((), (), s32[]{:S(2)}) async-start(), calls=%async_computation.6 | async-start | bytes 1703936 | tf_op jit(solution)/shard_map/psum | solution.py:58
  1032.3 129.6 %all-gather.23.cloned.1.call-start = ((), (), s32[]{:S(2)}) async-start(), calls=%async_computation.7 | async-start | bytes 6922240 | tf_op jit(solution)/shard_map/all_gather | solution.py:34
  1087.0 1315.3 %all-reduce.135.cloned.1.call-start = ((), (), s32[]{:S(2)}) async-start(), calls=%async_computation.15 | async-start | bytes 5111808 | tf_op jit(solution)/shard_map/psum | solution.py:58
  1962.7 1469.4 %all-reduce.129.cloned.1.call-start = ((), (), s32[]{:S(2)}) async-start(), calls=%async_computation.12 | async-start | bytes 72089600
  2028.5 1579.7 %all-reduce.133.cloned.1.call-start = ((), (), s32[]{:S(2)}) async-start(), calls=%async_computation.14 | async-start | bytes 46006272
  2445.3 63.0 %collective-permute-start.12 = (bf16[128,640]{0,1:T(8,128)(2,1)}, bf16[128,640]{0,1:T(8,128)(2,1)}, u32[]{:S(2)}, u32[]{:S(2)}) collective-permute-start(bf16[128,640]{0,1:T(8,128)(2,1)} %get-tuple-element.440), channel_id=1, source_target_pairs={{10,0},{12,2},{14,4},{16,6},{18,8},{20,10},{22,12},{24,14},{26,16}... | collective-permute-start | bytes 491528 | tf_op jit(solution)/shard_map/ppermute | solution.py:29
  2446.7 67.7 %collective-permute-start.11 = (bf16[128,640]{0,1:T(8,128)(2,1)}, bf16[128,640]{0,1:T(8,128)(2,1)}, u32[]{:S(2)}, u32[]{:S(2)}) collective-permute-start(bf16[128,640]{0,1:T(8,128)(2,1)} %get-tuple-element.441), channel_id=1, source_target_pairs={{12,0},{14,2},{16,4},{18,6},{20,8},{22,10},{24,12},{26,14},{28,16}... | collective-permute-start | bytes 491528 | tf_op jit(solution)/shard_map/ppermute | solution.py:29
  2448.7 68.4 %collective-permute-start.10 = (bf16[128,640]{0,1:T(8,128)(2,1)}, bf16[128,640]{0,1:T(8,128)(2,1)}, u32[]{:S(2)}, u32[]{:S(2)}) collective-permute-start(bf16[128,640]{0,1:T(8,128)(2,1)} %get-tuple-element.442), channel_id=1, source_target_pairs={{14,0},{16,2},{18,4},{20,6},{22,8},{24,10},{26,12},{28,14},{30,16}... | collective-permute-start | bytes 491528 | tf_op jit(solution)/shard_map/ppermute | solution.py:29
  2486.0 1254.1 %all-reduce.131.cloned.1.call-start = ((), (), s32[]{:S(2)}) async-start(), calls=%async_computation.13 | async-start | bytes 167936 | tf_op jit(solution)/shard_map/psum | solution.py:405
  2574.6 474.4 %collective-permute-start.64 = (f32[32,2752]{1,0:T(8,128)}, f32[32,2752]{1,0:T(8,128)}, u32[]{:S(2)}, u32[]{:S(2)}) collective-permute-start(f32[32,2752]{1,0:T(8,128)} %fusion.3), channel_id=1, source_target_pairs={{0,10},{2,12},{4,14},{6,16},{8,18},{10,20},{12,22},{14,24},{16,26}... | collective-permute-start | bytes 1056776
  2580.0 474.3 %collective-permute-start.63 = (f32[32,2752]{1,0:T(8,128)}, f32[32,2752]{1,0:T(8,128)}, u32[]{:S(2)}, u32[]{:S(2)}) collective-permute-start(f32[32,2752]{1,0:T(8,128)} %fusion.3), channel_id=1, source_target_pairs={{0,8},{2,10},{4,12},{6,14},{8,16},{10,18},{12,20},{14,22},{16,24},... | collective-permute-start | bytes 1056776
  2583.8 487.1 %collective-permute-start.62 = (f32[32,2752]{1,0:T(8,128)}, f32[32,2752]{1,0:T(8,128)}, u32[]{:S(2)}, u32[]{:S(2)}) collective-permute-start(f32[32,2752]{1,0:T(8,128)} %fusion.3), channel_id=1, source_target_pairs={{0,6},{2,8},{4,10},{6,12},{8,14},{10,16},{12,18},{14,20},{16,22},{... | collective-permute-start | bytes 1056776
  2600.8 471.4 %collective-permute-start.61 = (f32[32,2752]{1,0:T(8,128)}, f32[32,2752]{1,0:T(8,128)}, u32[]{:S(2)}, u32[]{:S(2)}) collective-permute-start(f32[32,2752]{1,0:T(8,128)} %fusion.3), channel_id=1, source_target_pairs={{0,4},{2,6},{4,8},{6,10},{8,12},{10,14},{12,16},{14,18},{16,20},{1... | collective-permute-start | bytes 1056776
  2603.6 483.8 %collective-permute-start.60 = (f32[32,2752]{1,0:T(8,128)}, f32[32,2752]{1,0:T(8,128)}, u32[]{:S(2)}, u32[]{:S(2)}) collective-permute-start(f32[32,2752]{1,0:T(8,128)} %fusion.3), channel_id=1, source_target_pairs={{0,2},{2,4},{4,6},{6,8},{8,10},{10,12},{12,14},{14,16},{16,18},{18... | collective-permute-start | bytes 1056776
  3109.2 87.8 %collective-permute-start.59 = (f32[25,1600]{1,0:T(8,128)}, f32[25,1600]{1,0:T(8,128)}, u32[]{:S(2)}, u32[]{:S(2)}) collective-permute-start(f32[25,1600]{1,0:T(8,128)} %slice.702), channel_id=1, source_target_pairs={{0,28},{2,30},{4,32},{6,34},{8,36},{10,38},{12,40},{14,42},{16,44}... | collective-permute-start | bytes 480008
  3115.3 60.6 %collective-permute-start.35 = (f32[32,800]{1,0:T(8,128)S(1)}, f32[32,800]{1,0:T(8,128)}, u32[]{:S(2)}, u32[]{:S(2)}) collective-permute-start(f32[32,800]{1,0:T(8,128)S(1)} %get-tuple-element.345), channel_id=1, source_target_pairs={{0,8},{2,10},{4,12},{6,14},{8,16},{10,18},{12,20},{14,22},{16,24},... | collective-permute-start | bytes 307208
  3117.7 64.5 %collective-permute-start.34 = (f32[32,800]{1,0:T(8,128)S(1)}, f32[32,800]{1,0:T(8,128)}, u32[]{:S(2)}, u32[]{:S(2)}) collective-permute-start(f32[32,800]{1,0:T(8,128)S(1)} %get-tuple-element.345), channel_id=1, source_target_pairs={{0,6},{2,8},{4,10},{6,12},{8,14},{10,16},{12,18},{14,20},{16,22},{... | collective-permute-start | bytes 307208
  3120.9 62.6 %collective-permute-start.33 = (f32[32,800]{1,0:T(8,128)S(1)}, f32[32,800]{1,0:T(8,128)}, u32[]{:S(2)}, u32[]{:S(2)}) collective-permute-start(f32[32,800]{1,0:T(8,128)S(1)} %get-tuple-element.345), channel_id=1, source_target_pairs={{0,4},{2,6},{4,8},{6,10},{8,12},{10,14},{12,16},{14,18},{16,20},{1... | collective-permute-start | bytes 307208
  3124.8 68.8 %collective-permute-start.32 = (f32[32,800]{1,0:T(8,128)S(1)}, f32[32,800]{1,0:T(8,128)}, u32[]{:S(2)}, u32[]{:S(2)}) collective-permute-start(f32[32,800]{1,0:T(8,128)S(1)} %get-tuple-element.345), channel_id=1, source_target_pairs={{0,2},{2,4},{4,6},{6,8},{8,10},{10,12},{12,14},{14,16},{16,18},{18... | collective-permute-start | bytes 307208
  3226.9 81.4 %collective-permute-start.30 = (f32[32,2240]{1,0:T(8,128)S(1)}, f32[32,2240]{1,0:T(8,128)S(1)}, u32[]{:S(2)}, u32[]{:S(2)}) collective-permute-start(f32[32,2240]{1,0:T(8,128)S(1)} %get-tuple-element.344), channel_id=1, source_target_pairs={{0,26},{2,28},{4,30},{6,32},{8,34},{10,36},{12,38},{14,40},{16,42}... | collective-permute-start | bytes 860168
  3234.8 80.3 %collective-permute-start.29 = (f32[32,2240]{1,0:T(8,128)S(1)}, f32[32,2240]{1,0:T(8,128)S(1)}, u32[]{:S(2)}, u32[]{:S(2)}) collective-permute-start(f32[32,2240]{1,0:T(8,128)S(1)} %get-tuple-element.344), channel_id=1, source_target_pairs={{0,24},{2,26},{4,28},{6,30},{8,32},{10,34},{12,36},{14,38},{16,40}... | collective-permute-start | bytes 860168
  3240.8 78.2 %collective-permute-start.28 = (f32[32,2240]{1,0:T(8,128)S(1)}, f32[32,2240]{1,0:T(8,128)S(1)}, u32[]{:S(2)}, u32[]{:S(2)}) collective-permute-start(f32[32,2240]{1,0:T(8,128)S(1)} %get-tuple-element.344), channel_id=1, source_target_pairs={{0,22},{2,24},{4,26},{6,28},{8,30},{10,32},{12,34},{14,36},{16,38}... | collective-permute-start | bytes 860168
  (321 other events, 10515.9 us)
Sparse Core Ops, SparseCore 0:
  10.9 88.9 all-gather.14
  134.2 25.8 all-reduce.122
  162.8 82.5 all-gather.24
  248.1 66.7 all-gather.26
  317.6 72.1 all-gather.28
  525.7 75.0 all-gather.16
  621.2 91.9 all-gather.18
  716.1 84.6 all-gather.30
  825.9 27.5 all-reduce.124
  856.6 108.9 all-gather.20
  1032.4 24.8 all-reduce.126
  1087.1 74.6 all-gather.22
  1962.8 32.0 all-reduce.134
  2028.6 1228.2 all-reduce.128
  3264.9 343.2 all-reduce.132
  3616.6 123.3 all-reduce.130
where the time goes:
time: 3810 us; the launch traced here: 3760 us
  local copies, waits for them, and re-layouts  1210 us (32%)
  blocking collectives  805 us (21%)
  waiting for transfers between devices  641 us (17%)
  other arithmetic  520 us (14%)
  starting transfers between devices  384 us (10%)
  matrix products  181 us (5%)
    pad x70, local copies, waits for them, and re-layouts, local_scan(): return lax.associative_scan(chain_link, (decay_step, drive_term), axis=0)  805 us
    unnamed x2, blocking collectives  793 us
    unnamed x58, starting transfers between devices  338 us
    unnamed x548, local copies, waits for them, and re-layouts  220 us
    all_gather x6, waiting for transfers between devices, fetch_rows(): lax.all_gather(shortened(arrays), 'ctx', axis=0, tiled=True)  200 us
    unnamed x74, waiting for transfers between devices  180 us
    select_n x126, other arithmetic, step(): jnp.where(position < mine, new, old)  130 us
    psum x1, waiting for transfers between devices, shards(): lax.psum((norm_gain_grad, heads_gain_grad, conv_weight_grad, conv_bias_gr...  130 us
  transfers between devices with their start and end apart: 90, of which 16 were waited for; matrix products, arithmetic and copies ran while one was open for 47% of the time, Pallas kernels for 0%

commit v1 on v0

v1 whole, which is shorter than its diff:
```python
import functools

import jax
import jax.numpy as jnp
from jax import lax
from jax.experimental import pallas as pl
from jax.experimental.pallas import tpu as pltpu
from jax.sharding import Mesh, PartitionSpec as P

KV_HEADS = 5
GROUP = 5
HEAD = 64
INNER = 3200
STATE = 16
CONV = 4
WINDOW = 1024
STEP = 8
LANES = 128

epsilon = 1e-06


def spread(row, like):
    return jnp.broadcast_to(row, like.shape)


def column(block, index, like):
    return jnp.broadcast_to(block[:, index : index + 1], like.shape)


def turned(block, start):
    return pltpu.roll(block, lax.rem(LANES - start, LANES), 1)


def local_kernel(dt_ref, x_ref, b_ref, rate_ref, out_ref, total_ref):
    @pl.when(pl.program_id(0) == 0)
    def _():
        out_ref[...] = jnp.zeros_like(out_ref)
        total_ref[...] = jnp.zeros_like(total_ref)

    rates = rate_ref[...]
    b_all = b_ref[...]

    def block(j, carry):
        state, total = carry
        start = pl.multiple_of(j * STEP, STEP)
        dt = dt_ref[pl.ds(start, STEP), :]
        drive = dt * x_ref[pl.ds(start, STEP), :]
        b_cols = turned(b_all, start)
        for i in range(STEP):
            decay = jnp.exp(spread(dt[i : i + 1], state) * rates)
            state = decay * state + spread(drive[i : i + 1], state) * column(b_cols, i, state)
        return state, total + dt

    state, total = lax.fori_loop(
        0, dt_ref.shape[0] // STEP, block, (out_ref[...], total_ref[...])
    )
    out_ref[...] = state
    total_ref[...] = total


def value_kernel(dt_ref, x_ref, b_ref, c_ref, rate_ref, enter_ref, out_ref, state_ref):
    @pl.when(pl.program_id(0) == 0)
    def _():
        state_ref[...] = enter_ref[...]

    rates = rate_ref[...]
    b_all = b_ref[...]
    c_all = c_ref[...]

    def block(j, state):
        start = pl.multiple_of(j * STEP, STEP)
        dt = dt_ref[pl.ds(start, STEP), :]
        drive = dt * x_ref[pl.ds(start, STEP), :]
        b_cols = turned(b_all, start)
        c_cols = turned(c_all, start)
        rows = []
        for i in range(STEP):
            decay = jnp.exp(spread(dt[i : i + 1], state) * rates)
            state = decay * state + spread(drive[i : i + 1], state) * column(b_cols, i, state)
            rows.append(jnp.sum(state * column(c_cols, i, state), 0, keepdims=True))
        out_ref[pl.ds(start, STEP), :] = jnp.concatenate(rows, 0)
        return state

    state_ref[...] = lax.fori_loop(0, dt_ref.shape[0] // STEP, block, state_ref[...])


def push_kernel(dt_ref, dy_ref, c_ref, rate_ref, out_ref):
    @pl.when(pl.program_id(0) == 0)
    def _():
        out_ref[...] = jnp.zeros_like(out_ref)

    rates = rate_ref[...]
    c_all = c_ref[...]
    count = dt_ref.shape[0] // STEP

    def block(k, push):
        start = pl.multiple_of((count - 1 - k) * STEP, STEP)
        dt = dt_ref[pl.ds(start, STEP), :]
        dy = dy_ref[pl.ds(start, STEP), :]
        c_cols = turned(c_all, start)
        for i in range(STEP - 1, -1, -1):
            decay = jnp.exp(spread(dt[i : i + 1], push) * rates)
            push = decay * (push + spread(dy[i : i + 1], push) * column(c_cols, i, push))
        return push

    out_ref[...] = lax.fori_loop(0, count, block, out_ref[...])


def back_kernel(
    half,
    dt_ref,
    x_ref,
    dy_ref,
    b_ref,
    c_ref,
    rate_ref,
    enter_ref,
    future_ref,
    ddt_ref,
    dx_ref,
    db_ref,
    dc_ref,
    drate_ref,
    kept_ref,
    state_ref,
):
    step = pl.program_id(0)
    rates = rate_ref[...]
    b_all = b_ref[...]
    rows = dt_ref.shape[0]
    count = rows // STEP

    @pl.when(step == 0)
    def _():
        state_ref[...] = enter_ref[...]

    @pl.when(step < half)
    def _():
        def block(j, state):
            start = pl.multiple_of(j * STEP, STEP)
            dt = dt_ref[pl.ds(start, STEP), :]
            drive = dt * x_ref[pl.ds(start, STEP), :]
            b_cols = turned(b_all, start)
            for i in range(STEP):
                kept_ref[step * rows + start + i] = state
                decay = jnp.exp(spread(dt[i : i + 1], state) * rates)
                state = decay * state + spread(drive[i : i + 1], state) * column(b_cols, i, state)
            return state

        state_ref[...] = lax.fori_loop(0, count, block, state_ref[...])

    @pl.when(step == half)
    def _():
        state_ref[...] = future_ref[...]
        drate_ref[...] = jnp.zeros_like(drate_ref)

    @pl.when(step >= half)
    def _():
        base = (2 * half - 1 - step) * rows
        c_all = c_ref[...]
        lane = lax.broadcasted_iota(jnp.int32, b_all.shape, 1)

        def narrow(wide):
            parts = wide[:, :LANES]
            for first in range(LANES, wide.shape[1], LANES):
                parts = parts + wide[:, first : first + LANES]
            return jnp.sum(parts, 1, keepdims=True)

        def block(k, carry):
            push, drate, db, dc = carry
            start = pl.multiple_of((count - 1 - k) * STEP, STEP)
            dt = dt_ref[pl.ds(start, STEP), :]
            x = x_ref[pl.ds(start, STEP), :]
            dy = dy_ref[pl.ds(start, STEP), :]
            drive = dt * x
            b_cols = turned(b_all, start)
            c_cols = turned(c_all, start)
            first_rows = [None] * STEP
            second_rows = [None] * STEP
            for i in range(STEP - 1, -1, -1):
                before = kept_ref[base + start + i]
                dt_wide = spread(dt[i : i + 1], before)
                dy_wide = spread(dy[i : i + 1], before)
                drive_wide = spread(drive[i : i + 1], before)
                b_wide = column(b_cols, i, before)
                decay = jnp.exp(dt_wide * rates)
                moved = decay * before
                state = moved + drive_wide * b_wide
                push = push + dy_wide * column(c_cols, i, before)
                here = lane == start + i
                dc = jnp.where(here, narrow(dy_wide * state), dc)
                db = jnp.where(here, narrow(push * drive_wide), db)
                mixed = push * moved
                drate = drate + dt_wide * mixed
                first_rows[i] = jnp.sum(rates * mixed, 0, keepdims=True)
                second_rows[i] = jnp.sum(push * b_wide, 0, keepdims=True)
                push = decay * push
            second = jnp.concatenate(second_rows, 0)
            ddt_ref[pl.ds(start, STEP), :] = jnp.concatenate(first_rows, 0) + x * second
            dx_ref[pl.ds(start, STEP), :] = dt * second
            return push, drate, db, dc

        zero = jnp.zeros(b_all.shape, jnp.float32)
        push, drate, db, dc = lax.fori_loop(
            0, count, block, (state_ref[...], drate_ref[...], zero, zero)
        )
        state_ref[...] = push
        drate_ref[...] = drate
        db_ref[...] = db
        dc_ref[...] = dc


def whole(shape):
    return pl.BlockSpec(shape, lambda s: (0,) * len(shape))


def params():
    return pltpu.CompilerParams(
        dimension_semantics=("arbitrary",), vmem_limit_bytes=48 * 1024 * 1024
    )


def cost(rows, width, states, ops):
    return pl.CostEstimate(
        flops=rows * width * states * ops,
        bytes_accessed=rows * width * 16,
        transcendentals=rows * width * states,
    )


def local_scan(dt, x, b_t, rates):
    rows, width = dt.shape
    states = rates.shape[0]
    by_row = pl.BlockSpec((LANES, width), lambda s: (s, 0))
    by_lane = pl.BlockSpec((states, LANES), lambda s: (0, s))
    state, total = pl.pallas_call(
        local_kernel,
        grid=(rows // LANES,),
        in_specs=[by_row, by_row, by_lane, whole((states, width))],
        out_specs=[whole((states, width)), whole((STEP, width))],
        out_shape=[
            jax.ShapeDtypeStruct((states, width), jnp.float32),
            jax.ShapeDtypeStruct((STEP, width), jnp.float32),
        ],
        compiler_params=params(),
        cost_estimate=cost(rows, width, states, 6),
        name="scan_local",
    )(dt, x, b_t, rates)
    return state, jnp.sum(total, 0, keepdims=True)


def value_scan(dt, x, b_t, c_t, rates, entering):
    rows, width = dt.shape
    states = rates.shape[0]
    by_row = pl.BlockSpec((LANES, width), lambda s: (s, 0))
    by_lane = pl.BlockSpec((states, LANES), lambda s: (0, s))
    wide = whole((states, width))
    return pl.pallas_call(
        value_kernel,
        grid=(rows // LANES,),
        in_specs=[by_row, by_row, by_lane, by_lane, wide, wide],
        out_specs=by_row,
        out_shape=jax.ShapeDtypeStruct((rows, width), jnp.float32),
        scratch_shapes=[pltpu.VMEM((states, width), jnp.float32)],
        compiler_params=params(),
        cost_estimate=cost(rows, width, states, 8),
        name="scan_value",
    )(dt, x, b_t, c_t, rates, entering)


def push_scan(dt, dy, c_t, rates):
    rows, width = dt.shape
    states = rates.shape[0]
    last = rows // LANES - 1
    by_row = pl.BlockSpec((LANES, width), lambda s: (last - s, 0))
    by_lane = pl.BlockSpec((states, LANES), lambda s: (0, last - s))
    wide = whole((states, width))
    return pl.pallas_call(
        push_kernel,
        grid=(rows // LANES,),
        in_specs=[by_row, by_row, by_lane, wide],
        out_specs=wide,
        out_shape=jax.ShapeDtypeStruct((states, width), jnp.float32),
        compiler_params=params(),
        cost_estimate=cost(rows, width, states, 6),
        name="scan_push",
    )(dt, dy, c_t, rates)


def back_scan(dt, x, dy, b_t, c_t, rates, entering, future):
    rows, width = dt.shape
    states = rates.shape[0]
    half = rows // LANES
    both = lambda s: jnp.where(s < half, s, 2 * half - 1 - s)
    late = lambda s: jnp.where(s < half, half - 1, 2 * half - 1 - s)
    row_both = pl.BlockSpec((LANES, width), lambda s: (both(s), 0))
    lane_both = pl.BlockSpec((states, LANES), lambda s: (0, both(s)))
    row_late = pl.BlockSpec((LANES, width), lambda s: (late(s), 0))
    lane_late = pl.BlockSpec((states, LANES), lambda s: (0, late(s)))
    wide = whole((states, width))
    return pl.pallas_call(
        functools.partial(back_kernel, half),
        grid=(2 * half,),
        in_specs=[row_both, row_both, row_late, lane_both, lane_late, wide, wide, wide],
        out_specs=[row_late, row_late, lane_late, lane_late, wide],
        out_shape=[
            jax.ShapeDtypeStruct((rows, width), jnp.float32),
            jax.ShapeDtypeStruct((rows, width), jnp.float32),
            jax.ShapeDtypeStruct((states, rows), jnp.float32),
            jax.ShapeDtypeStruct((states, rows), jnp.float32),
            jax.ShapeDtypeStruct((states, width), jnp.float32),
        ],
        scratch_shapes=[
            pltpu.VMEM((rows, states, width), jnp.float32),
            pltpu.VMEM((states, width), jnp.float32),
        ],
        compiler_params=params(),
        cost_estimate=cost(rows, width, states, 20),
        name="scan_back",
    )(dt, x, dy, b_t, c_t, rates, entering, future)


BLOCK = 64
PAD_ROWS = 32


def bf(value):
    return value.astype(jnp.bfloat16)


def fl(value):
    return value.astype(jnp.float32)


def dot(left, right, contract):
    return lax.dot_general(
        left, right, (contract, ((), ())), preferred_element_type=jnp.float32
    )


def mm(left, right):
    return dot(left, right, ((1,), (0,)))


def mm_t(left, right):
    return dot(left, right, ((1,), (1,)))


def t_mm(left, right):
    return dot(left, right, ((0,), (0,)))


def swap(value):
    return lax.ppermute(value, "w", [(0, 1), (1, 0)])


def pull(value, axis, amount):
    count = lax.axis_size(axis)
    return lax.ppermute(value, axis, [((i + amount) % count, i) for i in range(count)])


def around(value, axis):
    return [value] + [pull(value, axis, k) for k in range(1, lax.axis_size(axis))]


def ordered(pieces, axis):
    count = len(pieces)
    ring = jnp.stack(pieces + pieces[:-1])
    start = lax.rem(count - lax.axis_index(axis), count)
    return lax.dynamic_slice_in_dim(ring, start, count, 0)


def pick(value, index, dim):
    return lax.dynamic_index_in_dim(value, index, dim, keepdims=False)


def sum_group(value):
    value = value + swap(value)
    value = value + lax.ppermute(value, "y", [(0, 1), (1, 0), (2, 3), (3, 2)])
    return value + lax.ppermute(value, "y", [(0, 3), (3, 0), (1, 2), (2, 1)])


def finish_scatter(parts):
    total = parts[0]
    count = len(parts)
    for k in range(1, count):
        route = [(i, (i + k) % count) for i in range(count)]
        total = total + fl(lax.ppermute(bf(parts[k]), "y", route))
    return total


def scatter_near(part):
    rows, width = part.shape
    split = part.reshape(2, 4, rows // 8, width)
    summed = split[0] + fl(swap(bf(split[1])))
    return finish_scatter([summed[k] for k in range(4)])


def scatter_true(part):
    rows, width = part.shape
    mine, half = lax.axis_index("y"), lax.axis_index("w")
    split = part.reshape(4, 2, rows // 8, width)
    summed = pick(split, half, 1) + fl(swap(bf(pick(split, 1 - half, 1))))
    return finish_scatter([pick(summed, lax.rem(mine + k, 4), 0) for k in range(4)])


def gather_near(value):
    stacked = jnp.stack(around(value, "y"))
    return jnp.stack((stacked, swap(stacked))).reshape(-1, value.shape[-1])


def gather_true(value):
    stacked = ordered(around(value, "y"), "y")
    other = swap(stacked)
    first = lax.axis_index("w") == 0
    both = jnp.stack((jnp.where(first, stacked, other), jnp.where(first, other, stacked)), 1)
    return both.reshape(-1, value.shape[-1])


def by_half(own, other, dim):
    first = lax.axis_index("w") == 0
    return jnp.concatenate((jnp.where(first, own, other), jnp.where(first, other, own)), dim)


def chain(value, rates, axis, backward):
    states = rates.shape[0]
    pieces = ordered(around(value, axis), axis)
    count = pieces.shape[0]
    mine = lax.axis_index(axis)
    before = jnp.zeros_like(value)
    total = jnp.zeros_like(value)

    def join(earlier, later):
        decay = jnp.exp(rates * later[states:])
        return jnp.concatenate(
            (decay * earlier[:states] + later[:states], earlier[states:] + later[states:]), 0
        )

    for k in range(count - 1, -1, -1) if backward else range(count):
        ahead = k > mine if backward else k < mine
        before = jnp.where(ahead, join(before, pieces[k]), before)
        total = join(total, pieces[k])
    return before, total


def entering(state, steps, rates, backward):
    states = rates.shape[0]
    value = jnp.concatenate((state, steps), 0)
    near, total = chain(value, rates, "z", backward)
    far, _ = chain(total, rates, "x", backward)
    return jnp.exp(rates * near[states:]) * far[:states] + near[:states]


def from_behind(block, axes, distance):
    count = 1
    for axis in axes:
        count *= lax.axis_size(axis)
    route = [(i - distance, i) for i in range(count) if 0 <= i - distance < count]
    return lax.ppermute(block, axes, route)


def selector(width):
    place = jnp.arange(width, dtype=jnp.int32)
    block = width // BLOCK
    target = place + (PAD_ROWS - block) * (place // block)
    return bf(target[:, None] == jnp.arange(BLOCK * PAD_ROWS, dtype=jnp.int32)[None])


def pad_gain(gain):
    block = gain.shape[0] // BLOCK
    return jnp.pad(gain.reshape(BLOCK, block), ((0, 0), (0, PAD_ROWS - block))).reshape(-1)


def trim_gain(gain, width):
    return gain.reshape(BLOCK, PAD_ROWS)[:, : width // BLOCK].reshape(-1)


def trim_wide(value, chosen):
    top = lax.reduce_precision(value, 8, 7)
    return mm_t(bf(top), chosen) + mm_t(bf(value - top), chosen)


def norm_apply(values, gain):
    return values * lax.rsqrt(jnp.mean(values * values, -1, keepdims=True) + epsilon) * gain


def norm_scale(values, width):
    return lax.rsqrt(jnp.sum(values * values, -1, keepdims=True) / width + epsilon)


def norm_back(values, scale, gain, grad, width):
    pushed = grad * gain
    along = jnp.sum(pushed * values, -1, keepdims=True) / width
    return pushed * scale - values * (scale * scale * scale) * along, jnp.sum(
        grad * values * scale, 0
    )


def swiglu_gate(gate_part, up_part):
    return jax.nn.silu(gate_part) * up_part


def widen(value, dim, size):
    pads = [(0, 0)] * value.ndim
    pads[dim] = (0, size - value.shape[dim])
    return jnp.pad(value, pads)


def round_up(value, unit):
    return -(-value // unit) * unit


def chunked(weight):
    rows, parts, columns = weight.shape
    wide = round_up(columns // 4, 128)
    cut = widen(weight.reshape(rows, parts, 4, columns // 4), 3, wide)
    cut = jnp.transpose(cut, (2, 0, 1, 3)).reshape(4, rows, parts * wide)
    return widen(cut, 1, PAD_ROWS)


def unchunked(grad, rows, parts, columns):
    wide = grad.shape[2] // parts
    cut = grad[:, :rows].reshape(4, rows, parts, wide)[..., : columns // 4]
    return fl(jnp.transpose(cut, (1, 2, 0, 3)).reshape(rows, parts, columns))


def to_chunks(packed):
    moved = lax.all_to_all(packed, "y", 0, 0)
    return moved.reshape(-1, packed.shape[-1])


def gather_rows(rows):
    return lax.all_gather(rows, ("x", "z"), axis=0, tiled=True)


def settle(grad):
    rows = lax.psum_scatter(bf(grad), ("x", "z"), scatter_dimension=0, tiled=True)
    return rows.reshape(4, -1, rows.shape[-1])


def visible_mask(query_rows, key_rows, first_pos, key_first):
    query_pos = first_pos + jnp.arange(query_rows, dtype=jnp.int32)
    key_pos = key_first + jnp.arange(key_rows, dtype=jnp.int32)
    earlier = key_pos[None, :] <= query_pos[:, None]
    nearby = key_pos[None, :] > query_pos[:, None] - WINDOW
    return earlier & nearby & (key_pos[None, :] >= 0)


def head_scores(queries, keys_all, visible, score_scale):
    scores = (
        jnp.einsum("tkgd,skd->kgts", queries, keys_all, preferred_element_type=jnp.float32)
        * score_scale
    )
    return jnp.where(visible, scores, -1e30)


def attend_forward(queries, keys_all, values_all, visible, score_scale):
    scores = head_scores(queries, keys_all, visible, score_scale)
    row_max = jnp.max(scores, -1, keepdims=True)
    lifted = jnp.exp(scores - row_max)
    row_total = jnp.sum(lifted, -1, keepdims=True)
    probability = (lifted / row_total).astype(jnp.bfloat16)
    mixed_heads = jnp.einsum(
        "kgts,skd->tkgd", probability, values_all, preferred_element_type=jnp.float32
    )
    return (mixed_heads.reshape(mixed_heads.shape[0], -1), row_max + jnp.log(row_total))


def attend_backward(queries, keys_all, values_all, visible, score_scale, log_total, heads_grad):
    scores = head_scores(queries, keys_all, visible, score_scale)
    probability = jnp.where(visible, jnp.exp(scores - log_total), 0.0)
    prob_grad = jnp.einsum(
        "tkgd,skd->kgts", heads_grad, values_all, preferred_element_type=jnp.float32
    )
    row_delta = jnp.sum(probability * prob_grad, -1, keepdims=True)
    score_grad = (probability * (prob_grad - row_delta)).astype(jnp.bfloat16)
    query_grad = (
        jnp.einsum("kgts,skd->tkgd", score_grad, keys_all, preferred_element_type=jnp.float32)
        * score_scale
    )
    key_grad = (
        jnp.einsum("kgts,tkgd->skd", score_grad, queries, preferred_element_type=jnp.float32)
        * score_scale
    )
    value_grad = jnp.einsum(
        "kgts,tkgd->skd",
        probability.astype(jnp.bfloat16),
        heads_grad,
        preferred_element_type=jnp.float32,
    )
    return (query_grad, key_grad, value_grad)


def conv_apply(extended, conv_taps, conv_bias):
    tap_count = conv_taps.shape[0]
    out_rows = extended.shape[0] - tap_count + 1
    summed = conv_bias + conv_taps[0] * extended[0:out_rows]
    for offset in range(1, tap_count):
        summed = summed + conv_taps[offset] * extended[offset : offset + out_rows]
    return jax.nn.silu(summed)


def shards(
    tokens,
    norm_gain,
    qkv_weight,
    heads_gain,
    mamba_in,
    conv_weight,
    conv_bias,
    state_proj,
    step_proj,
    step_bias,
    decay_log,
    skip_gain,
    mamba_gain,
    heads_out,
    mamba_out,
    mlp_gain,
    gate_up,
    down_proj,
    cotangent,
):
    tok_rows, width = tokens.shape
    shard_rows = qkv_weight.shape[0]
    inner_half = conv_weight.shape[1]
    inner = inner_half // 4
    lanes = round_up(inner, 128)
    hidden_half = gate_up.shape[2]
    hidden = round_up(hidden_half // 4, 128)
    heads_width = KV_HEADS * GROUP * HEAD
    kv_width = KV_HEADS * HEAD
    half_width = heads_width // 2
    qkv_half = qkv_weight.shape[1] // 2
    halo_count = WINDOW // tok_rows
    score_scale = HEAD ** (-0.5)
    x_pos, z_pos = lax.axis_index("x"), lax.axis_index("z")
    y_pos, w_pos = lax.axis_index("y"), lax.axis_index("w")
    group_axes, all_axes = ("x", "z"), ("x", "z", "y")
    own_rows = tok_rows // 2
    rank = step_proj.shape[0]

    def own_half(value, dim=0):
        size = value.shape[dim] // 2
        return lax.dynamic_slice_in_dim(value, w_pos * size, size, dim)

    def own_block(value):
        return lax.dynamic_slice_in_dim(value, y_pos * tok_rows, tok_rows, 0)

    def channels(value, dim):
        part = lax.dynamic_slice_in_dim(value, y_pos * inner, inner, dim)
        return widen(fl(part), dim, lanes)

    in_full = gather_rows(to_chunks(chunked(mamba_in)))
    rest = to_chunks(
        jnp.concatenate(
            (chunked(mamba_out[:, None]), chunked(gate_up), chunked(down_proj[:, None])), 2
        )
    )
    near_rows = jnp.concatenate((own_half(qkv_weight, 1), heads_out), 1)
    near_full = lax.all_gather(
        widen(near_rows, 0, PAD_ROWS), all_axes, axis=0, tiled=True
    )
    qkv_full = near_full[:, :qkv_half]
    hout_full = near_full[:, qkv_half:]
    rest_full = gather_rows(rest)
    mout_full = rest_full[:, :lanes]
    gu_full = rest_full[:, lanes : lanes + 2 * hidden]
    down_full = rest_full[:, lanes + 2 * hidden :]

    chosen = selector(width)
    gain_first = pad_gain(norm_gain)
    gain_mid = pad_gain(mlp_gain)
    tokens_group = ordered(around(tokens, "y"), "y").reshape(4 * tok_rows, width)
    residual = mm(tokens_group, chosen)
    scale_first = norm_scale(residual, width)
    normed = bf(residual * scale_first * gain_first)
    normed_own = own_block(normed)

    mixed_in = bf(mm(normed, in_full))
    conv_in = mixed_in[:, :lanes]
    gate_float = fl(mixed_in[:, lanes:])
    tail = from_behind(conv_in[-(CONV - 1) :], group_axes, 1)
    extended = fl(jnp.concatenate((tail, conv_in), 0))
    conv_taps = channels(conv_weight, 1)
    conv_shift = channels(conv_bias, 0)
    acted_b = bf(conv_apply(extended, conv_taps, conv_shift))
    acted = fl(acted_b)
    state_weight = bf(channels(state_proj, 0))
    state_t = sum_group(dot(state_weight, acted_b, ((0,), (1,))))
    low_rank_t = bf(state_t[:rank])
    input_t = state_t[rank : rank + STATE]
    output_t = state_t[rank + STATE :]
    step_weight = bf(channels(step_proj, 1))
    step_pre = t_mm(low_rank_t, step_weight) + channels(step_bias, 0)
    steps = jax.nn.softplus(step_pre)
    rates = -jnp.exp(channels(decay_log, 0)).T
    local_state, step_total = local_scan(steps, acted, input_t, rates)
    carry_in = entering(local_state, step_total, rates, False)

    first_pos = (lax.axis_index(all_axes)) * tok_rows
    projected_half = bf(mm(normed_own, qkv_full))
    projected = by_half(projected_half, swap(projected_half), 1)
    queries = projected[:, :heads_width].reshape(tok_rows, KV_HEADS, GROUP, HEAD)
    own_pair = projected[:, heads_width:]
    sent = own_half(own_pair, 1)
    halo_half = jnp.concatenate(
        [from_behind(sent, all_axes, k) for k in range(halo_count, 0, -1)], 0
    )
    halo_pair = by_half(halo_half, swap(halo_half), 1)
    pair_all = jnp.concatenate((halo_pair, own_pair), 0)
    keys_all = pair_all[:, :kv_width].reshape(-1, KV_HEADS, HEAD)
    values_all = pair_all[:, kv_width:].reshape(-1, KV_HEADS, HEAD)
    visible = visible_mask(
        tok_rows, pair_all.shape[0], first_pos, first_pos - halo_count * tok_rows
    )
    heads_value, log_total = attend_forward(queries, keys_all, values_all, visible, score_scale)
    heads_normed = norm_apply(heads_value, heads_gain)
    heads_half = bf(own_half(heads_normed, 1))
    heads_part = mm_t(heads_half, hout_full)

    skip = channels(skip_gain, 0)
    ssm_value = value_scan(steps, acted, input_t, output_t, rates, carry_in) + skip * acted
    gate_act = jax.nn.silu(gate_float)
    gated = ssm_value * gate_act
    square_total = sum_group(jnp.sum(gated * gated, -1))
    mamba_scale = lax.rsqrt(square_total / INNER + epsilon)[:, None]
    gain_mamba = channels(mamba_gain, 0)
    mamba_normed = bf(gated * mamba_scale * gain_mamba)

    def add_block(value, block):
        held = own_block(value) + block
        return lax.dynamic_update_slice_in_dim(value, held, y_pos * tok_rows, 0)

    mixer = 0.5 * scatter_true(add_block(mm_t(mamba_normed, mout_full), heads_part))
    own_tokens = mm(own_half(tokens), chosen)
    middle = own_tokens + mixer
    scale_mid = norm_scale(middle, width)

    normed_mid = gather_near(bf(middle * scale_mid * gain_mid))
    cot_own = bf(mm(own_half(cotangent), chosen))
    cot_near = gather_near(cot_own)
    gate_values = mm(normed_mid, gu_full)
    gate_part, up_part = gate_values[:, :hidden], gate_values[:, hidden:]
    hidden_b = bf(swiglu_gate(gate_part, up_part))
    mlp = scatter_near(mm_t(hidden_b, down_full))
    out_half = bf(mm_t(bf(middle + mlp), chosen))
    layer_out = by_half(out_half, swap(out_half), 0)
    hidden_grad = mm(cot_near, down_full)
    gate_grad, up_grad = jax.vjp(swiglu_gate, gate_part, up_part)[1](hidden_grad)
    gate_values_grad = bf(jnp.concatenate((gate_grad, up_grad), 1))
    mid_grad = scatter_near(mm_t(gate_values_grad, gu_full))
    mid_back, mlp_gain_grad = norm_back(middle, scale_mid, gain_mid, mid_grad, width)
    middle_grad = fl(cot_own) + mid_back
    gu_rows = settle(t_mm(normed_mid, gate_values_grad))
    down_rows = settle(t_mm(cot_near, hidden_b))

    mixer_grad = gather_true(bf(middle_grad))
    mamba_normed_grad = 0.5 * mm(mixer_grad, mout_full)
    half_grad = 0.5 * mm(own_block(mixer_grad), hout_full)
    heads_cut = widen(heads_half.reshape(tok_rows, 4, half_width // 4), 2, 256)
    heads_chunk = to_chunks(jnp.transpose(heads_cut, (1, 0, 2)))
    out_rows = settle(
        0.5 * t_mm(mixer_grad, jnp.concatenate((mamba_normed, heads_chunk), 1))
    )
    row_total = sum_group(jnp.sum(mamba_normed_grad * gain_mamba * gated, -1))
    gated_grad = (
        mamba_normed_grad * gain_mamba * mamba_scale
        - gated * mamba_scale**3 * row_total[:, None] / INNER
    )
    mamba_gain_grad = jnp.sum(mamba_normed_grad * gated * mamba_scale, 0)
    ssm_grad = gated_grad * gate_act
    gate_in_grad = jax.vjp(jax.nn.silu, gate_float)[1](gated_grad * ssm_value)[0]
    push = push_scan(steps, ssm_grad, output_t, rates)
    future = entering(push, step_total, rates, True)

    heads_normed_grad = by_half(half_grad, swap(half_grad), 1)
    heads_value_grad, heads_gain_grad = jax.vjp(norm_apply, heads_value, heads_gain)[1](
        heads_normed_grad
    )
    heads_grad = bf(heads_value_grad).reshape(tok_rows, KV_HEADS, GROUP, HEAD)
    query_grad, key_grad, value_grad = attend_backward(
        queries, keys_all, values_all, visible, score_scale, log_total, heads_grad
    )
    key_grad = key_grad.reshape(-1, kv_width)
    value_grad = value_grad.reshape(-1, kv_width)
    pair_half = jnp.where(w_pos == 0, key_grad, value_grad)
    own_pair_grad = pair_half[halo_count * tok_rows :]
    for amount in range(halo_count, 0, -1):
        first = (halo_count - amount) * tok_rows
        own_pair_grad = own_pair_grad + fl(
            from_behind(bf(pair_half[first : first + tok_rows]), all_axes, -amount)
        )
    own_pair_grad = bf(own_pair_grad)
    projected_grad = jnp.concatenate(
        (
            bf(query_grad.reshape(tok_rows, heads_width)),
            by_half(own_pair_grad, swap(own_pair_grad), 1),
        ),
        1,
    )
    projected_grad_half = own_half(projected_grad, 1)
    heads_back = mm_t(projected_grad_half, qkv_full)
    qkv_cut = widen(projected_grad_half.reshape(tok_rows, 4, qkv_half // 4), 2, 384)
    qkv_chunk = to_chunks(jnp.transpose(qkv_cut, (1, 0, 2)))

    step_grad, acted_core_grad, input_grad_t, output_grad_t, rate_grad = back_scan(
        steps, acted, ssm_grad, input_t, output_t, rates, carry_in, future
    )
    acted_core_grad = acted_core_grad + skip * ssm_grad
    skip_grad = jnp.sum(ssm_grad * acted, 0)
    step_pre_grad = step_grad * jax.nn.sigmoid(step_pre)
    step_bias_grad = jnp.sum(step_pre_grad, 0)
    step_pre_b = bf(step_pre_grad)
    step_proj_grad = mm(low_rank_t, step_pre_b)
    low_rank_grad_t = mm_t(step_weight, step_pre_b)
    state_grad_t = bf(
        sum_group(jnp.concatenate((low_rank_grad_t, input_grad_t, output_grad_t), 0))
    )
    state_proj_grad_t = mm(state_grad_t, acted_b)
    acted_grad = acted_core_grad + dot(state_grad_t, state_weight, ((0,), (1,)))
    extended_grad, conv_weight_grad, conv_bias_grad = jax.vjp(
        conv_apply, extended, conv_taps, conv_shift
    )[1](acted_grad)
    returned = from_behind(extended_grad[: CONV - 1], group_axes, -1)
    group_rows = 4 * tok_rows
    conv_in_grad = jnp.concatenate(
        (extended_grad[CONV - 1 : group_rows], extended_grad[group_rows:] + returned), 0
    )
    mixed_in_grad = bf(jnp.concatenate((conv_in_grad, gate_in_grad), 1))
    in_rows = settle(t_mm(normed, jnp.concatenate((mixed_in_grad, qkv_chunk), 1)))
    normed_grad = scatter_true(add_block(mm_t(mixed_in_grad, in_full), heads_back))
    own_scale = own_half(own_block(scale_first))
    first_back, norm_gain_grad = norm_back(
        own_tokens, own_scale, gain_first, normed_grad, width
    )
    tokens_half = trim_wide(middle_grad + first_back, chosen)
    tokens_grad = by_half(tokens_half, swap(tokens_half), 0)

    out_moved = lax.all_to_all(
        jnp.concatenate((gu_rows, down_rows, out_rows), 2), "y", 0, 0
    )
    in_moved = lax.all_to_all(in_rows, "y", 0, 0)
    gu_settled = unchunked(out_moved[:, :, : 2 * hidden], shard_rows, 2, hidden_half)
    down_settled = unchunked(
        out_moved[:, :, 2 * hidden : 3 * hidden], shard_rows, 1, hidden_half
    )[:, 0]
    mout_settled = unchunked(
        out_moved[:, :, 3 * hidden : 3 * hidden + lanes], shard_rows, 1, inner_half
    )[:, 0]
    hout_settled = unchunked(out_moved[:, :, 3 * hidden + lanes :], shard_rows, 1, half_width)[
        :, 0
    ]
    in_settled = unchunked(in_moved[:, :, : 2 * lanes], shard_rows, 2, inner_half)
    qkv_own = unchunked(in_moved[:, :, 2 * lanes :], shard_rows, 1, qkv_half)[:, 0]
    qkv_settled = by_half(qkv_own, swap(qkv_own), 1)

    inner_rows = jnp.concatenate(
        (
            state_proj_grad_t,
            step_proj_grad,
            rate_grad * rates,
            conv_weight_grad,
            conv_bias_grad[None],
            step_bias_grad[None],
            skip_grad[None],
            mamba_gain_grad[None],
        ),
        0,
    )
    gains = jnp.concatenate(
        (norm_gain_grad, mlp_gain_grad, 0.5 * widen(heads_gain_grad, 0, BLOCK * PAD_ROWS))
    ).reshape(-1, lanes)
    gains = gains + swap(gains)
    small = lax.psum(jnp.concatenate((inner_rows, gains), 0), group_axes)
    small = lax.all_gather(small, "y", axis=0)
    gains = jnp.sum(small[:, inner_rows.shape[0] :], 0).reshape(3, -1)
    by_channel = jnp.transpose(small[:, : inner_rows.shape[0], :inner], (1, 0, 2)).reshape(
        -1, inner_half
    )
    ends = state_proj.shape[1] + rank
    last = ends + STATE + CONV
    return (
        layer_out,
        tokens_grad,
        trim_gain(gains[0], width),
        qkv_settled,
        gains[2, :heads_width],
        in_settled,
        by_channel[ends + STATE : last],
        by_channel[last],
        by_channel[: state_proj.shape[1]].T,
        by_channel[state_proj.shape[1] : ends],
        by_channel[last + 1],
        by_channel[ends : ends + STATE].T,
        by_channel[last + 2],
        by_channel[last + 3],
        hout_settled,
        mout_settled,
        trim_gain(gains[1], width),
        gu_settled,
        down_settled,
    )


def solution(mesh):
    split = Mesh(mesh.devices.reshape(4, 4, 4, 2), ("x", "z", "y", "w"))
    ctx = ("x", "z", "y")
    placed = (
        P(ctx, None),
        P(),
        P(ctx, None),
        P(),
        P(ctx, None, "w"),
        P(None, "w"),
        P("w"),
        P("w", None),
        P(None, "w"),
        P("w"),
        P("w", None),
        P("w"),
        P("w"),
        P(ctx, "w"),
        P(ctx, "w"),
        P(),
        P(ctx, None, "w"),
        P(ctx, "w"),
        P(ctx, None),
    )
    return jax.shard_map(
        shards,
        mesh=split,
        in_specs=placed,
        out_specs=(
            P(ctx, None),
            P(ctx, None),
            P(),
            P(ctx, None),
            P(),
            P(ctx, None, "w"),
            P(None, "w"),
            P("w"),
            P("w", None),
            P(None, "w"),
            P("w"),
            P("w", None),
            P("w"),
            P("w"),
            P(ctx, "w"),
            P(ctx, "w"),
            P(),
            P(ctx, None, "w"),
            P(ctx, "w"),
        ),
        check_vma=False,
    )
```

time: 3810 us -> 1070 us (0.28); the launches traced: 3760 us -> 1060 us
  local copies, waits for them, and re-layouts: 1210 us -> 78.1 us
  blocking collectives: 805 us -> 29.3 us
  other arithmetic: 520 us -> 57.6 us
  starting transfers between devices: 384 us -> 157 us
  waiting for transfers between devices: 641 us -> 505 us
  Pallas kernels: 0 us -> 81.5 us
  matrix products: 181 us -> 137 us
    pad x70 -> x6, local copies, waits for them, and re-layouts: 805 us -> 0.06 us  [the longest x4 0.04 us: widen(): return jnp.pad(value, pads)]
    unnamed x2 -> x0, blocking collectives: 793 us -> none
    unnamed x58 -> x0, starting transfers between devices: 338 us -> none
    reduce_scatter x0 -> x4, waiting for transfers between devices: none -> 243 us  [settle(): lax.psum_scatter(bf(grad), ('x', 'z'), scatter_dimension=0, tiled=True)]
    all_gather x9 -> x4, waiting for transfers between devices: 252 us -> 47 us  [the longest x1 31 us: shards(): small = lax.all_gather(small, 'y', axis=0)]
    unnamed x548 -> x251, local copies, waits for them, and re-layouts: 220 us -> 22.9 us
    unnamed x74 -> x9, waiting for transfers between devices: 180 us -> 0.15 us
    select_n x126 -> x21, other arithmetic: 130 us -> 2.23 us  [the longest x6 2.07 us: by_half(): jnp.where(first, own, other)]
  transfers between devices with their start and end apart: 90 -> 93, of which waited for: 16 -> 57; matrix products, arithmetic and copies ran while one was open for 47% -> 20% of each run, Pallas kernels for 0% -> 8%
where the time goes in v1:
time: 1070 us; the launch traced here: 1060 us
  waiting for transfers between devices  505 us (47%)
  starting transfers between devices  157 us (15%)
  matrix products  137 us (13%)
  Pallas kernels  81.5 us (8%)
  local copies, waits for them, and re-layouts  78.1 us (7%)
  other arithmetic  57.6 us (5%)
  blocking collectives  29.3 us (3%)
  between operations  17 us (2%)
    reduce_scatter x4, waiting for transfers between devices, settle(): lax.psum_scatter(bf(grad), ('x', 'z'), scatter_dimension=0, tiled=True)  243 us
    dot_general x28, matrix products, dot(): lax.dot_general(left, right, (contract, ((), ())), preferred_element_type...  97.4 us
    psum x1, waiting for transfers between devices, shards(): small = lax.psum(jnp.concatenate((inner_rows, gains), 0), group_axes)  68.9 us
    ppermute x24, waiting for transfers between devices, pull(): lax.ppermute(value, axis, [((i + amount) % count, i) for i in range(count)])  46 us
    pallas_call x1, Pallas kernels, back_scan(): pl.pallas_call(functools.partial(back_kernel, half), grid=(2 * half,), in...  45.3 us
    ppermute x18, starting transfers between devices, from_behind(): return lax.ppermute(block, axes, route)  45.2 us
    ppermute x12, waiting for transfers between devices, finish_scatter(): total = total + fl(lax.ppermute(bf(parts[k]), 'y', route))  41.7 us
    ppermute x19, starting transfers between devices, swap(): return lax.ppermute(value, 'w', [(0, 1), (1, 0)])  37.6 us
  transfers between devices with their start and end apart: 93, of which 57 were waited for; matrix products, arithmetic and copies ran while one was open for 20% of the time, Pallas kernels for 8%

profile of v1, /device:TPU:1, one launch (start us, length us, event | category | flops | bytes accessed | tf_op | source)
XLA Modules:
  0.0 1063.1 jit_solution(3801048823344228969)
XLA Ops:
  9.4 10.5 all_to_all.30
  32.7 6.7 collective-permute-done.1
  53.7 5.9 multiply_reduce_fusion.1
  60.1 13.4 %all-gather.5.cloned.1.call-done = bf16[2048,1024]{1,0:T(8,128)(2,1)} async-done(((bf16[128,1024]{1,0:T(8,128)(2,1)}), bf16[2048,1024]{1,0:T(8,128)(2,1)}) %all-gather.5.cloned.1.call-update) | async-done | bytes 4194320 | tf_op jit(solution)/shard_map/all_gather | solution.py:534
  89.7 6.9 collective-permute-done.5
  107.3 11.2 %scan_local.1 = (f32[16,512]{1,0:T(8,128)S(1)}, f32[8,512]{1,0:T(8,128)S(1)}) custom-call(f32[512,512]{1,0:T(8,128)S(1)} %get-tuple-element.267.dt_ref, f32[512,512]{1,0:T(8,128)S(1)} %get-tuple-element.192.x_ref, f32[16,512]{1,0:T(8,128)S(1)} %get-tuple-element.244.b_ref, f32[16,512]{1,0:T(8,128)S(1)} %negate_bitcast_fusion.rate_ref), custom_call_target="tpu_custom_call" | custom-call | flops 25165824 | bytes 4194304 | tf_op jit(solution)/shard_map/scan_local/pallas_call | solution.py:237
  136.9 14.2 %scan_value.1 = f32[512,512]{1,0:T(8,128)S(1)} custom-call(f32[512,512]{1,0:T(8,128)S(1)} %get-tuple-element.267.dt_ref, f32[512,512]{1,0:T(8,128)S(1)} %get-tuple-element.192.x_ref, f32[16,512]{1,0:T(8,128)S(1)} %get-tuple-element.244.b_ref, f32[16,512]{1,0:T(8,128)S(1)} %get-tuple-element.243.c_ref, f32[16,512]{1,0:T(8,128)S(1)} %negate_bitcast_fusion.rate_ref, ...), custom_call_target="tpu_custom_call" | custom-call | flops 33554432 | bytes 4194304 | tf_op jit(solution)/shard_map/scan_value/pallas_call | solution.py:259
  201.7 6.1 collective-permute-start.21
  211.4 6.1 collective-permute-start.25
  221.1 7.4 fusion.231
  228.5 7.5 fusion.8
  236.1 8.0 fusion.106
  311.4 6.4 fusion.22
  337.1 6.4 collective-permute-done.45
  383.7 10.8 %scan_push.1 = f32[16,512]{1,0:T(8,128)S(1)} custom-call(f32[512,512]{1,0:T(8,128)S(1)} %get-tuple-element.267.dt_ref, f32[512,512]{1,0:T(8,128)S(1)} %get-tuple-element.146.dy_ref, f32[16,512]{1,0:T(8,128)S(1)} %get-tuple-element.243.c_ref, f32[16,512]{1,0:T(8,128)S(1)} %negate_bitcast_fusion.rate_ref), custom_call_target="tpu_custom_call" | custom-call | flops 25165824 | bytes 4194304 | tf_op jit(solution)/shard_map/scan_push/pallas_call | solution.py:279
  394.6 6.4 collective-permute-start.55
  419.6 45.3 %scan_back.1 = (f32[512,512]{1,0:T(8,128)S(1)}, f32[512,512]{1,0:T(8,128)S(1)}, f32[16,512]{1,0:T(8,128)S(1)}, f32[16,512]{1,0:T(8,128)S(1)}, f32[16,512]{1,0:T(8,128)S(1)}) custom-call(f32[512,512]{1,0:T(8,128)S(1)} %get-tuple-element.267.dt_ref, f32[512,512]{1,0:T(8,128)S(1)} %get-tuple-element.192.x_ref, f32[512,512]{1,0:T(8,128)S(1)} %get-tuple-element.146.dy_ref, ...), custom_call_target="tpu_custom_call" | custom-call | flops 83886080 | bytes 4194304 | tf_op jit(solution)/shard_map/scan_back/pallas_call | solution.py:302
  469.2 13.1 %multiply_reduce_fusion = (f32[5,5,128]{2,1,0:T(8,128)S(1)}, f32[5,5,128,1152]{2,3,1,0:T(8,128)}) fusion(f32[5,5,128,1152]{2,3,1,0:T(8,128)} %get-tuple-element.270, f32[5,5,128]{2,1,0:T(8,128)S(1)} %log_add_fusion, pred[128,1152]{0,1:T(8,128)(4,1)S(1)} %and_and_fusion, bf16[1152,5,64,1]{0,2,3,1:T(8,128)(2,1)S(1)} %bitcast.567, ...), kind=kOutput, calls=%fused_computation.5 | convolution fusion | flops 486601600 | bytes 30811136 | tf_op jit(solution)/shard_map/tkgd,skd->kgts/dot_general | solution.py:573
  482.3 10.7 %multiply_convert_fusion = bf16[5,5,128,1152]{2,3,1,0:T(8,128)(2,1)S(1)} fusion(f32[5,5,128,1152]{2,3,1,0:T(8,128)} %get-tuple-element.275, f32[5,5,128,1152]{2,3,1,0:T(8,128)} %get-tuple-element.270, f32[5,5,128]{2,1,0:T(8,128)S(1)} %get-tuple-element.274, f32[5,5,128]{2,1,0:T(8,128)S(1)} %log_add_fusion, pred[128,1152]{0,1:T(8,128)(4,1)S(1)} %and_and_fusion), kind=kLoop, calls=%fused_computation.4 | loop fusion | flops 18432000 | bytes 37037056 | tf_op jit(solution)/shard_map/convert_element_type | solution.py:577
  495.4 7.7 fusion.232
  569.2 6.5 collective-permute-done.76
  590.6 8.8 all_to_all.31
  606.3 6.8 convolution_convert_fusion
  613.1 68.9 %all-reduce.32.cloned.1.call-done = f32[1,268,512]{2,1,0:T(8,128)} async-done(((f32[1,268,512]{2,1,0:T(8,128)}), f32[1,268,512]{2,1,0:T(8,128)}) %all-reduce.32.cloned.1.call-update) | async-done | bytes 548880 | tf_op jit(solution)/shard_map/psum | solution.py:876
  682.2 10.0 all_to_all.32
  693.2 6.6 convolution_convert_fusion.1
  714.0 6.6 collective-permute-done.35
  738.8 21.2 %reduce-scatter.9.cloned.1.call-done = bf16[128,768]{1,0:T(8,128)(2,1)} async-done(((bf16[2048,768]{1,0:T(8,128)(2,1)}), bf16[128,768]{1,0:T(8,128)(2,1)}) %reduce-scatter.9.cloned.1.call-update) | async-done | bytes 196624 | tf_op jit(solution)/shard_map/reduce_scatter | solution.py:538
  759.9 78.2 %reduce-scatter.11.cloned.1.call-done = bf16[128,768]{1,0:T(8,128)(2,1)} async-done(((bf16[2048,768]{1,0:T(8,128)(2,1)}), bf16[128,768]{1,0:T(8,128)(2,1)}) %reduce-scatter.11.cloned.1.call-update) | async-done | bytes 196624 | tf_op jit(solution)/shard_map/reduce_scatter | solution.py:538
  838.1 84.7 %reduce-scatter.7.cloned.1.call-done = bf16[128,1536]{1,0:T(8,128)(2,1)} async-done(((bf16[2048,1536]{1,0:T(8,128)(2,1)}), bf16[128,1536]{1,0:T(8,128)(2,1)}) %reduce-scatter.7.cloned.1.call-update) | async-done | bytes 393232 | tf_op jit(solution)/shard_map/reduce_scatter | solution.py:538
  929.2 31.0 %all-gather.11.cloned.1.call-done = f32[4,268,512]{2,1,0:T(8,128)} async-done(((f32[1,268,512]{2,1,0:T(8,128)}), f32[4,268,512]{2,1,0:T(8,128)}) %all-gather.11.cloned.1.call-update) | async-done | bytes 2195472 | tf_op jit(solution)/shard_map/all_gather | solution.py:877
  981.5 58.5 %reduce-scatter.5.cloned.1.call-done = bf16[128,1408]{1,0:T(8,128)(2,1)} async-done(((bf16[2048,1408]{1,0:T(8,128)(2,1)}), bf16[128,1408]{1,0:T(8,128)(2,1)}) %reduce-scatter.5.cloned.1.call-update) | async-done | bytes 360464 | tf_op jit(solution)/shard_map/reduce_scatter | solution.py:538
  (728 shorter events, 447.7 us)
Async XLA Ops:
  7.3 66.2 %all-gather.5.cloned.1.call-start = ((), (), s32[]{:S(2)}) async-start(), calls=%async_computation.10 | async-start | bytes 4456448 | tf_op jit(solution)/shard_map/all_gather | solution.py:534
  19.9 137.3 %all-gather.9.cloned.1.call-start = ((), (), s32[]{:S(2)}) async-start(), calls=%async_computation.12 | async-start | bytes 7987200 | tf_op jit(solution)/shard_map/all_gather | solution.py:662
  21.8 18.4 %collective-permute-start.2 = (bf16[128,1600]{0,1:T(8,128)(2,1)S(1)}, bf16[128,1600]{0,1:T(8,128)(2,1)S(1)}, u32[]{:S(2)}, u32[]{:S(2)}) collective-permute-start(bf16[128,1600]{0,1:T(8,128)(2,1)S(1)} %copy-done.43), channel_id=1, source_target_pairs={{6,0},{0,2},{2,4},{4,6},{7,1},{1,3},{3,5},{5,7},{14,8},{8,10},{10,... | collective-permute-start | bytes 1228808 | tf_op jit(solution)/shard_map/ppermute | solution.py:360
  22.4 17.0 %collective-permute-start.1 = (bf16[128,1600]{0,1:T(8,128)(2,1)S(1)}, bf16[128,1600]{0,1:T(8,128)(2,1)S(1)}, u32[]{:S(2)}, u32[]{:S(2)}) collective-permute-start(bf16[128,1600]{0,1:T(8,128)(2,1)S(1)} %copy-done.43), channel_id=1, source_target_pairs={{4,0},{6,2},{0,4},{2,6},{5,1},{7,3},{1,5},{3,7},{12,8},{14,10},{8,... | collective-permute-start | bytes 1228808 | tf_op jit(solution)/shard_map/ppermute | solution.py:360
  26.5 20.4 %all-to-all-start.1 = ((bf16[4,32,2816]{2,1,0:T(8,128)(2,1)}), bf16[4,32,2816]{2,1,0:T(8,128)(2,1)S(1)}, u32[]{:S(2)}, u32[]{:S(2)}) async-start(bf16[4,32,2816]{2,1,0:T(8,128)(2,1)} %copy.128), calls=%async_computation.1 | async-start | bytes 1441792 | tf_op jit(solution)/shard_map/all_to_all | solution.py:529
  30.0 218.5 %all-gather.7.cloned.1.call-start = ((), (), s32[]{:S(2)}) async-start(), calls=%async_computation.11 | async-start | bytes 12255232 | tf_op jit(solution)/shard_map/all_gather | solution.py:534
  47.8 634.3 %all-reduce.32.cloned.1.call-start = ((), (), s32[]{:S(2)}) async-start(), calls=%async_computation.13 | async-start | bytes 1114112 | tf_op jit(solution)/shard_map/psum | solution.py:876
  167.8 18.6 %collective-permute-start.17 = (bf16[128,320]{0,1:T(8,128)(2,1)S(1)}, bf16[128,320]{0,1:T(8,128)(2,1)}, u32[]{:S(2)}, u32[]{:S(2)}) collective-permute-start(bf16[128,320]{0,1:T(8,128)(2,1)S(1)} %constant_dynamic-slice_fusion.16), channel_id=1, source_target_pairs={{0,16},{2,18},{4,20},{6,22},{8,24},{10,26},{12,28},{14,30},{16,32}... | collective-permute-start | bytes 245768 | tf_op jit(solution)/shard_map/ppermute | solution.py:460
  173.1 44.4 %collective-permute-start.15 = (f32[512]{0:T(512)S(1)}, f32[512]{0:T(512)S(1)}, u32[]{:S(2)}, u32[]{:S(2)}) collective-permute-start(f32[512]{0:T(512)S(1)} %add.690), channel_id=1, source_target_pairs={{0,6},{6,0},{2,4},{4,2},{1,7},{7,1},{3,5},{5,3},{8,14},{14,8},{10,... | collective-permute-start | bytes 6152 | tf_op jit(solution)/shard_map/ppermute | solution.py:381
  176.4 35.0 %collective-permute-start.24 = (bf16[128,320]{0,1:T(8,128)(2,1)S(1)}, bf16[128,320]{0,1:T(8,128)(2,1)S(1)}, u32[]{:S(2)}, u32[]{:S(2)}) collective-permute-start(bf16[128,320]{0,1:T(8,128)(2,1)S(1)} %constant_dynamic-slice_fusion.16), channel_id=1, source_target_pairs={{0,2},{2,4},{4,6},{6,8},{8,10},{10,12},{12,14},{14,16},{16,18},{18... | collective-permute-start | bytes 245768 | tf_op jit(solution)/shard_map/ppermute | solution.py:460
  179.2 32.2 %collective-permute-start.23 = (bf16[128,320]{0,1:T(8,128)(2,1)S(1)}, bf16[128,320]{0,1:T(8,128)(2,1)S(1)}, u32[]{:S(2)}, u32[]{:S(2)}) collective-permute-start(bf16[128,320]{0,1:T(8,128)(2,1)S(1)} %constant_dynamic-slice_fusion.16), channel_id=1, source_target_pairs={{0,4},{2,6},{4,8},{6,10},{8,12},{10,14},{12,16},{14,18},{16,20},{1... | collective-permute-start | bytes 245768 | tf_op jit(solution)/shard_map/ppermute | solution.py:460
  181.4 29.9 %collective-permute-start.22 = (bf16[128,320]{0,1:T(8,128)(2,1)S(1)}, bf16[128,320]{0,1:T(8,128)(2,1)S(1)}, u32[]{:S(2)}, u32[]{:S(2)}) collective-permute-start(bf16[128,320]{0,1:T(8,128)(2,1)S(1)} %constant_dynamic-slice_fusion.16), channel_id=1, source_target_pairs={{0,6},{2,8},{4,10},{6,12},{8,14},{10,16},{12,18},{14,20},{16,22},{... | collective-permute-start | bytes 245768 | tf_op jit(solution)/shard_map/ppermute | solution.py:460
  264.7 14.9 %collective-permute-start.40 = (bf16[64,2048]{1,0:T(8,128)(2,1)}, bf16[64,2048]{1,0:T(8,128)(2,1)}, u32[]{:S(2)}, u32[]{:S(2)}) collective-permute-start(bf16[64,2048]{1,0:T(8,128)(2,1)} %fusion.63), channel_id=1, source_target_pairs={{4,0},{6,2},{0,4},{2,6},{5,1},{7,3},{1,5},{3,7},{12,8},{14,10},{8,... | collective-permute-start | bytes 786440 | tf_op jit(solution)/shard_map/ppermute | solution.py:360
  267.1 12.4 %collective-permute-start.39 = (bf16[64,2048]{1,0:T(8,128)(2,1)}, bf16[64,2048]{1,0:T(8,128)(2,1)}, u32[]{:S(2)}, u32[]{:S(2)}) collective-permute-start(bf16[64,2048]{1,0:T(8,128)(2,1)} %fusion.63), channel_id=1, source_target_pairs={{2,0},{4,2},{6,4},{0,6},{3,1},{5,3},{7,5},{1,7},{10,8},{12,10},{14... | collective-permute-start | bytes 786440 | tf_op jit(solution)/shard_map/ppermute | solution.py:360
  271.9 13.8 %collective-permute-start.27 = (bf16[64,2048]{1,0:T(8,128)(2,1)}, bf16[64,2048]{1,0:T(8,128)(2,1)}, u32[]{:S(2)}, u32[]{:S(2)}) collective-permute-start(bf16[64,2048]{1,0:T(8,128)(2,1)} %get-tuple-element.204), channel_id=1, source_target_pairs={{0,2},{2,4},{4,6},{6,0},{1,3},{3,5},{5,7},{7,1},{8,10},{10,12},{12... | collective-permute-start | bytes 786440 | tf_op jit(solution)/shard_map/ppermute | solution.py:389
  273.1 12.6 %collective-permute-start.29 = (bf16[64,2048]{1,0:T(8,128)(2,1)}, bf16[64,2048]{1,0:T(8,128)(2,1)}, u32[]{:S(2)}, u32[]{:S(2)}) collective-permute-start(bf16[64,2048]{1,0:T(8,128)(2,1)} %get-tuple-element.205), channel_id=1, source_target_pairs={{0,6},{2,0},{4,2},{6,4},{1,7},{3,1},{5,3},{7,5},{8,14},{10,8},{12,... | collective-permute-start | bytes 786440 | tf_op jit(solution)/shard_map/ppermute | solution.py:389
  274.6 16.2 %collective-permute-start.28 = (bf16[64,2048]{1,0:T(8,128)(2,1)}, bf16[64,2048]{1,0:T(8,128)(2,1)}, u32[]{:S(2)}, u32[]{:S(2)}) collective-permute-start(bf16[64,2048]{1,0:T(8,128)(2,1)} %get-tuple-element.206), channel_id=1, source_target_pairs={{0,4},{2,6},{4,0},{6,2},{1,5},{3,7},{5,1},{7,3},{8,12},{10,14},{12... | collective-permute-start | bytes 786440 | tf_op jit(solution)/shard_map/ppermute | solution.py:389
  280.9 28.0 %collective-permute-start.42 = (bf16[4,64,2048]{2,1,0:T(8,128)(2,1)S(1)}, bf16[4,64,2048]{2,1,0:T(8,128)(2,1)S(1)}, u32[]{:S(2)}, u32[]{:S(2)}) collective-permute-start(bf16[4,64,2048]{2,1,0:T(8,128)(2,1)S(1)} %get-tuple-element.219), channel_id=1, source_target_pairs={{0,1},{1,0},{2,3},{3,2},{4,5},{5,4},{6,7},{7,6},{8,9},{9,8},{10,11... | collective-permute-start | bytes 3145736 | tf_op jit(solution)/shard_map/ppermute | solution.py:355
  293.1 13.7 %collective-permute-start.30 = (bf16[64,2048]{1,0:T(8,128)(2,1)S(1)}, bf16[64,2048]{1,0:T(8,128)(2,1)S(1)}, u32[]{:S(2)}, u32[]{:S(2)}) collective-permute-start(bf16[64,2048]{1,0:T(8,128)(2,1)S(1)} %multiply_convert_fusion.7), channel_id=1, source_target_pairs={{2,0},{4,2},{6,4},{0,6},{3,1},{5,3},{7,5},{1,7},{10,8},{12,10},{14... | collective-permute-start | bytes 786440 | tf_op jit(solution)/shard_map/ppermute | solution.py:360
  331.0 12.5 %collective-permute-start.45 = (bf16[64,2048]{1,0:T(8,128)(2,1)S(1)}, bf16[64,2048]{1,0:T(8,128)(2,1)S(1)}, u32[]{:S(2)}, u32[]{:S(2)}) collective-permute-start(bf16[64,2048]{1,0:T(8,128)(2,1)S(1)} %get-tuple-element.217), channel_id=1, source_target_pairs={{0,4},{2,6},{4,0},{6,2},{1,5},{3,7},{5,1},{7,3},{8,12},{10,14},{12... | collective-permute-start | bytes 786440 | tf_op jit(solution)/shard_map/ppermute | solution.py:389
  380.1 87.9 %collective-permute-start.64 = (f32[128,800]{0,1:T(8,128)S(1)}, f32[128,800]{0,1:T(8,128)S(1)}, u32[]{:S(2)}, u32[]{:S(2)}) collective-permute-start(f32[128,800]{0,1:T(8,128)S(1)} %fusion.84), channel_id=1, source_target_pairs={{0,1},{1,0},{2,3},{3,2},{4,5},{5,4},{6,7},{7,6},{8,9},{9,8},{10,11... | collective-permute-start | bytes 1228808 | tf_op jit(solution)/shard_map/ppermute | solution.py:355
  394.6 13.1 %collective-permute-start.55 = (f32[17,512]{1,0:T(8,128)S(1)}, f32[17,512]{1,0:T(8,128)S(1)}, u32[]{:S(2)}, u32[]{:S(2)}) collective-permute-start(f32[17,512]{1,0:T(8,128)S(1)} %pad_maximum_fusion.16), channel_id=1, source_target_pairs={{16,0},{24,8},{0,16},{8,24},{17,1},{25,9},{1,17},{9,25},{18,2},{26... | collective-permute-start | bytes 104456 | tf_op jit(solution)/shard_map/ppermute | solution.py:360
  465.5 43.1 %collective-permute-start.60 = (f32[132,512]{1,0:T(8,128)S(1)}, f32[132,512]{1,0:T(8,128)S(1)}, u32[]{:S(2)}, u32[]{:S(2)}) collective-permute-start(f32[132,512]{1,0:T(8,128)S(1)} %pad_maximum_fusion.15), channel_id=1, source_target_pairs={{0,1},{1,0},{2,3},{3,2},{4,5},{5,4},{6,7},{7,6},{8,9},{9,8},{10,11... | collective-permute-start | bytes 811016 | tf_op jit(solution)/shard_map/ppermute | solution.py:355
  513.6 12.9 %collective-permute-start.66 = (bf16[128,320]{0,1:T(8,128)(2,1)S(1)}, bf16[128,320]{0,1:T(8,128)(2,1)S(1)}, u32[]{:S(2)}, u32[]{:S(2)}) collective-permute-start(bf16[128,320]{0,1:T(8,128)(2,1)S(1)} %bitcast.611), channel_id=1, source_target_pairs={{14,0},{16,2},{18,4},{20,6},{22,8},{24,10},{26,12},{28,14},{30,16}... | collective-permute-start | bytes 245768 | tf_op jit(solution)/shard_map/ppermute | solution.py:460
  516.2 13.1 %collective-permute-start.61 = (f32[132,512]{1,0:T(8,128)S(1)}, f32[132,512]{1,0:T(8,128)S(1)}, u32[]{:S(2)}, u32[]{:S(2)}) collective-permute-start(f32[132,512]{1,0:T(8,128)S(1)} %fusion.211), channel_id=1, source_target_pairs={{0,2},{2,0},{4,6},{6,4},{1,3},{3,1},{5,7},{7,5},{8,10},{10,8},{12,... | collective-permute-start | bytes 811016 | tf_op jit(solution)/shard_map/ppermute | solution.py:380
  562.5 13.2 %collective-permute-start.76 = (bf16[64,2048]{1,0:T(8,128)(2,1)}, bf16[64,2048]{1,0:T(8,128)(2,1)}, u32[]{:S(2)}, u32[]{:S(2)}) collective-permute-start(bf16[64,2048]{1,0:T(8,128)(2,1)} %get-tuple-element.201), channel_id=1, source_target_pairs={{0,4},{2,6},{4,0},{6,2},{1,5},{3,7},{5,1},{7,3},{8,12},{10,14},{12... | collective-permute-start | bytes 786440 | tf_op jit(solution)/shard_map/ppermute | solution.py:389
  584.4 175.5 %reduce-scatter.9.cloned.1.call-start = ((), (), s32[]{:S(2)}) async-start(), calls=%async_computation.17 | async-start | bytes 3342336 | tf_op jit(solution)/shard_map/reduce_scatter | solution.py:538
  589.7 248.4 %reduce-scatter.11.cloned.1.call-start = ((), (), s32[]{:S(2)}) async-start(), calls=%async_computation.18 | async-start | bytes 3342336 | tf_op jit(solution)/shard_map/reduce_scatter | solution.py:538
  604.7 318.1 %reduce-scatter.7.cloned.1.call-start = ((), (), s32[]{:S(2)}) async-start(), calls=%async_computation.16 | async-start | bytes 6684672 | tf_op jit(solution)/shard_map/reduce_scatter | solution.py:538
  613.1 347.1 %all-gather.11.cloned.1.call-start = ((), (), s32[]{:S(2)}) async-start(), calls=%async_computation.14 | async-start | bytes 2785280 | tf_op jit(solution)/shard_map/all_gather | solution.py:877
  682.1 357.9 %reduce-scatter.5.cloned.1.call-start = ((), (), s32[]{:S(2)}) async-start(), calls=%async_computation.15 | async-start | bytes 6127616 | tf_op jit(solution)/shard_map/reduce_scatter | solution.py:538
  925.0 53.7 %all-to-all-start.5 = ((bf16[4,32,3072]{2,1,0:T(8,128)(2,1)}), bf16[4,32,3072]{2,1,0:T(8,128)(2,1)}, u32[]{:S(2)}, u32[]{:S(2)}) async-start(bf16[4,32,3072]{2,1,0:T(8,128)(2,1)} %pad_maximum_fusion.11), calls=%async_computation.9 | async-start | bytes 1572864 | tf_op jit(solution)/shard_map/all_to_all | solution.py:841
  (168 other events, 1926.5 us)
Sparse Core Ops, SparseCore 0:
  20.0 53.4 all-gather.4
  76.8 77.7 all-gather.8
  157.4 91.0 all-gather.6
  584.5 97.5 all-reduce.31
  685.3 74.6 reduce-scatter.8
  763.1 74.9 reduce-scatter.10
  841.5 81.2 reduce-scatter.6
  924.4 35.6 all-gather.10
  963.5 76.4 reduce-scatter.4

commit v2 on v1

v2 whole, which is shorter than its diff:
```python
import functools

import jax
import jax.numpy as jnp
from jax import lax
from jax.experimental import pallas as pl
from jax.experimental.pallas import tpu as pltpu
from jax.sharding import Mesh, PartitionSpec as P

KV_HEADS = 5
GROUP = 5
HEAD = 64
INNER = 3200
STATE = 16
CONV = 4
WINDOW = 1024
STEP = 64
CHAIN = 64
SPREAD = 32
LANES = 128
MIB = 1024 * 1024
LOG2 = 0.6931471805599453

epsilon = 1e-06


def row(ref, index, like):
    return jnp.broadcast_to(ref[pl.ds(index, 1), :], like.shape)


def column(block, index, like):
    return jnp.broadcast_to(block[:, index : index + 1], like.shape)


def turned(block, start):
    return pltpu.roll(block, lax.rem(LANES - start, LANES), 1)


def local_kernel(dt_ref, u_ref, b_ref, rate_ref, out_ref):
    @pl.when(pl.program_id(0) == 0)
    def _():
        out_ref[...] = jnp.zeros_like(out_ref)

    rates = rate_ref[...]
    b_all = b_ref[...]

    def block(j, state):
        start = pl.multiple_of(j * STEP, STEP)
        b_cols = turned(b_all, start)
        for i in range(STEP):
            decay = jnp.exp2(row(dt_ref, start + i, state) * rates)
            state = decay * state + row(u_ref, start + i, state) * column(b_cols, i, state)
        return state

    out_ref[...] = lax.fori_loop(0, dt_ref.shape[0] // STEP, block, out_ref[...])


def value_kernel(dt_ref, u_ref, b_ref, c_ref, rate_ref, enter_ref, out_ref, kept_ref, state_ref):
    @pl.when(pl.program_id(0) == 0)
    def _():
        state_ref[...] = enter_ref[...]

    rates = rate_ref[...]
    b_all = b_ref[...]
    c_all = c_ref[...]

    def block(j, state):
        start = pl.multiple_of(j * STEP, STEP)
        b_cols = turned(b_all, start)
        c_cols = turned(c_all, start)
        rows = []
        for i in range(STEP):
            kept_ref[start + i] = state
            decay = jnp.exp2(row(dt_ref, start + i, state) * rates)
            state = decay * state + row(u_ref, start + i, state) * column(b_cols, i, state)
            rows.append(jnp.sum(state * column(c_cols, i, state), 0, keepdims=True))
        out_ref[pl.ds(start, STEP), :] = jnp.concatenate(rows, 0)
        return state

    state_ref[...] = lax.fori_loop(0, dt_ref.shape[0] // STEP, block, state_ref[...])


def push_kernel(dt_ref, dy_ref, c_ref, rate_ref, out_ref):
    @pl.when(pl.program_id(0) == 0)
    def _():
        out_ref[...] = jnp.zeros_like(out_ref)

    rates = rate_ref[...]
    c_all = c_ref[...]
    count = dt_ref.shape[0] // STEP

    def block(k, push):
        start = pl.multiple_of((count - 1 - k) * STEP, STEP)
        c_cols = turned(c_all, start)
        for i in range(STEP - 1, -1, -1):
            decay = jnp.exp2(row(dt_ref, start + i, push) * rates)
            push = decay * (push + row(dy_ref, start + i, push) * column(c_cols, i, push))
        return push

    out_ref[...] = lax.fori_loop(0, count, block, out_ref[...])


def back_kernel(
    dt_ref,
    u_ref,
    dy_ref,
    b_ref,
    c_ref,
    rate_ref,
    kept_ref,
    future_ref,
    first_ref,
    second_ref,
    db_ref,
    dc_ref,
    drate_ref,
    push_ref,
    adjoint_ref,
    moved_ref,
    db_wide_ref,
    dc_wide_ref,
):
    @pl.when(pl.program_id(0) == 0)
    def _():
        push_ref[...] = future_ref[...]
        drate_ref[...] = jnp.zeros_like(drate_ref)

    rates = rate_ref[...]
    b_all = b_ref[...]
    c_all = c_ref[...]
    rows = dt_ref.shape[0]
    states = rates.shape[0]

    def chain(k, push):
        start = pl.multiple_of((rows // CHAIN - 1 - k) * CHAIN, CHAIN)
        c_cols = turned(c_all, start)
        for i in range(CHAIN - 1, -1, -1):
            decay = jnp.exp2(row(dt_ref, start + i, push) * rates)
            adjoint = push + row(dy_ref, start + i, push) * column(c_cols, i, push)
            adjoint_ref[start + i] = adjoint
            moved_ref[start + i] = decay * kept_ref[start + i]
            push = decay * adjoint
        return push

    push_ref[...] = lax.fori_loop(0, rows // CHAIN, chain, push_ref[...])

    def fold(wide):
        parts = wide[:, :LANES]
        for first in range(LANES, wide.shape[1], LANES):
            parts = parts + wide[:, first : first + LANES]
        return parts

    def spread(k, drate):
        start = pl.multiple_of(k * SPREAD, SPREAD)
        b_cols = turned(b_all, start)
        first_rows = []
        second_rows = []
        for i in range(SPREAD):
            adjoint = adjoint_ref[start + i]
            moved = moved_ref[start + i]
            u_wide = row(u_ref, start + i, moved)
            b_wide = column(b_cols, i, moved)
            dc_wide_ref[start + i] = fold(row(dy_ref, start + i, moved) * (moved + u_wide * b_wide))
            db_wide_ref[start + i] = fold(adjoint * u_wide)
            mixed = adjoint * moved
            drate = drate + row(dt_ref, start + i, moved) * mixed
            first_rows.append(jnp.sum(rates * mixed, 0, keepdims=True))
            second_rows.append(jnp.sum(adjoint * b_wide, 0, keepdims=True))
        first_ref[pl.ds(start, SPREAD), :] = jnp.concatenate(first_rows, 0)
        second_ref[pl.ds(start, SPREAD), :] = jnp.concatenate(second_rows, 0)
        return drate

    drate_ref[...] = lax.fori_loop(0, rows // SPREAD, spread, drate_ref[...])
    ones = jnp.ones((8, LANES), jnp.float32)
    for wide_ref, out_ref in ((db_wide_ref, db_ref), (dc_wide_ref, dc_ref)):
        out_ref[...] = lax.dot_general(
            ones,
            wide_ref[...].reshape(rows * states, LANES),
            (((1,), (1,)), ((), ())),
            precision=lax.Precision.HIGHEST,
            preferred_element_type=jnp.float32,
        )


def whole(shape):
    return pl.BlockSpec(shape, lambda s: (0,) * len(shape))


def params():
    return pltpu.CompilerParams(
        dimension_semantics=("arbitrary",), vmem_limit_bytes=40 * MIB
    )


def cost(rows, width, states, ops):
    return pl.CostEstimate(
        flops=rows * width * states * ops,
        bytes_accessed=rows * width * 16,
        transcendentals=rows * width * states,
    )


def real(*shape):
    return jax.ShapeDtypeStruct(shape, jnp.float32)


def local_scan(dt, u, b_t, rates):
    rows, width = dt.shape
    states = rates.shape[0]
    by_row = pl.BlockSpec((LANES, width), lambda s: (s, 0))
    by_lane = pl.BlockSpec((states, LANES), lambda s: (0, s))
    return pl.pallas_call(
        local_kernel,
        grid=(rows // LANES,),
        in_specs=[by_row, by_row, by_lane, whole((states, width))],
        out_specs=whole((states, width)),
        out_shape=real(states, width),
        compiler_params=params(),
        cost_estimate=cost(rows, width, states, 6),
        name="scan_local",
    )(dt, u, b_t, rates)


def value_scan(dt, u, b_t, c_t, rates, entering):
    rows, width = dt.shape
    states = rates.shape[0]
    by_row = pl.BlockSpec((LANES, width), lambda s: (s, 0))
    by_lane = pl.BlockSpec((states, LANES), lambda s: (0, s))
    wide = whole((states, width))
    return pl.pallas_call(
        value_kernel,
        grid=(rows // LANES,),
        in_specs=[by_row, by_row, by_lane, by_lane, wide, wide],
        out_specs=[by_row, pl.BlockSpec((LANES, states, width), lambda s: (s, 0, 0))],
        out_shape=[real(rows, width), real(rows, states, width)],
        scratch_shapes=[pltpu.VMEM((states, width), jnp.float32)],
        compiler_params=params(),
        cost_estimate=cost(rows, width, states, 8),
        name="scan_value",
    )(dt, u, b_t, c_t, rates, entering)


def push_scan(dt, dy, c_t, rates):
    rows, width = dt.shape
    states = rates.shape[0]
    last = rows // LANES - 1
    by_row = pl.BlockSpec((LANES, width), lambda s: (last - s, 0))
    by_lane = pl.BlockSpec((states, LANES), lambda s: (0, last - s))
    wide = whole((states, width))
    return pl.pallas_call(
        push_kernel,
        grid=(rows // LANES,),
        in_specs=[by_row, by_row, by_lane, wide],
        out_specs=wide,
        out_shape=real(states, width),
        compiler_params=params(),
        cost_estimate=cost(rows, width, states, 6),
        name="scan_push",
    )(dt, dy, c_t, rates)


def back_scan(dt, u, dy, b_t, c_t, rates, kept, future):
    rows, width = dt.shape
    states = rates.shape[0]
    last = rows // LANES - 1
    by_row = pl.BlockSpec((LANES, width), lambda s: (last - s, 0))
    by_lane = pl.BlockSpec((states, LANES), lambda s: (0, last - s))
    flat = pl.BlockSpec((8, LANES * states), lambda s: (0, last - s))
    held = pl.BlockSpec((LANES, states, width), lambda s: (last - s, 0, 0))
    wide = whole((states, width))
    first, second, db, dc, drate = pl.pallas_call(
        back_kernel,
        grid=(rows // LANES,),
        in_specs=[by_row, by_row, by_row, by_lane, by_lane, wide, held, wide],
        out_specs=[by_row, by_row, flat, flat, wide],
        out_shape=[
            real(rows, width),
            real(rows, width),
            real(8, rows * states),
            real(8, rows * states),
            real(states, width),
        ],
        scratch_shapes=[
            pltpu.VMEM((states, width), jnp.float32),
            pltpu.VMEM((LANES, states, width), jnp.float32),
            pltpu.VMEM((LANES, states, width), jnp.float32),
            pltpu.VMEM((LANES, states, LANES), jnp.float32),
            pltpu.VMEM((LANES, states, LANES), jnp.float32),
        ],
        compiler_params=params(),
        cost_estimate=cost(rows, width, states, 20),
        name="scan_back",
    )(dt, u, dy, b_t, c_t, rates, kept, future)
    return first, second, db[0].reshape(rows, states).T, dc[0].reshape(rows, states).T, drate

def stacked_heads(ref, head, group):
    first = head * group * HEAD
    parts = [ref[:, first + g * HEAD : first + (g + 1) * HEAD] for g in range(group)]
    return jnp.concatenate(parts, 0)


def flat_heads(value, group):
    rows = value.shape[0] // group
    return jnp.concatenate([value[g * rows : (g + 1) * rows] for g in range(group)], 1)


def over(left, right):
    return lax.dot_general(
        left, right, (((1,), (1,)), ((), ())), preferred_element_type=jnp.float32
    )


def down(left, right):
    return lax.dot_general(
        left, right, (((0,), (0,)), ((), ())), preferred_element_type=jnp.float32
    )


def biased_scores(queries, keys, bias, scale):
    scores = over(queries, keys)
    tokens = bias.shape[0]
    return (scores.reshape(-1, tokens, scores.shape[1]) * scale + bias[None]).reshape(scores.shape)


def attend_kernel(
    scale, first_ref, q_ref, mine_ref, other_ref, own_ref, bias_ref, out_ref, log_ref, all_ref
):
    bias = bias_ref[...]
    halo, width = mine_ref.shape
    half = first_ref[1]
    all_ref[half, :halo] = mine_ref[...]
    all_ref[1 - half, :halo] = other_ref[...]
    all_ref[0, halo:] = own_ref[:, :width]
    all_ref[1, halo:] = own_ref[:, width:]
    seen = pl.ds(pl.multiple_of(first_ref[0], HEAD), bias.shape[1])
    key_ref, value_ref = all_ref.at[0, seen], all_ref.at[1, seen]
    outs = []
    for head in range(KV_HEADS):
        queries = stacked_heads(q_ref, head, GROUP)
        keys = key_ref[:, head * HEAD : (head + 1) * HEAD]
        values = value_ref[:, head * HEAD : (head + 1) * HEAD]
        scores = biased_scores(queries, keys, bias, scale)
        row_max = jnp.max(scores, 1, keepdims=True)
        lifted = jnp.exp(scores - row_max)
        row_total = jnp.sum(lifted, 1, keepdims=True)
        probability = (lifted * (1.0 / row_total)).astype(jnp.bfloat16)
        outs.append(
            flat_heads(jnp.dot(probability, values, preferred_element_type=jnp.float32), GROUP)
        )
        log_ref[head] = row_max + jnp.log(row_total)
    out_ref[...] = jnp.concatenate(outs, 1)


def attend_back_kernel(
    scale, first_ref, q_ref, all_ref, bias_ref, log_ref, grad_ref, dq_ref, dpair_ref
):
    bias = bias_ref[...]
    seen = pl.ds(pl.multiple_of(first_ref[0], HEAD), bias.shape[1])
    key_ref, value_ref = all_ref.at[0, seen], all_ref.at[1, seen]
    dqs, dks, dvs = [], [], []
    for head in range(KV_HEADS):
        queries = stacked_heads(q_ref, head, GROUP)
        grad = stacked_heads(grad_ref, head, GROUP)
        keys = key_ref[:, head * HEAD : (head + 1) * HEAD]
        values = value_ref[:, head * HEAD : (head + 1) * HEAD]
        probability = jnp.exp(biased_scores(queries, keys, bias, scale) - log_ref[head])
        prob_grad = over(grad, values)
        delta = jnp.sum(probability * prob_grad, 1, keepdims=True)
        score_grad = (probability * (prob_grad - delta)).astype(jnp.bfloat16)
        dq = jnp.dot(score_grad, keys, preferred_element_type=jnp.float32) * scale
        dqs.append(flat_heads(dq, GROUP))
        dks.append(down(score_grad, queries) * scale)
        dvs.append(down(probability.astype(jnp.bfloat16), grad))
    dq_ref[...] = jnp.concatenate(dqs, 1).astype(dq_ref.dtype)
    dpair_ref[...] = jnp.zeros_like(dpair_ref)
    dpair_ref[0, seen] = jnp.concatenate(dks, 1)
    dpair_ref[1, seen] = jnp.concatenate(dvs, 1)


def attend_cost(rows, keys, products):
    return pl.CostEstimate(
        flops=2 * rows * GROUP * KV_HEADS * keys * HEAD * products,
        bytes_accessed=keys * KV_HEADS * HEAD * 12,
        transcendentals=rows * GROUP * KV_HEADS * keys,
    )


def in_smem():
    return pl.BlockSpec(memory_space=pltpu.SMEM)


def in_vmem(count):
    return [pl.BlockSpec(memory_space=pltpu.VMEM)] * count


def attend(first, queries, mine, other, own, bias, scale):
    rows, width = queries.shape
    keys = mine.shape[0] + own.shape[0]
    return pl.pallas_call(
        functools.partial(attend_kernel, scale),
        in_specs=[in_smem()] + in_vmem(5),
        out_shape=[
            real(rows, width),
            real(KV_HEADS, GROUP * rows, 1),
            jax.ShapeDtypeStruct((2, keys, KV_HEADS * HEAD), jnp.bfloat16),
        ],
        compiler_params=pltpu.CompilerParams(vmem_limit_bytes=40 * MIB),
        cost_estimate=attend_cost(rows, keys, 8),
        name="attend",
    )(first, queries, mine, other, own, bias)


def attend_back(first, queries, pair, bias, log_total, grad, scale):
    rows, width = queries.shape
    return pl.pallas_call(
        functools.partial(attend_back_kernel, scale),
        in_specs=[in_smem()] + in_vmem(5),
        out_shape=[
            jax.ShapeDtypeStruct((rows, width), jnp.bfloat16),
            real(*pair.shape),
        ],
        compiler_params=pltpu.CompilerParams(vmem_limit_bytes=40 * MIB),
        cost_estimate=attend_cost(rows, pair.shape[1], 20),
        name="attend_back",
    )(first, queries, pair, bias, log_total, grad)


def weights_kernel(first_ref, first_grad_ref, second_ref, second_grad_ref, out_ref):
    split = first_grad_ref.shape[1]
    out_ref[:, :split] = down(first_ref[...], first_grad_ref[...]).astype(out_ref.dtype)
    out_ref[:, split:] = down(second_ref[...], second_grad_ref[...]).astype(out_ref.dtype)


def weight_grads(first, first_grad, second, second_grad):
    tokens, rows = first.shape
    split, wide = first_grad.shape[1], first_grad.shape[1] + second_grad.shape[1]
    tile = 256
    by_column = pl.BlockSpec((tokens, tile), lambda s: (0, s))
    return pl.pallas_call(
        weights_kernel,
        grid=(rows // tile,),
        in_specs=[by_column, whole(first_grad.shape), by_column, whole(second_grad.shape)],
        out_specs=pl.BlockSpec((tile, wide), lambda s: (s, 0)),
        out_shape=jax.ShapeDtypeStruct((rows, wide), jnp.bfloat16),
        compiler_params=params(),
        cost_estimate=pl.CostEstimate(
            flops=2 * tokens * rows * wide,
            bytes_accessed=2 * (2 * tokens * rows + tokens * wide + rows * wide),
            transcendentals=0,
        ),
        name="weight_grads",
    )(first, first_grad, second, second_grad)


BLOCK = 64
PAD_ROWS = 32


def bf(value):
    return value.astype(jnp.bfloat16)


def fl(value):
    return value.astype(jnp.float32)


def dot(left, right, contract):
    return lax.dot_general(
        left, right, (contract, ((), ())), preferred_element_type=jnp.float32
    )


def mm(left, right):
    return dot(left, right, ((1,), (0,)))


def mm_t(left, right):
    return dot(left, right, ((1,), (1,)))


def t_mm(left, right):
    return dot(left, right, ((0,), (0,)))


def swap(value):
    return lax.ppermute(value, "w", [(0, 1), (1, 0)])


def pull(value, axis, amount):
    count = lax.axis_size(axis)
    return lax.ppermute(value, axis, [((i + amount) % count, i) for i in range(count)])


def around(value, axis):
    return [value] + [pull(value, axis, k) for k in range(1, lax.axis_size(axis))]


def ordered(pieces, axis):
    count = len(pieces)
    ring = jnp.stack(pieces + pieces[:-1])
    start = lax.rem(count - lax.axis_index(axis), count)
    return lax.dynamic_slice_in_dim(ring, start, count, 0)


def pick(value, index, dim):
    return lax.dynamic_index_in_dim(value, index, dim, keepdims=False)


def sum_group(value):
    value = value + fl(swap(bf(value)))
    sent = bf(value)
    for k in range(1, 4):
        value = value + fl(pull(sent, "y", k))
    return value


def finish_scatter(parts):
    total = parts[0]
    count = len(parts)
    for k in range(1, count):
        route = [(i, (i + k) % count) for i in range(count)]
        total = total + fl(lax.ppermute(bf(parts[k]), "y", route))
    return total


def scatter_true(part):
    rows, width = part.shape
    mine, half = lax.axis_index("y"), lax.axis_index("w")
    split = part.reshape(4, 2, rows // 8, width)
    summed = pick(split, half, 1) + fl(swap(bf(pick(split, 1 - half, 1))))
    return finish_scatter([pick(summed, lax.rem(mine + k, 4), 0) for k in range(4)])


def arrange_kernel(place_ref, own_ref, other_ref, out_ref):
    half = place_ref[1]
    out_ref[0, half] = own_ref[0]
    out_ref[0, 1 - half] = other_ref[0]


def arrange(own, other):
    count, rows, width = own.shape
    place = jnp.stack((lax.axis_index("y"), lax.axis_index("w")))
    block = pl.BlockSpec(
        (1, rows, width), lambda s, place_ref: (lax.rem(s + count - place_ref[0], count), 0, 0)
    )
    return pl.pallas_call(
        arrange_kernel,
        grid_spec=pltpu.PrefetchScalarGridSpec(
            num_scalar_prefetch=1,
            grid=(count,),
            in_specs=[block, block],
            out_specs=pl.BlockSpec((1, 2, rows, width), lambda s, place_ref: (s, 0, 0, 0)),
        ),
        out_shape=jax.ShapeDtypeStruct((count, 2, rows, width), own.dtype),
        compiler_params=params(),
        cost_estimate=pl.CostEstimate(
            flops=0, bytes_accessed=8 * count * rows * width, transcendentals=0
        ),
        name="arrange",
    )(place, own, other).reshape(-1, width)


def gather_true(value):
    stacked = jnp.stack(around(value, "y"))
    return arrange(stacked, swap(stacked))


def by_half(own, other, dim):
    first = lax.axis_index("w") == 0
    return jnp.concatenate((jnp.where(first, own, other), jnp.where(first, other, own)), dim)


def exchange(pieces, axes):
    return lax.all_to_all(pieces, axes, 0, 0)


def entering(state, steps, rates, backward):
    states = rates.shape[0]
    value = jnp.concatenate((state, steps), 0)
    count = lax.axis_size("x") * lax.axis_size("z")
    mine = lax.axis_index(("x", "z"))
    pieces = exchange(jnp.broadcast_to(value[None], (count,) + value.shape), ("x", "z"))
    before = jnp.zeros_like(state)
    for k in range(count - 1, 0, -1) if backward else range(count - 1):
        ahead = k > mine if backward else k < mine
        moved = jnp.exp(rates * pieces[k, states:]) * before + pieces[k, :states]
        before = jnp.where(ahead, moved, before)
    return before


def from_behind(block, axes, distance):
    count = 1
    for axis in axes:
        count *= lax.axis_size(axis)
    route = [(i - distance, i) for i in range(count) if 0 <= i - distance < count]
    return lax.ppermute(block, axes, route)


def from_earlier(block):
    groups = ("x", "z")
    mine = lax.axis_index("y")
    behind = from_behind(block, groups, 1)
    beyond = from_behind(block, groups, 2)
    near, far = [], []
    for k in range(1, 4):
        wraps = mine + k >= 4
        sent = jnp.concatenate(
            (jnp.where(wraps, beyond, behind), jnp.where(wraps, behind, block)), 0
        )
        got = lax.ppermute(sent, "y", [(i, (i + k) % 4) for i in range(4)])
        far.append(got[: block.shape[0]])
        near.append(got[block.shape[0] :])
    return jnp.concatenate([beyond] + far[::-1] + [behind] + near[::-1], 0)


def to_earlier(grads, rows):
    groups = ("x", "z")
    mine = lax.axis_index("y")
    block = [grads[k * rows : (k + 1) * rows] for k in range(9)]
    own, behind, beyond = block[8], block[4], block[0]
    for k in range(1, 4):
        sent = bf(jnp.concatenate((block[4 - k], block[8 - k]), 0))
        got = fl(lax.ppermute(sent, "y", [(i, (i - k) % 4) for i in range(4)]))
        far, near = got[:rows], got[rows:]
        wraps = mine + k >= 4
        own = own + jnp.where(wraps, 0.0, near)
        behind = behind + jnp.where(wraps, near, far)
        beyond = beyond + jnp.where(wraps, far, 0.0)
    return (
        own
        + fl(from_behind(bf(behind), groups, -1))
        + fl(from_behind(bf(beyond), groups, -2))
    )


def selector(width):
    place = jnp.arange(width, dtype=jnp.int32)
    block = width // BLOCK
    target = place + (PAD_ROWS - block) * (place // block)
    return bf(target[:, None] == jnp.arange(BLOCK * PAD_ROWS, dtype=jnp.int32)[None])


def pad_gain(gain):
    block = gain.shape[0] // BLOCK
    return jnp.pad(gain.reshape(BLOCK, block), ((0, 0), (0, PAD_ROWS - block))).reshape(-1)


def trim_gain(gain, width):
    return gain.reshape(BLOCK, PAD_ROWS)[:, : width // BLOCK].reshape(-1)


def trim_wide(value, chosen):
    top = lax.reduce_precision(value, 8, 7)
    return mm_t(bf(top), chosen) + mm_t(bf(value - top), chosen)


def norm_apply(values, gain):
    return values * lax.rsqrt(jnp.mean(values * values, -1, keepdims=True) + epsilon) * gain


def norm_scale(values, width):
    return lax.rsqrt(jnp.sum(values * values, -1, keepdims=True) / width + epsilon)


def norm_back(values, scale, gain, grad, width):
    pushed = grad * gain
    along = jnp.sum(pushed * values, -1, keepdims=True) / width
    return pushed * scale - values * (scale * scale * scale) * along, jnp.sum(
        grad * values * scale, 0
    )


def swiglu_gate(gate_part, up_part):
    return jax.nn.silu(gate_part) * up_part


def widen(value, dim, size):
    pads = [(0, 0)] * value.ndim
    pads[dim] = (0, size - value.shape[dim])
    return jnp.pad(value, pads)


def round_up(value, unit):
    return -(-value // unit) * unit


def chunked(weight):
    rows, parts, columns = weight.shape
    wide = round_up(columns // 4, 128)
    cut = widen(weight.reshape(rows, parts, 4, columns // 4), 3, wide)
    cut = jnp.transpose(cut, (2, 0, 1, 3)).reshape(4, rows, parts * wide)
    return widen(cut, 1, PAD_ROWS)


def unchunked(grad, rows, parts, columns):
    wide = grad.shape[2] // parts
    cut = grad[:, :rows].reshape(4, rows, parts, wide)[..., : columns // 4]
    return fl(jnp.transpose(cut, (1, 2, 0, 3)).reshape(rows, parts, columns))


def to_chunks(packed):
    moved = lax.all_to_all(packed, "y", 0, 0)
    return moved.reshape(-1, packed.shape[-1])


def gather_rows(rows):
    return lax.all_gather(rows, ("x", "z"), axis=0, tiled=True)


def settle(grad):
    rows = lax.psum_scatter(bf(grad), ("x", "z"), scatter_dimension=0, tiled=True)
    return rows.reshape(4, -1, rows.shape[-1])


def conv_apply(extended, conv_taps, conv_bias):
    tap_count = conv_taps.shape[0]
    out_rows = extended.shape[0] - tap_count + 1
    summed = conv_bias + conv_taps[0] * extended[0:out_rows]
    for offset in range(1, tap_count):
        summed = summed + conv_taps[offset] * extended[offset : offset + out_rows]
    return jax.nn.silu(summed)


def shards(
    tokens,
    norm_gain,
    qkv_weight,
    heads_gain,
    mamba_in,
    conv_weight,
    conv_bias,
    state_proj,
    step_proj,
    step_bias,
    decay_log,
    skip_gain,
    mamba_gain,
    heads_out,
    mamba_out,
    mlp_gain,
    gate_up,
    down_proj,
    cotangent,
):
    tok_rows, width = tokens.shape
    shard_rows = qkv_weight.shape[0]
    inner_half = conv_weight.shape[1]
    inner = inner_half // 4
    lanes = round_up(inner, 128)
    hidden_half = gate_up.shape[2]
    hidden = round_up(hidden_half // 4, 128)
    heads_width = KV_HEADS * GROUP * HEAD
    kv_width = KV_HEADS * HEAD
    half_width = heads_width // 2
    qkv_half = qkv_weight.shape[1] // 2
    halo_count = WINDOW // tok_rows
    score_scale = HEAD ** (-0.5)
    x_pos, z_pos = lax.axis_index("x"), lax.axis_index("z")
    y_pos, w_pos = lax.axis_index("y"), lax.axis_index("w")
    group_axes, all_axes = ("x", "z"), ("x", "z", "y")
    own_rows = tok_rows // 2
    rank = step_proj.shape[0]

    def own_half(value, dim=0):
        size = value.shape[dim] // 2
        return lax.dynamic_slice_in_dim(value, w_pos * size, size, dim)

    def other_half(value, dim=0):
        size = value.shape[dim] // 2
        return lax.dynamic_slice_in_dim(value, (1 - w_pos) * size, size, dim)

    def own_block(value):
        return lax.dynamic_slice_in_dim(value, y_pos * tok_rows, tok_rows, 0)

    def channels(value, dim):
        part = lax.dynamic_slice_in_dim(value, y_pos * inner, inner, dim)
        return widen(fl(part), dim, lanes)

    qkv_wide, hout_wide = round_up(qkv_half // 4, 128), round_up(half_width // 4, 128)
    in_wide = 2 * lanes + qkv_wide
    early_full = gather_rows(
        to_chunks(
            jnp.concatenate(
                (
                    chunked(mamba_in),
                    chunked(own_half(qkv_weight, 1)[:, None]),
                    chunked(mamba_out[:, None]),
                ),
                2,
            )
        )
    )
    hout_full = lax.all_gather(widen(heads_out, 0, PAD_ROWS), all_axes, axis=0, tiled=True)
    late_full = gather_rows(
        to_chunks(jnp.concatenate((chunked(gate_up), chunked(down_proj[:, None])), 2))
    )
    gu_full = late_full[:, : 2 * hidden]
    down_full = late_full[:, 2 * hidden :]

    def to_tokens(chunk, columns):
        moved = lax.all_to_all(chunk.reshape(4, tok_rows, -1), "y", 0, 0)
        return jnp.transpose(moved[:, :, : columns // 4], (1, 0, 2)).reshape(tok_rows, columns)

    def to_columns(parts):
        cuts = [widen(rows.reshape(tok_rows, 4, -1), 2, wide) for rows, wide in parts]
        return to_chunks(jnp.transpose(jnp.concatenate(cuts, 2), (1, 0, 2)))

    chosen = selector(width)
    gain_first = pad_gain(norm_gain)
    gain_mid = pad_gain(mlp_gain)
    tokens_group = ordered(around(tokens, "y"), "y").reshape(4 * tok_rows, width)
    residual = mm(tokens_group, chosen)
    scale_first = norm_scale(residual, width)
    normed = bf(residual * scale_first * gain_first)

    cot_own = bf(mm(own_half(cotangent), chosen))
    early_full, cot_all = lax.optimization_barrier((early_full, gather_true(cot_own)))
    in_full = early_full[:, :in_wide]
    mout_full = early_full[:, in_wide:]

    mixed_in = bf(mm(normed, in_full))
    conv_in = mixed_in[:, :lanes]
    gate_float = fl(mixed_in[:, lanes : 2 * lanes])
    tail = from_behind(conv_in[-(CONV - 1) :], group_axes, 1)
    extended = fl(jnp.concatenate((tail, conv_in), 0))
    conv_taps = channels(conv_weight, 1)
    conv_shift = channels(conv_bias, 0)
    acted_b = bf(conv_apply(extended, conv_taps, conv_shift))
    acted = fl(acted_b)
    state_weight = bf(channels(state_proj, 0))
    state_t = sum_group(dot(state_weight, acted_b, ((0,), (1,))))
    low_rank_t = bf(state_t[:rank])
    input_t = state_t[rank : rank + STATE]
    output_t = state_t[rank + STATE :]
    step_weight = bf(channels(step_proj, 1))
    step_pre = t_mm(low_rank_t, step_weight) + channels(step_bias, 0)
    steps = jax.nn.softplus(step_pre)
    rates = -jnp.exp(channels(decay_log, 0)).T
    fast_rates = rates * (1.0 / LOG2)
    drive = steps * acted
    step_total = jnp.sum(steps, 0, keepdims=True)
    local_state = local_scan(steps, drive, input_t, fast_rates)
    carry_in = entering(local_state, step_total, rates, False)

    first_pos = (lax.axis_index(all_axes)) * tok_rows
    projected_half = to_tokens(mixed_in[:, 2 * lanes :], qkv_half)
    projected = by_half(projected_half, swap(projected_half), 1)
    own_first = w_pos * own_rows
    queries = own_half(projected[:, :heads_width])
    own_pair = projected[:, heads_width:]
    sent = own_half(own_pair, 1)
    halo_half = from_earlier(sent)
    seen = WINDOW + own_rows
    key_place = jnp.arange(seen, dtype=jnp.int32)[None]
    query_place = jnp.arange(own_rows, dtype=jnp.int32)[:, None]
    visible = (
        (key_place > query_place)
        & (key_place <= query_place + WINDOW)
        & (key_place >= WINDOW - first_pos - own_first)
    )
    bias = jnp.where(visible, 0.0, -1e30).astype(jnp.float32)
    place = jnp.stack((own_first, w_pos))
    heads_value, log_total, pair_all = attend(
        place, queries, halo_half, swap(halo_half), own_pair, bias, score_scale
    )
    heads_normed = bf(norm_apply(heads_value, heads_gain))
    heads_half = by_half(own_half(heads_normed, 1), swap(other_half(heads_normed, 1)), 0)
    heads_part = mm_t(heads_half, hout_full)
    heads_mixed = own_half(heads_part) + fl(swap(bf(other_half(heads_part))))

    skip = channels(skip_gain, 0)
    scanned, kept = value_scan(steps, drive, input_t, output_t, fast_rates, carry_in)
    ssm_value = scanned + skip * acted
    gate_act = jax.nn.silu(gate_float)
    gated = ssm_value * gate_act
    gain_mamba = channels(mamba_gain, 0)
    lane = lax.broadcasted_iota(jnp.int32, (1, BLOCK * PAD_ROWS), 1)

    def tuck(value, extras):
        for k, extra in enumerate(extras):
            value = jnp.where(lane == shard_rows + k, extra, value)
        return value

    squares = jnp.sum(gated * gated, -1, keepdims=True)
    unscaled = scatter_true(tuck(mm_t(bf(gated * gain_mamba), mout_full), (squares,)))
    mamba_scale_own = lax.rsqrt(unscaled[:, shard_rows : shard_rows + 1] / INNER + epsilon)
    unscaled = jnp.where(lane == shard_rows, 0.0, unscaled)
    mixer = 0.5 * (unscaled * mamba_scale_own + heads_mixed)
    own_tokens = mm(own_half(tokens), chosen)
    middle = own_tokens + mixer
    scale_mid = norm_scale(middle, width)

    normed_mid = gather_true(bf(middle * scale_mid * gain_mid))
    gate_values = mm(normed_mid, gu_full)
    gate_part, up_part = gate_values[:, :hidden], gate_values[:, hidden:]
    hidden_b = bf(swiglu_gate(gate_part, up_part))
    mlp_part = mm_t(hidden_b, down_full)
    hidden_grad = mm(cot_all, down_full)
    gate_grad, up_grad = jax.vjp(swiglu_gate, gate_part, up_part)[1](hidden_grad)
    gate_values_grad = bf(jnp.concatenate((gate_grad, up_grad), 1))
    ffn_grad = weight_grads(normed_mid, gate_values_grad, cot_all, hidden_b)
    mid_grad = scatter_true(mm_t(gate_values_grad, gu_full))
    mid_grad, ffn_grad = lax.optimization_barrier((mid_grad, ffn_grad))
    ffn_rows = settle(ffn_grad)
    mid_back, mlp_gain_grad = norm_back(middle, scale_mid, gain_mid, mid_grad, width)
    middle_grad = fl(cot_own) + mid_back

    mixer_grad_own = bf(middle_grad)
    row_total_own = 0.5 * jnp.sum(fl(mixer_grad_own) * unscaled, -1, keepdims=True)
    extras = []
    for value in (mamba_scale_own, row_total_own):
        top = lax.reduce_precision(value, 8, 7)
        extras += [bf(top), bf(value - top)]
    mixer_grad = gather_true(tuck(mixer_grad_own, extras))
    tucked = fl(mixer_grad[:, shard_rows : shard_rows + 4])
    mamba_scale = tucked[:, 0:1] + tucked[:, 1:2]
    row_total = tucked[:, 2:3] + tucked[:, 3:4]
    mamba_normed = bf(gated * mamba_scale * gain_mamba)
    mamba_normed_grad = 0.5 * mm(mixer_grad, mout_full)
    half_grad = bf(0.5 * mm(own_block(mixer_grad), hout_full))
    gated_grad = (
        mamba_normed_grad * gain_mamba * mamba_scale
        - gated * mamba_scale**3 * row_total / INNER
    )
    mamba_gain_grad = jnp.sum(mamba_normed_grad * gated * mamba_scale, 0)
    ssm_grad = gated_grad * gate_act
    gate_in_grad = jax.vjp(jax.nn.silu, gate_float)[1](gated_grad * ssm_value)[0]
    gate_in_grad = bf(gate_in_grad)
    push = push_scan(steps, ssm_grad, output_t, fast_rates)
    future = entering(push, step_total, rates, True)

    heads_normed_grad = by_half(own_half(half_grad), swap(other_half(half_grad)), 1)
    heads_value_grad, heads_gain_grad = jax.vjp(norm_apply, heads_value, heads_gain)[1](
        fl(heads_normed_grad)
    )
    query_grad, pair_grad = attend_back(
        place, queries, pair_all, bias, log_total, bf(heads_value_grad), score_scale
    )
    pair_half = pick(pair_grad, w_pos, 0) + fl(swap(bf(pick(pair_grad, 1 - w_pos, 0))))
    own_pair_grad = to_earlier(pair_half, tok_rows)
    own_pair_grad = bf(own_pair_grad)
    projected_grad = jnp.concatenate(
        (
            by_half(query_grad, swap(query_grad), 0),
            by_half(own_pair_grad, swap(own_pair_grad), 1),
        ),
        1,
    )
    projected_grad_half = own_half(projected_grad, 1)
    both_chunks = to_columns(((heads_half, hout_wide), (projected_grad_half, qkv_wide)))
    heads_chunk, qkv_chunk = both_chunks[:, :hout_wide], both_chunks[:, hout_wide:]
    gate_qkv_grad = jnp.concatenate((gate_in_grad, qkv_chunk), 1)
    out_grad = weight_grads(
        mixer_grad,
        0.5 * jnp.concatenate((mamba_normed, heads_chunk), 1),
        normed,
        gate_qkv_grad,
    )
    mlp = lax.psum_scatter(bf(mlp_part), ("y", "w"), scatter_dimension=0, tiled=True)
    future, out_grad, ffn_rows, mlp = lax.optimization_barrier(
        (future, out_grad, ffn_rows, mlp)
    )
    out_rows = settle(out_grad)
    side_back = mm_t(gate_qkv_grad, in_full[:, lanes:])

    first_part, second_part, input_grad_t, output_grad_t, rate_grad = back_scan(
        steps, drive, ssm_grad, input_t, output_t, fast_rates, kept, future
    )
    step_grad = LOG2 * first_part + acted * second_part
    acted_core_grad = steps * second_part + skip * ssm_grad
    skip_grad = jnp.sum(ssm_grad * acted, 0)
    step_pre_grad = step_grad * jax.nn.sigmoid(step_pre)
    step_bias_grad = jnp.sum(step_pre_grad, 0)
    step_pre_b = bf(step_pre_grad)
    step_proj_grad = mm(low_rank_t, step_pre_b)
    low_rank_grad_t = mm_t(step_weight, step_pre_b)
    state_grad_t = bf(
        sum_group(jnp.concatenate((low_rank_grad_t, input_grad_t, output_grad_t), 0))
    )
    state_proj_grad_t = mm(state_grad_t, acted_b)
    acted_grad = acted_core_grad + dot(state_grad_t, state_weight, ((0,), (1,)))
    extended_grad, conv_weight_grad, conv_bias_grad = jax.vjp(
        conv_apply, extended, conv_taps, conv_shift
    )[1](acted_grad)
    returned = from_behind(extended_grad[: CONV - 1], group_axes, -1)
    group_rows = 4 * tok_rows
    conv_in_grad = jnp.concatenate(
        (extended_grad[CONV - 1 : group_rows], extended_grad[group_rows:] + returned), 0
    )
    conv_in_grad = bf(conv_in_grad)
    out_half = bf(mm_t(bf(middle + fl(mlp)), chosen))
    layer_out = by_half(out_half, swap(out_half), 0)
    inner_rows = jnp.concatenate(
        (
            state_proj_grad_t,
            step_proj_grad,
            rate_grad * rates,
            conv_weight_grad,
            conv_bias_grad[None],
            step_bias_grad[None],
            skip_grad[None],
            mamba_gain_grad[None],
        ),
        0,
    )
    wide_gain = BLOCK * PAD_ROWS
    early_gains = jnp.concatenate((mlp_gain_grad, widen(heads_gain_grad, 0, wide_gain)))
    early_gains = early_gains.reshape(-1, lanes)
    inner_end, gains_end = inner_rows.shape[0], inner_rows.shape[0] + early_gains.shape[0]
    small = jnp.concatenate((inner_rows, early_gains + swap(early_gains)), 0)
    groups = lax.axis_size("x") * lax.axis_size("z")
    share = -(-gains_end // groups)
    small = widen(bf(small), 0, share * groups).reshape(groups, share, lanes)
    conv_grad = bf(t_mm(normed, conv_in_grad)).reshape(groups, -1, lanes)
    both = exchange(jnp.concatenate((conv_grad, small), 1), group_axes)
    both = bf(jnp.sum(fl(both), 0))
    conv_rows = both[:-share]
    conv_moved = exchange(conv_rows.reshape(4, -1, lanes), "y")
    normed_grad = scatter_true(side_back + mm_t(conv_in_grad, in_full[:, :lanes]))
    normed_grad, out_rows = lax.optimization_barrier((normed_grad, out_rows))
    own_scale = own_half(own_block(scale_first))
    first_back, norm_gain_grad = norm_back(
        own_tokens, own_scale, gain_first, normed_grad, width
    )
    tokens_half = trim_wide(middle_grad + first_back, chosen)
    tokens_grad = by_half(tokens_half, swap(tokens_half), 0)

    late_gain = norm_gain_grad.reshape(-1, lanes)
    late_gain = bf(late_gain + swap(late_gain))
    shared = jnp.concatenate((both[-share:], late_gain), 0)
    shared = exchange(jnp.broadcast_to(shared[None], (groups * 4,) + shared.shape), all_axes)
    late_gain = jnp.sum(fl(shared[:, share:]), 0).reshape(-1)
    small = fl(shared[:, :share].reshape(groups, 4, share, lanes))
    small = jnp.transpose(small, (1, 0, 2, 3)).reshape(4, groups * share, lanes)
    gains = jnp.sum(small[:, inner_end:gains_end], 0).reshape(2, -1)

    out_moved = lax.all_to_all(jnp.concatenate((ffn_rows, out_rows), 2), "y", 0, 0)

    def taken(moved, first, wide, parts, columns):
        return unchunked(moved[:, :, first : first + wide], shard_rows, parts, columns)

    gu_settled = taken(out_moved, 0, 2 * hidden, 2, hidden_half)
    down_settled = taken(out_moved, 2 * hidden, hidden, 1, hidden_half)[:, 0]
    first = 3 * hidden
    mout_settled = taken(out_moved, first, lanes, 1, inner_half)[:, 0]
    hout_settled = taken(out_moved, first + lanes, hout_wide, 1, half_width)[:, 0]
    first = first + lanes + hout_wide
    gate_settled = taken(out_moved, first, lanes, 1, inner_half)
    conv_settled = taken(conv_moved, 0, lanes, 1, inner_half)
    in_settled = jnp.concatenate((conv_settled, gate_settled), 1)
    qkv_own = taken(out_moved, first + lanes, qkv_wide, 1, qkv_half)[:, 0]
    qkv_settled = by_half(qkv_own, swap(qkv_own), 1)

    by_channel = jnp.transpose(small[:, :inner_end, :inner], (1, 0, 2)).reshape(
        -1, inner_half
    )
    ends = state_proj.shape[1] + rank
    last = ends + STATE + CONV
    return (
        layer_out,
        tokens_grad,
        trim_gain(late_gain, width),
        qkv_settled,
        gains[1, :heads_width],
        in_settled,
        by_channel[ends + STATE : last],
        by_channel[last],
        by_channel[: state_proj.shape[1]].T,
        by_channel[state_proj.shape[1] : ends],
        by_channel[last + 1],
        by_channel[ends : ends + STATE].T,
        by_channel[last + 2],
        by_channel[last + 3],
        hout_settled,
        mout_settled,
        trim_gain(gains[0], width),
        gu_settled,
        down_settled,
    )


def solution(mesh):
    split = Mesh(mesh.devices.reshape(4, 4, 4, 2), ("x", "z", "y", "w"))
    ctx = ("x", "z", "y")
    placed = (
        P(ctx, None),
        P(),
        P(ctx, None),
        P(),
        P(ctx, None, "w"),
        P(None, "w"),
        P("w"),
        P("w", None),
        P(None, "w"),
        P("w"),
        P("w", None),
        P("w"),
        P("w"),
        P(ctx, "w"),
        P(ctx, "w"),
        P(),
        P(ctx, None, "w"),
        P(ctx, "w"),
        P(ctx, None),
    )
    return jax.shard_map(
        shards,
        mesh=split,
        in_specs=placed,
        out_specs=(
            P(ctx, None),
            P(ctx, None),
            P(),
            P(ctx, None),
            P(),
            P(ctx, None, "w"),
            P(None, "w"),
            P("w"),
            P("w", None),
            P(None, "w"),
            P("w"),
            P("w", None),
            P("w"),
            P("w"),
            P(ctx, "w"),
            P(ctx, "w"),
            P(),
            P(ctx, None, "w"),
            P(ctx, "w"),
        ),
        check_vma=False,
    )
```

time: 1070 us -> 663 us (0.62)
  waiting for transfers between devices: 505 us -> 139 us
  matrix products: 137 us -> 81.4 us
  local copies, waits for them, and re-layouts: 78.1 us -> 125 us
  starting transfers between devices: 157 us -> 135 us
  blocking collectives: 29.3 us -> 13.1 us
    reduce_scatter x4 -> x2, waiting for transfers between devices: 243 us -> 0.02 us  [settle(): lax.psum_scatter(bf(grad), ('x', 'z'), scatter_dimension=0, tiled=True)]
    psum x1 -> x0, waiting for transfers between devices: 68.9 us -> none  [shards(): small = lax.psum(jnp.concatenate((inner_rows, gains), 0), group_axes)]
    all_to_all x2 -> x7, waiting for transfers between devices: 0.01 us -> 40.2 us  [the longest x5 22.6 us: exchange(): return lax.all_to_all(pieces, axes, 0, 0)]
    dot_general x6 -> x0, matrix products: 39.9 us -> none  [the longest x1 13.1 us: attend_backward(): jnp.einsum('tkgd,skd->kgts', heads_grad, values_all, preferred_element_ty...]
    all_to_all x2 -> x7, starting transfers between devices: 8.39 us -> 42.3 us  [the longest x5 34.7 us: exchange(): return lax.all_to_all(pieces, axes, 0, 0)]
    all_gather x2 -> x1, waiting for transfers between devices: 31 us -> 0.01 us  [shards(): lax.all_gather(widen(heads_out, 0, PAD_ROWS), all_axes, axis=0, tiled=True)]
    ppermute x18 -> x6, starting transfers between devices: 45.2 us -> 14.5 us  [from_behind(): return lax.ppermute(block, axes, route)]
    ppermute x12 -> x9, waiting for transfers between devices: 41.7 us -> 15.9 us  [finish_scatter(): total = total + fl(lax.ppermute(bf(parts[k]), 'y', route))]
  transfers between devices with their start and end apart: 93 -> 75, of which waited for: 57 -> 32; matrix products, arithmetic and copies ran while one was open for 20% -> 32% of each run, Pallas kernels for 8% -> 12%
where the time goes in v2:
time: 663 us; the launch traced here: 650 us
  waiting for transfers between devices  139 us (21%)
  starting transfers between devices  135 us (20%)
  local copies, waits for them, and re-layouts  125 us (19%)
  matrix products  81.4 us (12%)
  Pallas kernels  76.1 us (11%)
  other arithmetic  63.7 us (10%)
  between operations  17.2 us (3%)
  blocking collectives  13.1 us (2%)
    dot_general x24, matrix products, dot(): lax.dot_general(left, right, (contract, ((), ())), preferred_element_type...  81.4 us
    unnamed x253, local copies, waits for them, and re-layouts  43.4 us
    ppermute x18, waiting for transfers between devices, pull(): lax.ppermute(value, axis, [((i + amount) % count, i) for i in range(count)])  40.8 us
    all_to_all x5, starting transfers between devices, exchange(): return lax.all_to_all(pieces, axes, 0, 0)  34.7 us
    ppermute x21, starting transfers between devices, swap(): return lax.ppermute(value, 'w', [(0, 1), (1, 0)])  30.9 us
    pallas_call x1, Pallas kernels, back_scan(): pl.pallas_call(back_kernel, grid=(rows // LANES,), in_specs=[by_row, by_r...  25.9 us
    all_to_all x5, waiting for transfers between devices, exchange(): return lax.all_to_all(pieces, axes, 0, 0)  22.6 us
    ppermute x18, starting transfers between devices, pull(): lax.ppermute(value, axis, [((i + amount) % count, i) for i in range(count)])  21.1 us
  transfers between devices with their start and end apart: 75, of which 32 were waited for; matrix products, arithmetic and copies ran while one was open for 32% of the time, Pallas kernels for 12%

profile of v2, /device:TPU:1, one launch (start us, length us, event | category | flops | bytes accessed | tf_op | source)
XLA Modules:
  0.0 650.3 jit_solution(13179975823116979417)
XLA Ops:
  11.8 13.1 %all_to_all.50 = bf16[4,32,1920]{2,1,0:T(8,128)(2,1)} all-to-all(bf16[4,32,1920]{2,1,0:T(8,128)(2,1)S(1)} %copy.169), channel_id=1, replica_groups=mesh['x'=4,'z'=4,'y'=4,'w'=2] {'y'}, dimensions={0} | all-to-all | bytes 983040 | tf_op jit(solution)/shard_map/all_to_all | solution.py:702
  54.9 9.9 %collective-permute-done.1 = bf16[128,1600]{0,1:T(8,128)(2,1)S(1)} collective-permute-done((bf16[128,1600]{0,1:T(8,128)(2,1)}, bf16[128,1600]{0,1:T(8,128)(2,1)S(1)}, u32[]{:S(2)}, u32[]{:S(2)}) %collective-permute-start.1) | collective-permute-done | bytes 409632 | tf_op jit(solution)/shard_map/ppermute | solution.py:491
  79.0 5.8 multiply_reduce_fusion
  88.7 6.5 %all-gather.4.cloned.1.call-done = bf16[2048,1920]{1,0:T(8,128)(2,1)} async-done(((bf16[128,1920]{1,0:T(8,128)(2,1)}), bf16[2048,1920]{1,0:T(8,128)(2,1)}) %all-gather.4.cloned.1.call-update) | async-done | bytes 7864336 | tf_op jit(solution)/shard_map/all_gather | solution.py:707
  95.3 6.7 %fusion.20 = bf16[512,1408]{1,0:T(8,128)(2,1)S(1)} fusion(bf16[512,2048]{1,0:T(8,128)(2,1)} %multiply_convert_fusion.second_ref, bf16[2048,1920]{1,0:T(8,128)(2,1)} %all-gather.4.cloned.1.call-done), kind=kOutput, calls=%fused_computation.26 | convolution fusion | flops 2953510912 | bytes 9306112 | tf_op jit(solution)/shard_map/dot_general | solution.py:468
  139.3 8.4 %all-to-all-start.1 = ((f32[16,17,512]{2,1,0:T(8,128)}), f32[16,17,512]{2,1,0:T(8,128)}, u32[]{:S(2)}, u32[]{:S(2)}) async-start(f32[16,17,512]{2,1,0:T(8,128)} %broadcast_in_dim.164), calls=%async_computation.1 | async-start | bytes 1572864 | tf_op jit(solution)/shard_map/all_to_all | solution.py:574
  160.6 6.0 collective-permute-done.17
  172.9 9.3 %scan_value.1 = (f32[512,512]{1,0:T(8,128)S(1)}, f32[512,16,512]{2,1,0:T(8,128)}) custom-call(f32[512,512]{1,0:T(8,128)S(1)} %get-tuple-element.236.dt_ref, f32[512,512]{1,0:T(8,128)S(1)} %get-tuple-element.235.u_ref, f32[16,512]{1,0:T(8,128)S(1)} %get-tuple-element.290.b_ref, f32[16,512]{1,0:T(8,128)S(1)} %get-tuple-element.289.c_ref, ...), custom_call_target="tpu_custom_call" | custom-call | flops 33554432 | bytes 4194304 | tf_op jit(solution)/shard_map/scan_value/pallas_call | solution.py:230
  204.7 5.5 attend.1
  233.3 6.5 %collective-permute-done.14 = bf16[64,2048]{1,0:T(8,128)(2,1)} collective-permute-done((bf16[64,2048]{1,0:T(8,128)(2,1)S(1)}, bf16[64,2048]{1,0:T(8,128)(2,1)}, u32[]{:S(2)}, u32[]{:S(2)}) %collective-permute-start.14) | collective-permute-done | bytes 262176 | tf_op jit(solution)/shard_map/ppermute | solution.py:522
  244.8 5.8 collective-permute-done.26
  250.5 4.8 collective-permute-done.25
  262.4 6.3 fusion.16
  276.1 6.0 fusion.14
  290.4 8.7 %weight_grads.2 = bf16[2048,2304]{1,0:T(8,128)(2,1)} custom-call(bf16[512,2048]{1,0:T(8,128)(2,1)S(1)} %bitcast.758, bf16[512,1536]{1,0:T(8,128)(2,1)S(1)} %pad_maximum_fusion.1.first_grad_ref, bf16[512,2048]{1,0:T(8,128)(2,1)S(1)} %bitcast.756, bf16[512,768]{1,0:T(8,128)(2,1)S(1)} %get-tuple-element.212.second_grad_ref), custom_call_target="tpu_custom_call" | custom-call | flops 4831838208 | bytes 15990784 | tf_op jit(solution)/shard_map/weight_grads/pallas_call | solution.py:439
  299.3 8.8 %collective-permute-done.31 = bf16[64,2048]{1,0:T(8,128)(2,1)} collective-permute-done((bf16[64,2048]{1,0:T(8,128)(2,1)}, bf16[64,2048]{1,0:T(8,128)(2,1)}, u32[]{:S(2)}, u32[]{:S(2)}) %collective-permute-start.31) | collective-permute-done | bytes 262176 | tf_op jit(solution)/shard_map/ppermute | solution.py:522
  322.6 5.2 collective-permute-done.33
  340.6 8.2 %attend_back.1 = (bf16[64,1600]{1,0:T(8,128)(2,1)S(1)}, f32[2,1152,320]{2,1,0:T(8,128)S(1)}) custom-call(s32[2]{0:T(128)S(1)} %pad_add_fusion.3.first_ref, bf16[64,1600]{1,0:T(8,128)(2,1)S(1)} %copy-done.25, bf16[2,1152,320]{2,1,0:T(8,128)(2,1)S(1)} %copy-done.31, f32[64,1088]{1,0:T(8,128)S(1)} %copy-done.23, f32[5,320,1]{2,1,0:T(8,128)S(1)} %copy-done.33, ...), custom_call_target="tpu_custom_call" | custom-call | flops 4718592000 | bytes 4423680 | tf_op jit(solution)/shard_map/attend_back/pallas_call | solution.py:415
  378.0 9.3 %all-to-all-start.4 = ((f32[16,17,512]{2,1,0:T(8,128)}), f32[16,17,512]{2,1,0:T(8,128)}, u32[]{:S(2)}, u32[]{:S(2)}) async-start(f32[16,17,512]{2,1,0:T(8,128)} %broadcast_in_dim.177), calls=%async_computation.4 | async-start | bytes 1572864 | tf_op jit(solution)/shard_map/all_to_all | solution.py:574
  395.4 6.6 %collective-permute-done.43 = bf16[128,320]{1,0:T(8,128)(2,1)S(1)} collective-permute-done((bf16[128,320]{1,0:T(8,128)(2,1)S(1)}, bf16[128,320]{1,0:T(8,128)(2,1)S(1)}, u32[]{:S(2)}, u32[]{:S(2)}) %collective-permute-start.43) | collective-permute-done | bytes 81952 | tf_op jit(solution)/shard_map/ppermute | solution.py:596
  418.9 8.5 %all-to-all-done.5 = bf16[4,128,640]{1,2,0:T(8,128)(2,1)} async-done(((bf16[4,128,640]{1,2,0:T(8,128)(2,1)}), bf16[4,128,640]{1,2,0:T(8,128)(2,1)}, u32[]{:S(2)}, u32[]{:S(2)}) %all-to-all-start.5) | async-done | bytes 655392 | tf_op jit(solution)/shard_map/all_to_all | solution.py:702
  434.4 6.1 weight_grads.3
  445.5 6.8 %fusion.18 = f32[512,2048]{1,0:T(8,128)} fusion(bf16[2048,1920]{1,0:T(8,128)(2,1)} %all-gather.4.cloned.1.call-done, bf16[512,384]{1,0:T(8,128)(2,1)} %copy-done.66, bf16[512,512]{1,0:T(8,128)(2,1)} %get-tuple-element.211), kind=kOutput, calls=%fused_computation.21 | convolution fusion | flops 1880883200 | bytes 8781824 | tf_op jit(solution)/shard_map/dot_general | solution.py:468
  452.3 25.9 %scan_back.1 = (f32[512,512]{1,0:T(8,128)S(1)}, f32[512,512]{1,0:T(8,128)S(1)}, f32[8,8192]{1,0:T(8,128)S(1)}, f32[8,8192]{1,0:T(8,128)S(1)}, f32[16,512]{1,0:T(8,128)S(1)}) custom-call(f32[512,512]{1,0:T(8,128)S(1)} %get-tuple-element.236.dt_ref, f32[512,512]{1,0:T(8,128)S(1)} %get-tuple-element.235.u_ref, f32[512,512]{1,0:T(8,128)S(1)} %copy-done.15, ...), custom_call_target="tpu_custom_call" | custom-call | flops 83886080 | bytes 4194304 | tf_op jit(solution)/shard_map/scan_back/pallas_call | solution.py:271
  486.9 6.7 %collective-permute-done.50 = bf16[132,512]{1,0:T(8,128)(2,1)S(1)} collective-permute-done((bf16[132,512]{1,0:T(8,128)(2,1)S(1)}, bf16[132,512]{1,0:T(8,128)(2,1)S(1)}, u32[]{:S(2)}, u32[]{:S(2)}) %collective-permute-start.50) | collective-permute-done | bytes 135200 | tf_op jit(solution)/shard_map/ppermute | solution.py:491
  515.4 6.8 %all-to-all-start.6 = ((bf16[16,145,512]{2,1,0:T(8,128)(2,1)}), bf16[16,145,512]{2,1,0:T(8,128)(2,1)S(1)}, u32[]{:S(2)}, u32[]{:S(2)}) async-start(bf16[16,145,512]{2,1,0:T(8,128)(2,1)} %pad_maximum_fusion), calls=%async_computation.9 | async-start | bytes 4980736 | tf_op jit(solution)/shard_map/all_to_all | solution.py:574
  537.5 14.1 %all-to-all-done.6 = bf16[16,145,512]{2,1,0:T(8,128)(2,1)S(1)} async-done(((bf16[16,145,512]{2,1,0:T(8,128)(2,1)}), bf16[16,145,512]{2,1,0:T(8,128)(2,1)S(1)}, u32[]{:S(2)}, u32[]{:S(2)}) %all-to-all-start.6) | async-done | bytes 2375712 | tf_op jit(solution)/shard_map/all_to_all | solution.py:574
  552.6 4.8 all-to-all-start.9
  562.8 7.3 %collective-permute-start.58 = (f32[4,512]{1,0:T(4,128)S(1)}, f32[4,512]{1,0:T(4,128)S(1)}, u32[]{:S(2)}, u32[]{:S(2)}) collective-permute-start(f32[4,512]{1,0:T(4,128)S(1)} %reshape.478), channel_id=1, source_target_pairs={{0,1},{1,0},{2,3},{3,2},{4,5},{5,4},{6,7},{7,6},{8,9},{9,8},{10,11... | collective-permute-start | bytes 24584 | tf_op jit(solution)/shard_map/ppermute | solution.py:486
  581.9 13.0 %all-to-all-done.8 = bf16[4,32,3968]{2,1,0:T(8,128)(2,1)S(1)} async-done(((bf16[4,32,3968]{2,1,0:T(8,128)(2,1)}), bf16[4,32,3968]{2,1,0:T(8,128)(2,1)S(1)}, u32[]{:S(2)}, u32[]{:S(2)}) %all-to-all-start.8) | async-done | bytes 1015840 | tf_op jit(solution)/shard_map/all_to_all | solution.py:1037
  596.1 5.3 all-to-all-start.7
  617.6 5.1 all-to-all-done.7
  (672 shorter events, 375.2 us)
Async XLA Ops:
  7.2 88.1 %all-gather.4.cloned.1.call-start = ((), (), s32[]{:S(2)}) async-start(), calls=%async_computation.13 | async-start | bytes 8355840 | tf_op jit(solution)/shard_map/all_gather | solution.py:707
  25.0 203.5 %all-gather.6.cloned.1.call-start = ((), (), s32[]{:S(2)}) async-start(), calls=%async_computation.14 | async-start | bytes 3727360 | tf_op jit(solution)/shard_map/all_gather | solution.py:793
  28.6 17.0 %collective-permute-start.5 = (bf16[64,2048]{1,0:T(8,128)(2,1)S(1)}, bf16[64,2048]{1,0:T(8,128)(2,1)S(1)}, u32[]{:S(2)}, u32[]{:S(2)}) collective-permute-start(bf16[64,2048]{1,0:T(8,128)(2,1)S(1)} %fusion.27), channel_id=1, source_target_pairs={{6,0},{0,2},{2,4},{4,6},{7,1},{1,3},{3,5},{5,7},{14,8},{8,10},{10,... | collective-permute-start | bytes 786440 | tf_op jit(solution)/shard_map/ppermute | solution.py:491
  29.0 19.6 %collective-permute-start.4 = (bf16[64,2048]{1,0:T(8,128)(2,1)S(1)}, bf16[64,2048]{1,0:T(8,128)(2,1)S(1)}, u32[]{:S(2)}, u32[]{:S(2)}) collective-permute-start(bf16[64,2048]{1,0:T(8,128)(2,1)S(1)} %fusion.27), channel_id=1, source_target_pairs={{4,0},{6,2},{0,4},{2,6},{5,1},{7,3},{1,5},{3,7},{12,8},{14,10},{8,... | collective-permute-start | bytes 786440 | tf_op jit(solution)/shard_map/ppermute | solution.py:491
  30.8 17.8 %collective-permute-start.3 = (bf16[64,2048]{1,0:T(8,128)(2,1)S(1)}, bf16[64,2048]{1,0:T(8,128)(2,1)S(1)}, u32[]{:S(2)}, u32[]{:S(2)}) collective-permute-start(bf16[64,2048]{1,0:T(8,128)(2,1)S(1)} %fusion.27), channel_id=1, source_target_pairs={{2,0},{4,2},{6,4},{0,6},{3,1},{5,3},{7,5},{1,7},{10,8},{12,10},{14... | collective-permute-start | bytes 786440 | tf_op jit(solution)/shard_map/ppermute | solution.py:491
  31.5 21.6 %collective-permute-start = (bf16[128,1600]{0,1:T(8,128)(2,1)}, bf16[128,1600]{0,1:T(8,128)(2,1)}, u32[]{:S(2)}, u32[]{:S(2)}) collective-permute-start(bf16[128,1600]{0,1:T(8,128)(2,1)} %param.19), channel_id=1, source_target_pairs={{2,0},{4,2},{6,4},{0,6},{3,1},{5,3},{7,5},{1,7},{10,8},{12,10},{14... | collective-permute-start | bytes 1228808 | tf_op jit(solution)/shard_map/ppermute | solution.py:491
  32.3 34.2 %collective-permute-start.2 = (bf16[128,1600]{0,1:T(8,128)(2,1)}, bf16[128,1600]{0,1:T(8,128)(2,1)}, u32[]{:S(2)}, u32[]{:S(2)}) collective-permute-start(bf16[128,1600]{0,1:T(8,128)(2,1)} %param.19), channel_id=1, source_target_pairs={{6,0},{0,2},{2,4},{4,6},{7,1},{1,3},{3,5},{5,7},{14,8},{8,10},{10,... | collective-permute-start | bytes 1228808 | tf_op jit(solution)/shard_map/ppermute | solution.py:491
  35.9 29.7 %all-to-all-start.3 = ((bf16[4,32,2304]{2,1,0:T(8,128)(2,1)}), bf16[4,32,2304]{2,1,0:T(8,128)(2,1)S(1)}, u32[]{:S(2)}, u32[]{:S(2)}) async-start(bf16[4,32,2304]{2,1,0:T(8,128)(2,1)} %copy.178), calls=%async_computation.3 | async-start | bytes 1179648 | tf_op jit(solution)/shard_map/all_to_all | solution.py:702
  39.4 223.0 %all-gather.8.cloned.1.call-start = ((), (), s32[]{:S(2)}) async-start(), calls=%async_computation.15 | async-start | bytes 10027008 | tf_op jit(solution)/shard_map/all_gather | solution.py:707
  45.6 19.1 %collective-permute-start.1 = (bf16[128,1600]{0,1:T(8,128)(2,1)}, bf16[128,1600]{0,1:T(8,128)(2,1)S(1)}, u32[]{:S(2)}, u32[]{:S(2)}) collective-permute-start(bf16[128,1600]{0,1:T(8,128)(2,1)} %param.19), channel_id=1, source_target_pairs={{4,0},{6,2},{0,4},{2,6},{5,1},{7,3},{1,5},{3,7},{12,8},{14,10},{8,... | collective-permute-start | bytes 1228808 | tf_op jit(solution)/shard_map/ppermute | solution.py:491
  48.7 37.9 %collective-permute-start.6 = (bf16[4,64,2048]{2,1,0:T(8,128)(2,1)S(1)}, bf16[4,64,2048]{2,1,0:T(8,128)(2,1)S(1)}, u32[]{:S(2)}, u32[]{:S(2)}) collective-permute-start(bf16[4,64,2048]{2,1,0:T(8,128)(2,1)S(1)} %pad_maximum_fusion.2.own_ref), channel_id=1, source_target_pairs={{0,1},{1,0},{2,3},{3,2},{4,5},{5,4},{6,7},{7,6},{8,9},{9,8},{10,11... | collective-permute-start | bytes 3145736 | tf_op jit(solution)/shard_map/ppermute | solution.py:486
  139.3 31.5 %all-to-all-start.1 = ((f32[16,17,512]{2,1,0:T(8,128)}), f32[16,17,512]{2,1,0:T(8,128)}, u32[]{:S(2)}, u32[]{:S(2)}) async-start(f32[16,17,512]{2,1,0:T(8,128)} %broadcast_in_dim.164), calls=%async_computation.1 | async-start | bytes 1572864 | tf_op jit(solution)/shard_map/all_to_all | solution.py:574
  147.7 295.7 %reduce-scatter.6.cloned.1.call-start = ((), (), s32[]{:S(2)}) async-start(), calls=%async_computation.17 | async-start | bytes 2359296 | tf_op jit(solution)/shard_map/reduce_scatter | solution.py:959
  167.5 17.5 %collective-permute-start.19 = (bf16[256,320]{1,0:T(8,128)(2,1)}, bf16[256,320]{1,0:T(8,128)(2,1)}, u32[]{:S(2)}, u32[]{:S(2)}) collective-permute-start(bf16[256,320]{1,0:T(8,128)(2,1)} %pad_maximum_fusion.17), channel_id=1, source_target_pairs={{0,6},{2,0},{4,2},{6,4},{1,7},{3,1},{5,3},{7,5},{8,14},{10,8},{12,... | collective-permute-start | bytes 491528 | tf_op jit(solution)/shard_map/ppermute | solution.py:610
  168.3 17.5 %collective-permute-start.20 = (bf16[256,320]{1,0:T(8,128)(2,1)}, bf16[256,320]{1,0:T(8,128)(2,1)}, u32[]{:S(2)}, u32[]{:S(2)}) collective-permute-start(bf16[256,320]{1,0:T(8,128)(2,1)} %pad_maximum_fusion.18), channel_id=1, source_target_pairs={{0,4},{2,6},{4,0},{6,2},{1,5},{3,7},{5,1},{7,3},{8,12},{10,14},{12... | collective-permute-start | bytes 491528 | tf_op jit(solution)/shard_map/ppermute | solution.py:610
  170.7 16.1 %collective-permute-start.21 = (bf16[256,320]{1,0:T(8,128)(2,1)}, bf16[256,320]{1,0:T(8,128)(2,1)}, u32[]{:S(2)}, u32[]{:S(2)}) collective-permute-start(bf16[256,320]{1,0:T(8,128)(2,1)} %pad_maximum_fusion.19), channel_id=1, source_target_pairs={{0,2},{2,4},{4,6},{6,0},{1,3},{3,5},{5,7},{7,1},{8,10},{10,12},{12... | collective-permute-start | bytes 491528 | tf_op jit(solution)/shard_map/ppermute | solution.py:610
  199.3 19.5 %collective-permute-start.12 = (bf16[4,64,2048]{2,1,0:T(8,128)(2,1)}, bf16[4,64,2048]{2,1,0:T(8,128)(2,1)}, u32[]{:S(2)}, u32[]{:S(2)}) collective-permute-start(bf16[4,64,2048]{2,1,0:T(8,128)(2,1)} %fusion.54), channel_id=1, source_target_pairs={{0,1},{1,0},{2,3},{3,2},{4,5},{5,4},{6,7},{7,6},{8,9},{9,8},{10,11... | collective-permute-start | bytes 3145736 | tf_op jit(solution)/shard_map/ppermute | solution.py:486
  275.9 167.4 %reduce-scatter.4.cloned.1.call-start = ((), (), s32[]{:S(2)}) async-start(), calls=%async_computation.16 | async-start | bytes 10027008 | tf_op jit(solution)/shard_map/reduce_scatter | solution.py:711
  290.3 17.8 %collective-permute-start.31 = (bf16[64,2048]{1,0:T(8,128)(2,1)}, bf16[64,2048]{1,0:T(8,128)(2,1)}, u32[]{:S(2)}, u32[]{:S(2)}) collective-permute-start(bf16[64,2048]{1,0:T(8,128)(2,1)} %get-tuple-element.225), channel_id=1, source_target_pairs={{0,4},{2,6},{4,0},{6,2},{1,5},{3,7},{5,1},{7,3},{8,12},{10,14},{12... | collective-permute-start | bytes 786440 | tf_op jit(solution)/shard_map/ppermute | solution.py:522
  362.9 25.7 %collective-permute-start.41 = (bf16[256,320]{1,0:T(8,128)(2,1)}, bf16[256,320]{1,0:T(8,128)(2,1)}, u32[]{:S(2)}, u32[]{:S(2)}) collective-permute-start(bf16[256,320]{1,0:T(8,128)(2,1)} %pad_maximum_fusion.21), channel_id=1, source_target_pairs={{0,4},{2,6},{4,0},{6,2},{1,5},{3,7},{5,1},{7,3},{8,12},{10,14},{12... | collective-permute-start | bytes 491528 | tf_op jit(solution)/shard_map/ppermute | solution.py:623
  364.9 24.7 %collective-permute-start.42 = (bf16[256,320]{1,0:T(8,128)(2,1)}, bf16[256,320]{1,0:T(8,128)(2,1)}, u32[]{:S(2)}, u32[]{:S(2)}) collective-permute-start(bf16[256,320]{1,0:T(8,128)(2,1)} %pad_maximum_fusion.22), channel_id=1, source_target_pairs={{0,2},{2,4},{4,6},{6,0},{1,3},{3,5},{5,7},{7,1},{8,10},{10,12},{12... | collective-permute-start | bytes 491528 | tf_op jit(solution)/shard_map/ppermute | solution.py:623
  365.6 25.1 %collective-permute-start.40 = (bf16[256,320]{1,0:T(8,128)(2,1)S(1)}, bf16[256,320]{1,0:T(8,128)(2,1)}, u32[]{:S(2)}, u32[]{:S(2)}) collective-permute-start(bf16[256,320]{1,0:T(8,128)(2,1)S(1)} %pad_maximum_fusion.20), channel_id=1, source_target_pairs={{0,6},{2,0},{4,2},{6,4},{1,7},{3,1},{5,3},{7,5},{8,14},{10,8},{12,... | collective-permute-start | bytes 491528 | tf_op jit(solution)/shard_map/ppermute | solution.py:623
  378.0 34.5 %all-to-all-start.4 = ((f32[16,17,512]{2,1,0:T(8,128)}), f32[16,17,512]{2,1,0:T(8,128)}, u32[]{:S(2)}, u32[]{:S(2)}) async-start(f32[16,17,512]{2,1,0:T(8,128)} %broadcast_in_dim.177), calls=%async_computation.4 | async-start | bytes 1572864 | tf_op jit(solution)/shard_map/all_to_all | solution.py:574
  416.7 145.9 %reduce-scatter.8.cloned.1.call-start = ((), (), s32[]{:S(2)}) async-start(), calls=%async_computation.18 | async-start | bytes 7241728 | tf_op jit(solution)/shard_map/reduce_scatter | solution.py:711
  510.3 18.8 %collective-permute-start.52 = (bf16[4,64,2048]{2,1,0:T(8,128)(2,1)}, bf16[4,64,2048]{2,1,0:T(8,128)(2,1)}, u32[]{:S(2)}, u32[]{:S(2)}) collective-permute-start(bf16[4,64,2048]{2,1,0:T(8,128)(2,1)} %fusion.56), channel_id=1, source_target_pairs={{0,1},{1,0},{2,3},{3,2},{4,5},{5,4},{6,7},{7,6},{8,9},{9,8},{10,11... | collective-permute-start | bytes 3145736 | tf_op jit(solution)/shard_map/ppermute | solution.py:486
  515.4 36.2 %all-to-all-start.6 = ((bf16[16,145,512]{2,1,0:T(8,128)(2,1)}), bf16[16,145,512]{2,1,0:T(8,128)(2,1)S(1)}, u32[]{:S(2)}, u32[]{:S(2)}) async-start(bf16[16,145,512]{2,1,0:T(8,128)(2,1)} %pad_maximum_fusion), calls=%async_computation.9 | async-start | bytes 4980736 | tf_op jit(solution)/shard_map/all_to_all | solution.py:574
  532.8 24.7 %collective-permute-start.53 = (bf16[64,2048]{1,0:T(8,128)(2,1)}, bf16[64,2048]{1,0:T(8,128)(2,1)}, u32[]{:S(2)}, u32[]{:S(2)}) collective-permute-start(bf16[64,2048]{1,0:T(8,128)(2,1)} %get-tuple-element.220), channel_id=1, source_target_pairs={{0,2},{2,4},{4,6},{6,0},{1,3},{3,5},{5,7},{7,1},{8,10},{10,12},{12... | collective-permute-start | bytes 786440 | tf_op jit(solution)/shard_map/ppermute | solution.py:522
  532.9 24.5 %collective-permute-start.55 = (bf16[64,2048]{1,0:T(8,128)(2,1)}, bf16[64,2048]{1,0:T(8,128)(2,1)}, u32[]{:S(2)}, u32[]{:S(2)}) collective-permute-start(bf16[64,2048]{1,0:T(8,128)(2,1)} %get-tuple-element.221), channel_id=1, source_target_pairs={{0,6},{2,0},{4,2},{6,4},{1,7},{3,1},{5,3},{7,5},{8,14},{10,8},{12,... | collective-permute-start | bytes 786440 | tf_op jit(solution)/shard_map/ppermute | solution.py:522
  535.5 22.0 %collective-permute-start.54 = (bf16[64,2048]{1,0:T(8,128)(2,1)}, bf16[64,2048]{1,0:T(8,128)(2,1)}, u32[]{:S(2)}, u32[]{:S(2)}) collective-permute-start(bf16[64,2048]{1,0:T(8,128)(2,1)} %get-tuple-element.222), channel_id=1, source_target_pairs={{0,4},{2,6},{4,0},{6,2},{1,5},{3,7},{5,1},{7,3},{8,12},{10,14},{12... | collective-permute-start | bytes 786440 | tf_op jit(solution)/shard_map/ppermute | solution.py:522
  562.8 17.7 %collective-permute-start.58 = (f32[4,512]{1,0:T(4,128)S(1)}, f32[4,512]{1,0:T(4,128)S(1)}, u32[]{:S(2)}, u32[]{:S(2)}) collective-permute-start(f32[4,512]{1,0:T(4,128)S(1)} %reshape.478), channel_id=1, source_target_pairs={{0,1},{1,0},{2,3},{3,2},{4,5},{5,4},{6,7},{7,6},{8,9},{9,8},{10,11... | collective-permute-start | bytes 24584 | tf_op jit(solution)/shard_map/ppermute | solution.py:486
  577.0 17.9 %all-to-all-start.8 = ((bf16[4,32,3968]{2,1,0:T(8,128)(2,1)}), bf16[4,32,3968]{2,1,0:T(8,128)(2,1)S(1)}, u32[]{:S(2)}, u32[]{:S(2)}) async-start(bf16[4,32,3968]{2,1,0:T(8,128)(2,1)} %pad_maximum_fusion.5), calls=%async_computation.11 | async-start | bytes 2031616 | tf_op jit(solution)/shard_map/all_to_all | solution.py:1037
  596.1 26.6 %all-to-all-start.7 = ((bf16[64,21,512]{2,1,0:T(8,128)(2,1)}), bf16[64,21,512]{2,1,0:T(8,128)(2,1)S(1)}, u32[]{:S(2)}, u32[]{:S(2)}) async-start(bf16[64,21,512]{2,1,0:T(8,128)(2,1)} %broadcast_in_dim.183), calls=%async_computation.10 | async-start | bytes 3145728 | tf_op jit(solution)/shard_map/all_to_all | solution.py:574
  (165 other events, 1720.2 us)
Sparse Core Ops, SparseCore 0:
  25.1 70.1 all-gather.3
  98.2 77.7 all-gather.5
  178.8 77.0 all-gather.7
  276.0 39.9 reduce-scatter.5
  319.3 100.4 reduce-scatter.3
  443.5 81.3 reduce-scatter.7

commit v3 on v2

--- a/solution.py
+++ b/solution.py
@@ -171,15 +171,18 @@
         return drate
 
     drate_ref[...] = lax.fori_loop(0, rows // SPREAD, spread, drate_ref[...])
-    ones = jnp.ones((8, LANES), jnp.float32)
+    ones = jnp.ones((LANES, LANES), jnp.bfloat16)
+    place = lax.broadcasted_iota(jnp.int32, (rows, states, LANES), 0)
+    lane = lax.broadcasted_iota(jnp.int32, (rows, states, LANES), 2)
     for wide_ref, out_ref in ((db_wide_ref, db_ref), (dc_wide_ref, dc_ref)):
-        out_ref[...] = lax.dot_general(
-            ones,
-            wide_ref[...].reshape(rows * states, LANES),
-            (((1,), (1,)), ((), ())),
-            precision=lax.Precision.HIGHEST,
-            preferred_element_type=jnp.float32,
+        wide = wide_ref[...].reshape(rows * states, LANES)
+        top = wide.astype(jnp.bfloat16)
+        rest = (wide - top.astype(jnp.float32)).astype(jnp.bfloat16)
+        total = jnp.dot(top, ones, preferred_element_type=jnp.float32) + jnp.dot(
+            rest, ones, preferred_element_type=jnp.float32
         )
+        held = jnp.where(place == lane, total.reshape(rows, states, LANES), 0.0)
+        out_ref[...] = jnp.sum(held, 0)
 
 
 def whole(shape):
@@ -265,19 +268,18 @@
     last = rows // LANES - 1
     by_row = pl.BlockSpec((LANES, width), lambda s: (last - s, 0))
     by_lane = pl.BlockSpec((states, LANES), lambda s: (0, last - s))
-    flat = pl.BlockSpec((8, LANES * states), lambda s: (0, last - s))
     held = pl.BlockSpec((LANES, states, width), lambda s: (last - s, 0, 0))
     wide = whole((states, width))
-    first, second, db, dc, drate = pl.pallas_call(
+    return pl.pallas_call(
         back_kernel,
         grid=(rows // LANES,),
         in_specs=[by_row, by_row, by_row, by_lane, by_lane, wide, held, wide],
-        out_specs=[by_row, by_row, flat, flat, wide],
+        out_specs=[by_row, by_row, by_lane, by_lane, wide],
         out_shape=[
             real(rows, width),
             real(rows, width),
-            real(8, rows * states),
-            real(8, rows * states),
+            real(states, rows),
+            real(states, rows),
             real(states, width),
         ],
         scratch_shapes=[
@@ -291,7 +293,6 @@
         cost_estimate=cost(rows, width, states, 20),
         name="scan_back",
     )(dt, u, dy, b_t, c_t, rates, kept, future)
-    return first, second, db[0].reshape(rows, states).T, dc[0].reshape(rows, states).T, drate
 
 def stacked_heads(ref, head, group):
     first = head * group * HEAD
@@ -352,7 +353,7 @@
 
 
 def attend_back_kernel(
-    scale, first_ref, q_ref, all_ref, bias_ref, log_ref, grad_ref, dq_ref, dpair_ref
+    scale, first_ref, q_ref, all_ref, bias_ref, log_ref, grad_ref, dq_ref, kept_ref, sent_ref
 ):
     bias = bias_ref[...]
     seen = pl.ds(pl.multiple_of(first_ref[0], HEAD), bias.shape[1])
@@ -372,9 +373,20 @@
         dks.append(down(score_grad, queries) * scale)
         dvs.append(down(probability.astype(jnp.bfloat16), grad))
     dq_ref[...] = jnp.concatenate(dqs, 1).astype(dq_ref.dtype)
-    dpair_ref[...] = jnp.zeros_like(dpair_ref)
-    dpair_ref[0, seen] = jnp.concatenate(dks, 1)
-    dpair_ref[1, seen] = jnp.concatenate(dvs, 1)
+    kept_ref[...] = jnp.zeros_like(kept_ref)
+    sent_ref[...] = jnp.zeros_like(sent_ref)
+    key_grad = jnp.concatenate(dks, 1).astype(kept_ref.dtype)
+    value_grad = jnp.concatenate(dvs, 1).astype(kept_ref.dtype)
+
+    @pl.when(first_ref[1] == 0)
+    def _():
+        kept_ref[seen] = key_grad
+        sent_ref[seen] = value_grad
+
+    @pl.when(first_ref[1] != 0)
+    def _():
+        kept_ref[seen] = value_grad
+        sent_ref[seen] = key_grad
 
 
 def attend_cost(rows, keys, products):
@@ -417,7 +429,8 @@
         in_specs=[in_smem()] + in_vmem(5),
         out_shape=[
             jax.ShapeDtypeStruct((rows, width), jnp.bfloat16),
-            real(*pair.shape),
+            jax.ShapeDtypeStruct(pair.shape[1:], jnp.bfloat16),
+            jax.ShapeDtypeStruct(pair.shape[1:], jnp.bfloat16),
         ],
         compiler_params=pltpu.CompilerParams(vmem_limit_bytes=40 * MIB),
         cost_estimate=attend_cost(rows, pair.shape[1], 20),
@@ -425,21 +438,30 @@
     )(first, queries, pair, bias, log_total, grad)
 
 
-def weights_kernel(first_ref, first_grad_ref, second_ref, second_grad_ref, out_ref):
-    split = first_grad_ref.shape[1]
-    out_ref[:, :split] = down(first_ref[...], first_grad_ref[...]).astype(out_ref.dtype)
-    out_ref[:, split:] = down(second_ref[...], second_grad_ref[...]).astype(out_ref.dtype)
-
-
-def weight_grads(first, first_grad, second, second_grad):
-    tokens, rows = first.shape
-    split, wide = first_grad.shape[1], first_grad.shape[1] + second_grad.shape[1]
+def weights_kernel(plan, *refs):
+    out_ref = refs[-1]
+    place = 0
+    for left, right, first, columns, scale in plan:
+        product = down(refs[left][...], refs[right][:, first : first + columns])
+        out_ref[:, place : place + columns] = (product * scale).astype(out_ref.dtype)
+        place += columns
+
+
+def weight_grads(groups):
+    lefts = [left for left, _, _ in groups]
+    rights, plan = [], []
+    for k, (_, scale, parts) in enumerate(groups):
+        for right, first, columns in parts:
+            plan.append((k, len(groups) + len(rights), first, columns, scale))
+            rights.append(right)
+    tokens, rows = lefts[0].shape
+    wide = sum(part[3] for part in plan)
     tile = 256
     by_column = pl.BlockSpec((tokens, tile), lambda s: (0, s))
     return pl.pallas_call(
-        weights_kernel,
+        functools.partial(weights_kernel, tuple(plan)),
         grid=(rows // tile,),
-        in_specs=[by_column, whole(first_grad.shape), by_column, whole(second_grad.shape)],
+        in_specs=[by_column] * len(lefts) + [whole(right.shape) for right in rights],
         out_specs=pl.BlockSpec((tile, wide), lambda s: (s, 0)),
         out_shape=jax.ShapeDtypeStruct((rows, wide), jnp.bfloat16),
         compiler_params=params(),
@@ -449,7 +471,7 @@
             transcendentals=0,
         ),
         name="weight_grads",
-    )(first, first_grad, second, second_grad)
+    )(*lefts, *rights)
 
 
 BLOCK = 64
@@ -572,6 +594,15 @@
 
 def exchange(pieces, axes):
     return lax.all_to_all(pieces, axes, 0, 0)
+
+
+def exchange_near(blocks):
+    mine = lax.axis_index("y")
+    pieces = [pick(blocks, mine, 0)]
+    for k in range(1, 4):
+        sent = pick(blocks, lax.rem(mine + 4 - k, 4), 0)
+        pieces.append(lax.ppermute(sent, "y", [(i, (i - k) % 4) for i in range(4)]))
+    return ordered(pieces, "y")
 
 
 def entering(state, steps, rates, backward):
@@ -898,7 +929,12 @@
     hidden_grad = mm(cot_all, down_full)
     gate_grad, up_grad = jax.vjp(swiglu_gate, gate_part, up_part)[1](hidden_grad)
     gate_values_grad = bf(jnp.concatenate((gate_grad, up_grad), 1))
-    ffn_grad = weight_grads(normed_mid, gate_values_grad, cot_all, hidden_b)
+    ffn_grad = weight_grads(
+        (
+            (normed_mid, 1.0, ((gate_values_grad, 0, 2 * hidden),)),
+            (cot_all, 1.0, ((hidden_b, 0, hidden),)),
+        )
+    )
     mid_grad = scatter_true(mm_t(gate_values_grad, gu_full))
     mid_grad, ffn_grad = lax.optimization_barrier((mid_grad, ffn_grad))
     ffn_rows = settle(ffn_grad)
@@ -927,16 +963,17 @@
     gate_in_grad = jax.vjp(jax.nn.silu, gate_float)[1](gated_grad * ssm_value)[0]
     gate_in_grad = bf(gate_in_grad)
     push = push_scan(steps, ssm_grad, output_t, fast_rates)
+    push, half_grad = lax.optimization_barrier((push, half_grad))
     future = entering(push, step_total, rates, True)
 
     heads_normed_grad = by_half(own_half(half_grad), swap(other_half(half_grad)), 1)
     heads_value_grad, heads_gain_grad = jax.vjp(norm_apply, heads_value, heads_gain)[1](
         fl(heads_normed_grad)
     )
-    query_grad, pair_grad = attend_back(
+    query_grad, kept_grad, sent_grad = attend_back(
         place, queries, pair_all, bias, log_total, bf(heads_value_grad), score_scale
     )
-    pair_half = pick(pair_grad, w_pos, 0) + fl(swap(bf(pick(pair_grad, 1 - w_pos, 0))))
+    pair_half = fl(kept_grad) + fl(swap(sent_grad))
     own_pair_grad = to_earlier(pair_half, tok_rows)
     own_pair_grad = bf(own_pair_grad)
     projected_grad = jnp.concatenate(
@@ -948,20 +985,17 @@
     )
     projected_grad_half = own_half(projected_grad, 1)
     both_chunks = to_columns(((heads_half, hout_wide), (projected_grad_half, qkv_wide)))
-    heads_chunk, qkv_chunk = both_chunks[:, :hout_wide], both_chunks[:, hout_wide:]
-    gate_qkv_grad = jnp.concatenate((gate_in_grad, qkv_chunk), 1)
     out_grad = weight_grads(
-        mixer_grad,
-        0.5 * jnp.concatenate((mamba_normed, heads_chunk), 1),
-        normed,
-        gate_qkv_grad,
+        (
+            (mixer_grad, 0.5, ((mamba_normed, 0, lanes), (both_chunks, 0, hout_wide))),
+            (normed, 1.0, ((gate_in_grad, 0, lanes), (both_chunks, hout_wide, qkv_wide))),
+        )
     )
     mlp = lax.psum_scatter(bf(mlp_part), ("y", "w"), scatter_dimension=0, tiled=True)
     future, out_grad, ffn_rows, mlp = lax.optimization_barrier(
         (future, out_grad, ffn_rows, mlp)
     )
     out_rows = settle(out_grad)
-    side_back = mm_t(gate_qkv_grad, in_full[:, lanes:])
 
     first_part, second_part, input_grad_t, output_grad_t, rate_grad = back_scan(
         steps, drive, ssm_grad, input_t, output_t, fast_rates, kept, future
@@ -990,12 +1024,17 @@
     conv_in_grad = bf(conv_in_grad)
     out_half = bf(mm_t(bf(middle + fl(mlp)), chosen))
     layer_out = by_half(out_half, swap(out_half), 0)
+    wide_gain = BLOCK * PAD_ROWS
+    early_gains = jnp.concatenate((mlp_gain_grad, widen(heads_gain_grad, 0, wide_gain)))
+    early_gains = early_gains.reshape(-1, lanes)
+    early_gains = early_gains + swap(early_gains)
+    groups = lax.axis_size("x") * lax.axis_size("z")
     inner_rows = jnp.concatenate(
         (
+            rate_grad * rates,
             state_proj_grad_t,
+            conv_weight_grad,
             step_proj_grad,
-            rate_grad * rates,
-            conv_weight_grad,
             conv_bias_grad[None],
             step_bias_grad[None],
             skip_grad[None],
@@ -1003,20 +1042,23 @@
         ),
         0,
     )
-    wide_gain = BLOCK * PAD_ROWS
-    early_gains = jnp.concatenate((mlp_gain_grad, widen(heads_gain_grad, 0, wide_gain)))
-    early_gains = early_gains.reshape(-1, lanes)
-    inner_end, gains_end = inner_rows.shape[0], inner_rows.shape[0] + early_gains.shape[0]
-    small = jnp.concatenate((inner_rows, early_gains + swap(early_gains)), 0)
-    groups = lax.axis_size("x") * lax.axis_size("z")
-    share = -(-gains_end // groups)
-    small = widen(bf(small), 0, share * groups).reshape(groups, share, lanes)
+    share = -(-inner_rows.shape[0] // groups)
+    small = jnp.concatenate(
+        (
+            bf(widen(inner_rows, 0, share * groups)).reshape(groups, share, lanes),
+            bf(widen(early_gains, 0, groups))[:, None],
+        ),
+        1,
+    )
     conv_grad = bf(t_mm(normed, conv_in_grad)).reshape(groups, -1, lanes)
-    both = exchange(jnp.concatenate((conv_grad, small), 1), group_axes)
-    both = bf(jnp.sum(fl(both), 0))
-    conv_rows = both[:-share]
-    conv_moved = exchange(conv_rows.reshape(4, -1, lanes), "y")
-    normed_grad = scatter_true(side_back + mm_t(conv_in_grad, in_full[:, :lanes]))
+    share = small.shape[1]
+    sent, conv_in_grad = lax.optimization_barrier(
+        (jnp.concatenate((conv_grad, small), 1), conv_in_grad)
+    )
+    both = bf(jnp.sum(fl(exchange(sent, group_axes)), 0))
+    conv_rows, small = both[:-share], both[-share:]
+    back_grad = jnp.concatenate((conv_in_grad, gate_in_grad, both_chunks[:, hout_wide:]), 1)
+    normed_grad = scatter_true(mm_t(back_grad, in_full))
     normed_grad, out_rows = lax.optimization_barrier((normed_grad, out_rows))
     own_scale = own_half(own_block(scale_first))
     first_back, norm_gain_grad = norm_back(
@@ -1025,16 +1067,19 @@
     tokens_half = trim_wide(middle_grad + first_back, chosen)
     tokens_grad = by_half(tokens_half, swap(tokens_half), 0)
 
+    def to_all(rows):
+        every = (groups * lax.axis_size("y"),)
+        return exchange(jnp.broadcast_to(rows[None], every + rows.shape), all_axes)
+
     late_gain = norm_gain_grad.reshape(-1, lanes)
     late_gain = bf(late_gain + swap(late_gain))
-    shared = jnp.concatenate((both[-share:], late_gain), 0)
-    shared = exchange(jnp.broadcast_to(shared[None], (groups * 4,) + shared.shape), all_axes)
+    shared = to_all(jnp.concatenate((small, late_gain), 0))
+    conv_moved = exchange_near(conv_rows.reshape(4, -1, lanes))
+    out_moved = exchange_near(jnp.concatenate((ffn_rows, out_rows), 2))
     late_gain = jnp.sum(fl(shared[:, share:]), 0).reshape(-1)
-    small = fl(shared[:, :share].reshape(groups, 4, share, lanes))
-    small = jnp.transpose(small, (1, 0, 2, 3)).reshape(4, groups * share, lanes)
-    gains = jnp.sum(small[:, inner_end:gains_end], 0).reshape(2, -1)
-
-    out_moved = lax.all_to_all(jnp.concatenate((ffn_rows, out_rows), 2), "y", 0, 0)
+    small = shared[:, :share].reshape(groups, -1, share, lanes)
+    gains = jnp.sum(fl(small[: early_gains.shape[0], :, -1]), 1).reshape(2, -1)
+
 
     def taken(moved, first, wide, parts, columns):
         return unchunked(moved[:, :, first : first + wide], shard_rows, parts, columns)
@@ -1051,11 +1096,11 @@
     qkv_own = taken(out_moved, first + lanes, qkv_wide, 1, qkv_half)[:, 0]
     qkv_settled = by_half(qkv_own, swap(qkv_own), 1)
 
-    by_channel = jnp.transpose(small[:, :inner_end, :inner], (1, 0, 2)).reshape(
-        -1, inner_half
-    )
-    ends = state_proj.shape[1] + rank
-    last = ends + STATE + CONV
+    by_channel = jnp.transpose(small[:, :, :-1, :inner], (0, 2, 1, 3)).reshape(-1, inner_half)
+    by_channel = fl(by_channel)
+    states_end = STATE + state_proj.shape[1]
+    taps_end = states_end + CONV
+    last = taps_end + rank
     return (
         layer_out,
         tokens_grad,
@@ -1063,12 +1108,12 @@
         qkv_settled,
         gains[1, :heads_width],
         in_settled,
-        by_channel[ends + STATE : last],
+        by_channel[states_end:taps_end],
         by_channel[last],
-        by_channel[: state_proj.shape[1]].T,
-        by_channel[state_proj.shape[1] : ends],
+        by_channel[STATE:states_end].T,
+        by_channel[taps_end:last],
         by_channel[last + 1],
-        by_channel[ends : ends + STATE].T,
+        by_channel[:STATE].T,
         by_channel[last + 2],
         by_channel[last + 3],
         hout_settled,

time: 663 us -> 626 us (0.944)
  other arithmetic: 63.7 us -> 46.9 us
  matrix products: 81.4 us -> 71 us
  local copies, waits for them, and re-layouts: 125 us -> 115 us
    all_to_all x1 -> x0, waiting for transfers between devices: 13 us -> none  [shards(): lax.all_to_all(jnp.concatenate((ffn_rows, out_rows), 2), 'y', 0, 0)]
    all_gather x2, waiting for transfers between devices: 6.54 us -> 17.6 us  [gather_rows(): return lax.all_gather(rows, ('x', 'z'), axis=0, tiled=True)]
    dot_general x24 -> x23, matrix products: 81.4 us -> 71 us  [dot(): lax.dot_general(left, right, (contract, ((), ())), preferred_element_type...]
    ppermute x21, starting transfers between devices: 30.9 us -> 40.8 us  [swap(): return lax.ppermute(value, 'w', [(0, 1), (1, 0)])]
    all_to_all x5 -> x4, starting transfers between devices: 34.7 us -> 24.9 us  [exchange(): return lax.all_to_all(pieces, axes, 0, 0)]
    all_to_all x5 -> x4, waiting for transfers between devices: 22.6 us -> 13.4 us  [exchange(): return lax.all_to_all(pieces, axes, 0, 0)]
    ppermute x0 -> x6, starting transfers between devices: none -> 8.4 us  [exchange_near(): pieces.append(lax.ppermute(sent, 'y', [(i, (i - k) % 4) for i in range(4)]))]
    ppermute x0 -> x6, waiting for transfers between devices: none -> 6.88 us  [exchange_near(): pieces.append(lax.ppermute(sent, 'y', [(i, (i - k) % 4) for i in range(4)]))]
  transfers between devices with their start and end apart: 75 -> 79, of which waited for: 32 -> 34; matrix products, arithmetic and copies ran while one was open for 32% -> 28% of each run, Pallas kernels for 12% -> 12%
where the time goes in v3:
time: 626 us; the launch traced here: 615 us
  starting transfers between devices  141 us (23%)
  waiting for transfers between devices  139 us (22%)
  local copies, waits for them, and re-layouts  115 us (18%)
  Pallas kernels  72.3 us (12%)
  matrix products  71 us (11%)
  other arithmetic  46.9 us (7%)
  between operations  17.3 us (3%)
  blocking collectives  13.1 us (2%)
    dot_general x23, matrix products, dot(): lax.dot_general(left, right, (contract, ((), ())), preferred_element_type...  71 us
    unnamed x285, local copies, waits for them, and re-layouts  46 us
    ppermute x21, starting transfers between devices, swap(): return lax.ppermute(value, 'w', [(0, 1), (1, 0)])  40.8 us
    ppermute x18, waiting for transfers between devices, pull(): lax.ppermute(value, axis, [((i + amount) % count, i) for i in range(count)])  39.7 us
    all_to_all x4, starting transfers between devices, exchange(): return lax.all_to_all(pieces, axes, 0, 0)  24.9 us
    ppermute x6, waiting for transfers between devices, from_behind(): return lax.ppermute(block, axes, route)  22.1 us
    pallas_call x1, Pallas kernels, back_scan(): pl.pallas_call(back_kernel, grid=(rows // LANES,), in_specs=[by_row, by_r...  21.8 us
    ppermute x18, starting transfers between devices, pull(): lax.ppermute(value, axis, [((i + amount) % count, i) for i in range(count)])  21 us
  transfers between devices with their start and end apart: 79, of which 34 were waited for; matrix products, arithmetic and copies ran while one was open for 28% of the time, Pallas kernels for 12%

profile of v3, /device:TPU:1, one launch (start us, length us, event | category | flops | bytes accessed | tf_op | source)
XLA Modules:
  0.0 615.2 jit_solution(4546067466350355632)
XLA Ops:
  11.8 13.1 %all_to_all.40 = bf16[4,32,1920]{2,1,0:T(8,128)(2,1)} all-to-all(bf16[4,32,1920]{2,1,0:T(8,128)(2,1)S(1)} %copy.129), channel_id=1, replica_groups=mesh['x'=4,'z'=4,'y'=4,'w'=2] {'y'}, dimensions={0} | all-to-all | bytes 983040 | tf_op jit(solution)/shard_map/all_to_all | solution.py:733
  54.8 10.0 %collective-permute-done.1 = bf16[128,1600]{0,1:T(8,128)(2,1)S(1)} collective-permute-done((bf16[128,1600]{0,1:T(8,128)(2,1)S(1)}, bf16[128,1600]{0,1:T(8,128)(2,1)S(1)}, u32[]{:S(2)}, u32[]{:S(2)}) %collective-permute-start.1) | collective-permute-done | bytes 409632 | tf_op jit(solution)/shard_map/ppermute | solution.py:513
  73.8 5.8 multiply_reduce_fusion
  84.8 10.5 %all-gather.4.cloned.1.call-done = bf16[2048,1920]{1,0:T(8,128)(2,1)} async-done(((bf16[128,1920]{1,0:T(8,128)(2,1)}), bf16[2048,1920]{1,0:T(8,128)(2,1)}) %all-gather.4.cloned.1.call-update) | async-done | bytes 7864336 | tf_op jit(solution)/shard_map/all_gather | solution.py:738
  95.3 6.1 fusion.20
  124.6 4.7 all-to-all-done.2
  138.4 7.9 %all-to-all-start.1 = ((f32[16,17,512]{2,1,0:T(8,128)}), f32[16,17,512]{2,1,0:T(8,128)}, u32[]{:S(2)}, u32[]{:S(2)}) async-start(f32[16,17,512]{2,1,0:T(8,128)} %broadcast_in_dim.167), calls=%async_computation.1 | async-start | bytes 1572864 | tf_op jit(solution)/shard_map/all_to_all | solution.py:596
  159.6 5.6 collective-permute-done.17
  171.2 9.3 %scan_value.1 = (f32[512,512]{1,0:T(8,128)S(1)}, f32[512,16,512]{2,1,0:T(8,128)}) custom-call(f32[512,512]{1,0:T(8,128)S(1)} %get-tuple-element.229.dt_ref, f32[512,512]{1,0:T(8,128)S(1)} %get-tuple-element.228.u_ref, f32[16,512]{1,0:T(8,128)S(1)} %get-tuple-element.285.b_ref, f32[16,512]{1,0:T(8,128)S(1)} %get-tuple-element.284.c_ref, ...), custom_call_target="tpu_custom_call" | custom-call | flops 33554432 | bytes 4194304 | tf_op jit(solution)/shard_map/scan_value/pallas_call | solution.py:233
  194.9 5.5 attend.1
  220.2 6.0 collective-permute-done.14
  231.2 5.1 collective-permute-done.26
  236.3 5.4 collective-permute-done.25
  248.8 7.1 %all-gather.8.cloned.1.call-done = bf16[2048,2304]{1,0:T(8,128)(2,1)} async-done(((bf16[128,2304]{1,0:T(8,128)(2,1)}), bf16[2048,2304]{1,0:T(8,128)(2,1)}) %all-gather.8.cloned.1.call-update) | async-done | bytes 9437200 | tf_op jit(solution)/shard_map/all_gather | solution.py:738
  255.9 6.3 %fusion.14 = f32[512,1536]{1,0:T(8,128)S(1)} fusion(bf16[512,2048]{1,0:T(8,128)(2,1)} %bitcast.786, bf16[2048,2304]{1,0:T(8,128)(2,1)} %all-gather.8.cloned.1.call-done), kind=kOutput, calls=%fused_computation.15 | convolution fusion | flops 3221225472 | bytes 11534336 | tf_op jit(solution)/shard_map/dot_general | solution.py:490
  269.7 6.0 fusion.12
  285.7 8.7 %weight_grads.2 = bf16[2048,2304]{1,0:T(8,128)(2,1)} custom-call(bf16[512,2048]{1,0:T(8,128)(2,1)S(1)} %bitcast.787, bf16[512,2048]{1,0:T(8,128)(2,1)S(1)} %bitcast.785, bf16[512,1536]{1,0:T(8,128)(2,1)S(1)} %pad_maximum_fusion.1.refs_2_, bf16[512,768]{1,0:T(8,128)(2,1)S(1)} %get-tuple-element.205.refs_3_), custom_call_target="tpu_custom_call" | custom-call | flops 4831838208 | bytes 15990784 | tf_op jit(solution)/shard_map/weight_grads/pallas_call | solution.py:461
  294.4 8.3 %collective-permute-done.31 = bf16[64,2048]{1,0:T(8,128)(2,1)} collective-permute-done((bf16[64,2048]{1,0:T(8,128)(2,1)}, bf16[64,2048]{1,0:T(8,128)(2,1)}, u32[]{:S(2)}, u32[]{:S(2)}) %collective-permute-start.31) | collective-permute-done | bytes 262176 | tf_op jit(solution)/shard_map/ppermute | solution.py:544
  309.6 4.6 collective-permute-done.34
  314.2 5.5 collective-permute-done.33
  330.3 5.4 fusion.57
  343.4 8.1 %attend_back.1 = (bf16[64,1600]{1,0:T(8,128)(2,1)S(1)}, bf16[1152,320]{1,0:T(8,128)(2,1)S(1)}, bf16[1152,320]{1,0:T(8,128)(2,1)S(1)}) custom-call(s32[2]{0:T(128)S(1)} %pad_add_fusion.3.first_ref, bf16[64,1600]{1,0:T(8,128)(2,1)S(1)} %copy-done.31, bf16[2,1152,320]{2,1,0:T(8,128)(2,1)S(1)} %copy-done.37, f32[64,1088]{1,0:T(8,128)S(1)} %copy-done.29, ...), custom_call_target="tpu_custom_call" | custom-call | flops 4718592000 | bytes 4423680 | tf_op jit(solution)/shard_map/attend_back/pallas_call | solution.py:427
  381.2 9.0 %collective-permute-done.43 = bf16[128,320]{1,0:T(8,128)(2,1)S(1)} collective-permute-done((bf16[128,320]{1,0:T(8,128)(2,1)S(1)}, bf16[128,320]{1,0:T(8,128)(2,1)S(1)}, u32[]{:S(2)}, u32[]{:S(2)}) %collective-permute-start.43) | collective-permute-done | bytes 81952 | tf_op jit(solution)/shard_map/ppermute | solution.py:627
  403.1 8.5 %all-to-all-done.5 = bf16[4,128,640]{1,2,0:T(8,128)(2,1)} async-done(((bf16[4,128,640]{1,2,0:T(8,128)(2,1)}), bf16[4,128,640]{1,2,0:T(8,128)(2,1)}, u32[]{:S(2)}, u32[]{:S(2)}) %all-to-all-start.5) | async-done | bytes 655392 | tf_op jit(solution)/shard_map/all_to_all | solution.py:733
  416.7 6.1 weight_grads.3
  430.5 21.8 %scan_back.1 = (f32[512,512]{1,0:T(8,128)S(1)}, f32[512,512]{1,0:T(8,128)S(1)}, f32[16,512]{1,0:T(8,128)S(1)}, f32[16,512]{1,0:T(8,128)S(1)}, f32[16,512]{1,0:T(8,128)S(1)}) custom-call(f32[512,512]{1,0:T(8,128)S(1)} %copy-done.10, f32[512,512]{1,0:T(8,128)S(1)} %copy-done.7, f32[512,512]{1,0:T(8,128)S(1)} %copy-done.18, f32[16,512]{1,0:T(8,128)S(1)} %copy-done.35, ...), custom_call_target="tpu_custom_call" | custom-call | flops 83886080 | bytes 4194304 | tf_op jit(solution)/shard_map/scan_back/pallas_call | solution.py:273
  476.1 6.8 %all-to-all-start.6 = ((bf16[16,145,512]{2,1,0:T(8,128)(2,1)}), bf16[16,145,512]{2,1,0:T(8,128)(2,1)S(1)}, u32[]{:S(2)}, u32[]{:S(2)}) async-start(bf16[16,145,512]{2,1,0:T(8,128)(2,1)} %pad_maximum_fusion), calls=%async_computation.9 | async-start | bytes 4980736 | tf_op jit(solution)/shard_map/all_to_all | solution.py:596
  482.9 5.6 fusion.16
  503.2 13.4 %all-to-all-done.6 = bf16[16,145,512]{2,1,0:T(8,128)(2,1)S(1)} async-done(((bf16[16,145,512]{2,1,0:T(8,128)(2,1)}), bf16[16,145,512]{2,1,0:T(8,128)(2,1)S(1)}, u32[]{:S(2)}, u32[]{:S(2)}) %all-to-all-start.6) | async-done | bytes 2375712 | tf_op jit(solution)/shard_map/all_to_all | solution.py:596
  527.1 8.6 %collective-permute-start.58 = (f32[4,512]{1,0:T(4,128)S(1)}, f32[4,512]{1,0:T(4,128)S(1)}, u32[]{:S(2)}, u32[]{:S(2)}) collective-permute-start(f32[4,512]{1,0:T(4,128)S(1)} %reshape.461), channel_id=1, source_target_pairs={{0,1},{1,0},{2,3},{3,2},{4,5},{5,4},{6,7},{7,6},{8,9},{9,8},{10,11... | collective-permute-start | bytes 24584 | tf_op jit(solution)/shard_map/ppermute | solution.py:508
  548.6 5.9 all-to-all-start.7
  566.7 8.6 %collective-permute-start.62 = (f32[25,1120]{1,0:T(8,128)S(1)}, f32[25,1120]{1,0:T(8,128)}, u32[]{:S(2)}, u32[]{:S(2)}) collective-permute-start(f32[25,1120]{1,0:T(8,128)S(1)} %reshape.474), channel_id=1, source_target_pairs={{0,1},{1,0},{2,3},{3,2},{4,5},{5,4},{6,7},{7,6},{8,9},{9,8},{10,11... | collective-permute-start | bytes 336008 | tf_op jit(solution)/shard_map/ppermute | solution.py:508
  (699 shorter events, 348.4 us)
Async XLA Ops:
  7.2 88.1 %all-gather.4.cloned.1.call-start = ((), (), s32[]{:S(2)}) async-start(), calls=%async_computation.11 | async-start | bytes 8355840 | tf_op jit(solution)/shard_map/all_gather | solution.py:738
  25.0 190.5 %all-gather.6.cloned.1.call-start = ((), (), s32[]{:S(2)}) async-start(), calls=%async_computation.12 | async-start | bytes 3727360 | tf_op jit(solution)/shard_map/all_gather | solution.py:824
  28.6 16.0 %collective-permute-start.5 = (bf16[64,2048]{1,0:T(8,128)(2,1)S(1)}, bf16[64,2048]{1,0:T(8,128)(2,1)S(1)}, u32[]{:S(2)}, u32[]{:S(2)}) collective-permute-start(bf16[64,2048]{1,0:T(8,128)(2,1)S(1)} %fusion.27), channel_id=1, source_target_pairs={{6,0},{0,2},{2,4},{4,6},{7,1},{1,3},{3,5},{5,7},{14,8},{8,10},{10,... | collective-permute-start | bytes 786440 | tf_op jit(solution)/shard_map/ppermute | solution.py:513
  29.0 18.6 %collective-permute-start.4 = (bf16[64,2048]{1,0:T(8,128)(2,1)S(1)}, bf16[64,2048]{1,0:T(8,128)(2,1)S(1)}, u32[]{:S(2)}, u32[]{:S(2)}) collective-permute-start(bf16[64,2048]{1,0:T(8,128)(2,1)S(1)} %fusion.27), channel_id=1, source_target_pairs={{4,0},{6,2},{0,4},{2,6},{5,1},{7,3},{1,5},{3,7},{12,8},{14,10},{8,... | collective-permute-start | bytes 786440 | tf_op jit(solution)/shard_map/ppermute | solution.py:513
  30.8 16.8 %collective-permute-start.3 = (bf16[64,2048]{1,0:T(8,128)(2,1)S(1)}, bf16[64,2048]{1,0:T(8,128)(2,1)}, u32[]{:S(2)}, u32[]{:S(2)}) collective-permute-start(bf16[64,2048]{1,0:T(8,128)(2,1)S(1)} %fusion.27), channel_id=1, source_target_pairs={{2,0},{4,2},{6,4},{0,6},{3,1},{5,3},{7,5},{1,7},{10,8},{12,10},{14... | collective-permute-start | bytes 786440 | tf_op jit(solution)/shard_map/ppermute | solution.py:513
  31.5 22.5 %collective-permute-start = (bf16[128,1600]{0,1:T(8,128)(2,1)S(1)}, bf16[128,1600]{0,1:T(8,128)(2,1)S(1)}, u32[]{:S(2)}, u32[]{:S(2)}) collective-permute-start(bf16[128,1600]{0,1:T(8,128)(2,1)S(1)} %copy-done.67), channel_id=1, source_target_pairs={{2,0},{4,2},{6,4},{0,6},{3,1},{5,3},{7,5},{1,7},{10,8},{12,10},{14... | collective-permute-start | bytes 1228808 | tf_op jit(solution)/shard_map/ppermute | solution.py:513
  32.3 34.2 %collective-permute-start.2 = (bf16[128,1600]{0,1:T(8,128)(2,1)S(1)}, bf16[128,1600]{0,1:T(8,128)(2,1)S(1)}, u32[]{:S(2)}, u32[]{:S(2)}) collective-permute-start(bf16[128,1600]{0,1:T(8,128)(2,1)S(1)} %copy-done.67), channel_id=1, source_target_pairs={{6,0},{0,2},{2,4},{4,6},{7,1},{1,3},{3,5},{5,7},{14,8},{8,10},{10,... | collective-permute-start | bytes 1228808 | tf_op jit(solution)/shard_map/ppermute | solution.py:513
  35.9 29.7 %all-to-all-start.3 = ((bf16[4,32,2304]{2,1,0:T(8,128)(2,1)}), bf16[4,32,2304]{2,1,0:T(8,128)(2,1)S(1)}, u32[]{:S(2)}, u32[]{:S(2)}) async-start(bf16[4,32,2304]{2,1,0:T(8,128)(2,1)} %copy.138), calls=%async_computation.3 | async-start | bytes 1179648 | tf_op jit(solution)/shard_map/all_to_all | solution.py:733
  39.4 216.5 %all-gather.8.cloned.1.call-start = ((), (), s32[]{:S(2)}) async-start(), calls=%async_computation.13 | async-start | bytes 10027008 | tf_op jit(solution)/shard_map/all_gather | solution.py:738
  44.6 20.1 %collective-permute-start.1 = (bf16[128,1600]{0,1:T(8,128)(2,1)S(1)}, bf16[128,1600]{0,1:T(8,128)(2,1)S(1)}, u32[]{:S(2)}, u32[]{:S(2)}) collective-permute-start(bf16[128,1600]{0,1:T(8,128)(2,1)S(1)} %copy-done.67), channel_id=1, source_target_pairs={{4,0},{6,2},{0,4},{2,6},{5,1},{7,3},{1,5},{3,7},{12,8},{14,10},{8,... | collective-permute-start | bytes 1228808 | tf_op jit(solution)/shard_map/ppermute | solution.py:513
  49.7 30.6 %collective-permute-start.6 = (bf16[4,64,2048]{2,1,0:T(8,128)(2,1)}, bf16[4,64,2048]{2,1,0:T(8,128)(2,1)}, u32[]{:S(2)}, u32[]{:S(2)}) collective-permute-start(bf16[4,64,2048]{2,1,0:T(8,128)(2,1)} %pad_maximum_fusion.2.own_ref), channel_id=1, source_target_pairs={{0,1},{1,0},{2,3},{3,2},{4,5},{5,4},{6,7},{7,6},{8,9},{9,8},{10,11... | collective-permute-start | bytes 3145736 | tf_op jit(solution)/shard_map/ppermute | solution.py:508
  130.4 16.0 %collective-permute-start.16 = (bf16[128,1120]{1,0:T(8,128)(2,1)S(1)}, bf16[128,1120]{1,0:T(8,128)(2,1)}, u32[]{:S(2)}, u32[]{:S(2)}) collective-permute-start(bf16[128,1120]{1,0:T(8,128)(2,1)S(1)} %copy.133), channel_id=1, source_target_pairs={{0,1},{1,0},{2,3},{3,2},{4,5},{5,4},{6,7},{7,6},{8,9},{9,8},{10,11... | collective-permute-start | bytes 860168 | tf_op jit(solution)/shard_map/ppermute | solution.py:508
  138.4 30.6 %all-to-all-start.1 = ((f32[16,17,512]{2,1,0:T(8,128)}), f32[16,17,512]{2,1,0:T(8,128)}, u32[]{:S(2)}, u32[]{:S(2)}) async-start(f32[16,17,512]{2,1,0:T(8,128)} %broadcast_in_dim.167), calls=%async_computation.1 | async-start | bytes 1572864 | tf_op jit(solution)/shard_map/all_to_all | solution.py:596
  146.4 279.2 %reduce-scatter.6.cloned.1.call-start = ((), (), s32[]{:S(2)}) async-start(), calls=%async_computation.15 | async-start | bytes 2359296 | tf_op jit(solution)/shard_map/reduce_scatter | solution.py:994
  151.0 14.2 %collective-permute-start.17 = (bf16[128,320]{1,0:T(8,128)(2,1)S(1)}, bf16[128,320]{1,0:T(8,128)(2,1)S(1)}, u32[]{:S(2)}, u32[]{:S(2)}) collective-permute-start(bf16[128,320]{1,0:T(8,128)(2,1)S(1)} %constant_dynamic-slice_fusion.4), channel_id=1, source_target_pairs={{0,16},{8,24},{16,32},{24,40},{32,48},{40,56},{48,64},{56,72},{64,... | collective-permute-start | bytes 245768 | tf_op jit(solution)/shard_map/ppermute | solution.py:627
  166.0 15.1 %collective-permute-start.19 = (bf16[256,320]{1,0:T(8,128)(2,1)}, bf16[256,320]{1,0:T(8,128)(2,1)}, u32[]{:S(2)}, u32[]{:S(2)}) collective-permute-start(bf16[256,320]{1,0:T(8,128)(2,1)} %pad_maximum_fusion.13), channel_id=1, source_target_pairs={{0,6},{2,0},{4,2},{6,4},{1,7},{3,1},{5,3},{7,5},{8,14},{10,8},{12,... | collective-permute-start | bytes 491528 | tf_op jit(solution)/shard_map/ppermute | solution.py:641
  167.2 14.8 %collective-permute-start.20 = (bf16[256,320]{1,0:T(8,128)(2,1)}, bf16[256,320]{1,0:T(8,128)(2,1)}, u32[]{:S(2)}, u32[]{:S(2)}) collective-permute-start(bf16[256,320]{1,0:T(8,128)(2,1)} %pad_maximum_fusion.14), channel_id=1, source_target_pairs={{0,4},{2,6},{4,0},{6,2},{1,5},{3,7},{5,1},{7,3},{8,12},{10,14},{12... | collective-permute-start | bytes 491528 | tf_op jit(solution)/shard_map/ppermute | solution.py:641
  269.4 156.2 %reduce-scatter.4.cloned.1.call-start = ((), (), s32[]{:S(2)}) async-start(), calls=%async_computation.14 | async-start | bytes 10027008 | tf_op jit(solution)/shard_map/reduce_scatter | solution.py:742
  284.1 18.6 %collective-permute-start.31 = (bf16[64,2048]{1,0:T(8,128)(2,1)}, bf16[64,2048]{1,0:T(8,128)(2,1)}, u32[]{:S(2)}, u32[]{:S(2)}) collective-permute-start(bf16[64,2048]{1,0:T(8,128)(2,1)} %get-tuple-element.214), channel_id=1, source_target_pairs={{0,4},{2,6},{4,0},{6,2},{1,5},{3,7},{5,1},{7,3},{8,12},{10,14},{12... | collective-permute-start | bytes 786440 | tf_op jit(solution)/shard_map/ppermute | solution.py:544
  368.6 28.1 %all-to-all-start.4 = ((f32[16,17,512]{2,1,0:T(8,128)}), f32[16,17,512]{2,1,0:T(8,128)}, u32[]{:S(2)}, u32[]{:S(2)}) async-start(f32[16,17,512]{2,1,0:T(8,128)} %broadcast_in_dim.180), calls=%async_computation.4 | async-start | bytes 1572864 | tf_op jit(solution)/shard_map/all_to_all | solution.py:596
  396.7 14.9 %all-to-all-start.5 = ((bf16[4,128,640]{1,2,0:T(8,128)(2,1)}), bf16[4,128,640]{1,2,0:T(8,128)(2,1)}, u32[]{:S(2)}, u32[]{:S(2)}) async-start(bf16[4,128,640]{1,2,0:T(8,128)(2,1)} %fusion.67), calls=%async_computation.5 | async-start | bytes 1310720 | tf_op jit(solution)/shard_map/all_to_all | solution.py:733
  401.0 126.0 %reduce-scatter.8.cloned.1.call-start = ((), (), s32[]{:S(2)}) async-start(), calls=%async_computation.16 | async-start | bytes 7241728 | tf_op jit(solution)/shard_map/reduce_scatter | solution.py:742
  476.1 40.6 %all-to-all-start.6 = ((bf16[16,145,512]{2,1,0:T(8,128)(2,1)}), bf16[16,145,512]{2,1,0:T(8,128)(2,1)S(1)}, u32[]{:S(2)}, u32[]{:S(2)}) async-start(bf16[16,145,512]{2,1,0:T(8,128)(2,1)} %pad_maximum_fusion), calls=%async_computation.9 | async-start | bytes 4980736 | tf_op jit(solution)/shard_map/all_to_all | solution.py:596
  499.0 21.1 %collective-permute-start.54 = (bf16[64,2048]{1,0:T(8,128)(2,1)}, bf16[64,2048]{1,0:T(8,128)(2,1)}, u32[]{:S(2)}, u32[]{:S(2)}) collective-permute-start(bf16[64,2048]{1,0:T(8,128)(2,1)} %get-tuple-element.209), channel_id=1, source_target_pairs={{0,2},{2,4},{4,6},{6,0},{1,3},{3,5},{5,7},{7,1},{8,10},{10,12},{12... | collective-permute-start | bytes 786440 | tf_op jit(solution)/shard_map/ppermute | solution.py:544
  499.0 21.1 %collective-permute-start.56 = (bf16[64,2048]{1,0:T(8,128)(2,1)}, bf16[64,2048]{1,0:T(8,128)(2,1)}, u32[]{:S(2)}, u32[]{:S(2)}) collective-permute-start(bf16[64,2048]{1,0:T(8,128)(2,1)} %get-tuple-element.210), channel_id=1, source_target_pairs={{0,6},{2,0},{4,2},{6,4},{1,7},{3,1},{5,3},{7,5},{8,14},{10,8},{12,... | collective-permute-start | bytes 786440 | tf_op jit(solution)/shard_map/ppermute | solution.py:544
  501.6 18.4 %collective-permute-start.55 = (bf16[64,2048]{1,0:T(8,128)(2,1)}, bf16[64,2048]{1,0:T(8,128)(2,1)}, u32[]{:S(2)}, u32[]{:S(2)}) collective-permute-start(bf16[64,2048]{1,0:T(8,128)(2,1)} %get-tuple-element.211), channel_id=1, source_target_pairs={{0,4},{2,6},{4,0},{6,2},{1,5},{3,7},{5,1},{7,3},{8,12},{10,14},{12... | collective-permute-start | bytes 786440 | tf_op jit(solution)/shard_map/ppermute | solution.py:544
  527.1 20.1 %collective-permute-start.58 = (f32[4,512]{1,0:T(4,128)S(1)}, f32[4,512]{1,0:T(4,128)S(1)}, u32[]{:S(2)}, u32[]{:S(2)}) collective-permute-start(f32[4,512]{1,0:T(4,128)S(1)} %reshape.461), channel_id=1, source_target_pairs={{0,1},{1,0},{2,3},{3,2},{4,5},{5,4},{6,7},{7,6},{8,9},{9,8},{10,11... | collective-permute-start | bytes 24584 | tf_op jit(solution)/shard_map/ppermute | solution.py:508
  542.2 46.5 %collective-permute-start.57 = (f32[64,1600]{1,0:T(8,128)}, f32[64,1600]{1,0:T(8,128)}, u32[]{:S(2)}, u32[]{:S(2)}) collective-permute-start(f32[64,1600]{1,0:T(8,128)} %fusion.26), channel_id=1, source_target_pairs={{0,1},{1,0},{2,3},{3,2},{4,5},{5,4},{6,7},{7,6},{8,9},{9,8},{10,11... | collective-permute-start | bytes 1228808 | tf_op jit(solution)/shard_map/ppermute | solution.py:508
  543.2 16.6 %collective-permute-start.61 = (bf16[32,3968]{1,0:T(8,128)(2,1)S(1)}, bf16[32,3968]{1,0:T(8,128)(2,1)}, u32[]{:S(2)}, u32[]{:S(2)}) collective-permute-start(bf16[32,3968]{1,0:T(8,128)(2,1)S(1)} %get-tuple-element.230), channel_id=1, source_target_pairs={{0,2},{2,4},{4,6},{6,0},{1,3},{3,5},{5,7},{7,1},{8,10},{10,12},{12... | collective-permute-start | bytes 761864 | tf_op jit(solution)/shard_map/ppermute | solution.py:604
  543.4 15.7 %collective-permute-start.60 = (bf16[32,3968]{1,0:T(8,128)(2,1)}, bf16[32,3968]{1,0:T(8,128)(2,1)S(1)}, u32[]{:S(2)}, u32[]{:S(2)}) collective-permute-start(bf16[32,3968]{1,0:T(8,128)(2,1)} %get-tuple-element.232), channel_id=1, source_target_pairs={{0,4},{2,6},{4,0},{6,2},{1,5},{3,7},{5,1},{7,3},{8,12},{10,14},{12... | collective-permute-start | bytes 761864 | tf_op jit(solution)/shard_map/ppermute | solution.py:604
  548.6 42.6 %all-to-all-start.7 = ((bf16[64,21,512]{2,1,0:T(8,128)(2,1)}), bf16[64,21,512]{2,1,0:T(8,128)(2,1)S(1)}, u32[]{:S(2)}, u32[]{:S(2)}) async-start(bf16[64,21,512]{2,1,0:T(8,128)(2,1)} %broadcast_in_dim.187), calls=%async_computation.10 | async-start | bytes 3145728 | tf_op jit(solution)/shard_map/all_to_all | solution.py:596
  566.7 20.3 %collective-permute-start.62 = (f32[25,1120]{1,0:T(8,128)S(1)}, f32[25,1120]{1,0:T(8,128)}, u32[]{:S(2)}, u32[]{:S(2)}) collective-permute-start(f32[25,1120]{1,0:T(8,128)S(1)} %reshape.474), channel_id=1, source_target_pairs={{0,1},{1,0},{2,3},{3,2},{4,5},{5,4},{6,7},{7,6},{8,9},{9,8},{10,11... | collective-permute-start | bytes 336008 | tf_op jit(solution)/shard_map/ppermute | solution.py:508
  (179 other events, 1967.8 us)
Sparse Core Ops, SparseCore 0:
  25.1 70.1 all-gather.3
  98.2 76.6 all-gather.5
  177.6 78.2 all-gather.7
  269.5 36.2 reduce-scatter.5
  309.2 103.7 reduce-scatter.3
  425.8 97.5 reduce-scatter.7

commit v4 on v3

--- a/solution.py
+++ b/solution.py
@@ -992,10 +992,6 @@
         )
     )
     mlp = lax.psum_scatter(bf(mlp_part), ("y", "w"), scatter_dimension=0, tiled=True)
-    future, out_grad, ffn_rows, mlp = lax.optimization_barrier(
-        (future, out_grad, ffn_rows, mlp)
-    )
-    out_rows = settle(out_grad)
 
     first_part, second_part, input_grad_t, output_grad_t, rate_grad = back_scan(
         steps, drive, ssm_grad, input_t, output_t, fast_rates, kept, future
@@ -1008,9 +1004,11 @@
     step_pre_b = bf(step_pre_grad)
     step_proj_grad = mm(low_rank_t, step_pre_b)
     low_rank_grad_t = mm_t(step_weight, step_pre_b)
-    state_grad_t = bf(
-        sum_group(jnp.concatenate((low_rank_grad_t, input_grad_t, output_grad_t), 0))
-    )
+    state_grad_t = sum_group(jnp.concatenate((low_rank_grad_t, input_grad_t, output_grad_t), 0))
+    state_grad_t, out_grad, ffn_rows, mlp = lax.optimization_barrier(
+        (bf(state_grad_t), out_grad, ffn_rows, mlp)
+    )
+    out_rows = settle(out_grad)
     state_proj_grad_t = mm(state_grad_t, acted_b)
     acted_grad = acted_core_grad + dot(state_grad_t, state_weight, ((0,), (1,)))
     extended_grad, conv_weight_grad, conv_bias_grad = jax.vjp(
@@ -1059,7 +1057,6 @@
     conv_rows, small = both[:-share], both[-share:]
     back_grad = jnp.concatenate((conv_in_grad, gate_in_grad, both_chunks[:, hout_wide:]), 1)
     normed_grad = scatter_true(mm_t(back_grad, in_full))
-    normed_grad, out_rows = lax.optimization_barrier((normed_grad, out_rows))
     own_scale = own_half(own_block(scale_first))
     first_back, norm_gain_grad = norm_back(
         own_tokens, own_scale, gain_first, normed_grad, width

time: 626 us -> 677 us (1.081)
  waiting for transfers between devices: 139 us -> 177 us
  local copies, waits for them, and re-layouts: 115 us -> 127 us
    all_to_all x4, waiting for transfers between devices: 13.4 us -> 45.9 us  [exchange(): return lax.all_to_all(pieces, axes, 0, 0)]
    ppermute x21, starting transfers between devices: 40.8 us -> 27.3 us  [swap(): return lax.ppermute(value, 'w', [(0, 1), (1, 0)])]
    all_to_all x4, starting transfers between devices: 24.9 us -> 34.3 us  [exchange(): return lax.all_to_all(pieces, axes, 0, 0)]
    unnamed x285 -> x311, local copies, waits for them, and re-layouts: 46 us -> 55 us
    all_to_all x2, waiting for transfers between devices: 8.52 us -> 0.01 us  [to_chunks(): moved = lax.all_to_all(packed, 'y', 0, 0)]
    ppermute x9, waiting for transfers between devices: 14.4 us -> 22.7 us  [finish_scatter(): total = total + fl(lax.ppermute(bf(parts[k]), 'y', route))]
  transfers between devices with their start and end apart: 79 -> 79, of which waited for: 34 -> 35; matrix products, arithmetic and copies ran while one was open for 28% -> 28% of each run, Pallas kernels for 12% -> 11%
where the time goes in v4:
time: 677 us; the launch traced here: 665 us
  waiting for transfers between devices  177 us (26%)
  starting transfers between devices  137 us (20%)
  local copies, waits for them, and re-layouts  127 us (19%)
  matrix products  73.4 us (11%)
  Pallas kernels  72.7 us (11%)
  other arithmetic  48.1 us (7%)
  between operations  17.2 us (3%)
  blocking collectives  13.1 us (2%)
    dot_general x23, matrix products, dot(): lax.dot_general(left, right, (contract, ((), ())), preferred_element_type...  73.4 us
    unnamed x311, local copies, waits for them, and re-layouts  55 us
    all_to_all x4, waiting for transfers between devices, exchange(): return lax.all_to_all(pieces, axes, 0, 0)  45.9 us
    ppermute x18, waiting for transfers between devices, pull(): lax.ppermute(value, axis, [((i + amount) % count, i) for i in range(count)])  44.6 us
    all_to_all x4, starting transfers between devices, exchange(): return lax.all_to_all(pieces, axes, 0, 0)  34.3 us
    ppermute x21, starting transfers between devices, swap(): return lax.ppermute(value, 'w', [(0, 1), (1, 0)])  27.3 us
    ppermute x18, starting transfers between devices, pull(): lax.ppermute(value, axis, [((i + amount) % count, i) for i in range(count)])  23.2 us
    ppermute x9, waiting for transfers between devices, finish_scatter(): total = total + fl(lax.ppermute(bf(parts[k]), 'y', route))  22.7 us
  transfers between devices with their start and end apart: 79, of which 35 were waited for; matrix products, arithmetic and copies ran while one was open for 28% of the time, Pallas kernels for 11%

profile of v4, /device:TPU:1, one launch (start us, length us, event | category | flops | bytes accessed | tf_op | source)
XLA Modules:
  0.0 665.4 jit_solution(12181093385978720693)
XLA Ops:
  11.8 13.1 %all_to_all.40 = bf16[4,32,1920]{2,1,0:T(8,128)(2,1)} all-to-all(bf16[4,32,1920]{2,1,0:T(8,128)(2,1)S(1)} %copy.129), channel_id=1, replica_groups=mesh['x'=4,'z'=4,'y'=4,'w'=2] {'y'}, dimensions={0} | all-to-all | bytes 983040 | tf_op jit(solution)/shard_map/all_to_all | solution.py:733
  54.7 10.1 %collective-permute-done.1 = bf16[128,1600]{0,1:T(8,128)(2,1)S(1)} collective-permute-done((bf16[128,1600]{0,1:T(8,128)(2,1)S(1)}, bf16[128,1600]{0,1:T(8,128)(2,1)S(1)}, u32[]{:S(2)}, u32[]{:S(2)}) %collective-permute-start.1) | collective-permute-done | bytes 409632 | tf_op jit(solution)/shard_map/ppermute | solution.py:513
  73.7 5.8 multiply_reduce_fusion
  84.7 10.6 %all-gather.4.cloned.1.call-done = bf16[2048,1920]{1,0:T(8,128)(2,1)} async-done(((bf16[128,1920]{1,0:T(8,128)(2,1)}), bf16[2048,1920]{1,0:T(8,128)(2,1)}) %all-gather.4.cloned.1.call-update) | async-done | bytes 7864336 | tf_op jit(solution)/shard_map/all_gather | solution.py:738
  95.3 6.1 fusion.20
  138.3 8.0 %all-to-all-start.1 = ((f32[16,17,512]{2,1,0:T(8,128)}), f32[16,17,512]{2,1,0:T(8,128)}, u32[]{:S(2)}, u32[]{:S(2)}) async-start(f32[16,17,512]{2,1,0:T(8,128)} %broadcast_in_dim.167), calls=%async_computation.1 | async-start | bytes 1572864 | tf_op jit(solution)/shard_map/all_to_all | solution.py:596
  158.7 6.3 collective-permute-done.17
  170.9 9.3 %scan_value.1 = (f32[512,512]{1,0:T(8,128)S(1)}, f32[512,16,512]{2,1,0:T(8,128)}) custom-call(f32[512,512]{1,0:T(8,128)S(1)} %get-tuple-element.226.dt_ref, f32[512,512]{1,0:T(8,128)S(1)} %get-tuple-element.225.u_ref, f32[16,512]{1,0:T(8,128)S(1)} %get-tuple-element.282.b_ref, f32[16,512]{1,0:T(8,128)S(1)} %get-tuple-element.281.c_ref, ...), custom_call_target="tpu_custom_call" | custom-call | flops 33554432 | bytes 4194304 | tf_op jit(solution)/shard_map/scan_value/pallas_call | solution.py:233
  194.7 5.5 attend.1
  220.2 6.1 collective-permute-done.14
  231.2 5.1 collective-permute-done.26
  236.3 5.2 collective-permute-done.25
  248.8 6.8 %all-gather.8.cloned.1.call-done = bf16[2048,2304]{1,0:T(8,128)(2,1)} async-done(((bf16[128,2304]{1,0:T(8,128)(2,1)}), bf16[2048,2304]{1,0:T(8,128)(2,1)}) %all-gather.8.cloned.1.call-update) | async-done | bytes 9437200 | tf_op jit(solution)/shard_map/all_gather | solution.py:738
  255.5 6.3 fusion.14
  269.2 6.0 fusion.12
  285.2 8.7 %weight_grads.2 = bf16[2048,2304]{1,0:T(8,128)(2,1)} custom-call(bf16[512,2048]{1,0:T(8,128)(2,1)S(1)} %bitcast.788, bf16[512,2048]{1,0:T(8,128)(2,1)S(1)} %bitcast.786, bf16[512,1536]{1,0:T(8,128)(2,1)S(1)} %pad_maximum_fusion.1.refs_2_, bf16[512,768]{1,0:T(8,128)(2,1)S(1)} %get-tuple-element.202.refs_3_), custom_call_target="tpu_custom_call" | custom-call | flops 4831838208 | bytes 15990784 | tf_op jit(solution)/shard_map/weight_grads/pallas_call | solution.py:461
  294.0 8.3 %collective-permute-done.31 = bf16[64,2048]{1,0:T(8,128)(2,1)} collective-permute-done((bf16[64,2048]{1,0:T(8,128)(2,1)}, bf16[64,2048]{1,0:T(8,128)(2,1)}, u32[]{:S(2)}, u32[]{:S(2)}) %collective-permute-start.31) | collective-permute-done | bytes 262176 | tf_op jit(solution)/shard_map/ppermute | solution.py:544
  313.7 5.5 collective-permute-done.33
  329.8 5.4 fusion.57
  346.8 8.7 %attend_back.1 = (bf16[64,1600]{1,0:T(8,128)(2,1)}, bf16[1152,320]{1,0:T(8,128)(2,1)S(1)}, bf16[1152,320]{1,0:T(8,128)(2,1)S(1)}) custom-call(s32[2]{0:T(128)S(1)} %pad_add_fusion.3.first_ref, bf16[64,1600]{1,0:T(8,128)(2,1)S(1)} %copy-done.37, bf16[2,1152,320]{2,1,0:T(8,128)(2,1)S(1)} %copy-done.43, f32[64,1088]{1,0:T(8,128)S(1)} %copy-done.35, ...), custom_call_target="tpu_custom_call" | custom-call | flops 4718592000 | bytes 4423680 | tf_op jit(solution)/shard_map/attend_back/pallas_call | solution.py:427
  358.6 5.7 all-to-all-start.4
  368.4 13.5 %all-to-all-done.4 = f32[16,17,512]{2,1,0:T(8,128)} async-done(((f32[16,17,512]{2,1,0:T(8,128)}), f32[16,17,512]{2,1,0:T(8,128)}, u32[]{:S(2)}, u32[]{:S(2)}) %all-to-all-start.4) | async-done | bytes 557088 | tf_op jit(solution)/shard_map/all_to_all | solution.py:596
  387.7 21.7 %scan_back.1 = (f32[512,512]{1,0:T(8,128)S(1)}, f32[512,512]{1,0:T(8,128)S(1)}, f32[16,512]{1,0:T(8,128)S(1)}, f32[16,512]{1,0:T(8,128)S(1)}, f32[16,512]{1,0:T(8,128)S(1)}) custom-call(f32[512,512]{1,0:T(8,128)S(1)} %copy-done.10, f32[512,512]{1,0:T(8,128)S(1)} %copy-done.7, f32[512,512]{1,0:T(8,128)S(1)} %copy-done.18, f32[16,512]{1,0:T(8,128)S(1)} %copy-done.41, ...), custom_call_target="tpu_custom_call" | custom-call | flops 83886080 | bytes 4194304 | tf_op jit(solution)/shard_map/scan_back/pallas_call | solution.py:273
  421.6 5.4 collective-permute-done.46
  453.2 8.2 %collective-permute-done.40 = bf16[132,512]{1,0:T(8,128)(2,1)S(1)} collective-permute-done((bf16[132,512]{1,0:T(8,128)(2,1)S(1)}, bf16[132,512]{1,0:T(8,128)(2,1)S(1)}, u32[]{:S(2)}, u32[]{:S(2)}) %collective-permute-start.40) | collective-permute-done | bytes 135200 | tf_op jit(solution)/shard_map/ppermute | solution.py:513
  469.8 6.1 weight_grads.3
  484.0 5.2 multiply_reduce_fusion.5
  510.9 9.6 %all-to-all-start.6 = ((bf16[16,145,512]{2,1,0:T(8,128)(2,1)}), bf16[16,145,512]{2,1,0:T(8,128)(2,1)S(1)}, u32[]{:S(2)}, u32[]{:S(2)}) async-start(bf16[16,145,512]{2,1,0:T(8,128)(2,1)} %pad_maximum_fusion), calls=%async_computation.8 | async-start | bytes 4980736 | tf_op jit(solution)/shard_map/all_to_all | solution.py:596
  553.2 7.3 %all-to-all-done.6 = bf16[16,145,512]{2,1,0:T(8,128)(2,1)S(1)} async-done(((bf16[16,145,512]{2,1,0:T(8,128)(2,1)}), bf16[16,145,512]{2,1,0:T(8,128)(2,1)S(1)}, u32[]{:S(2)}, u32[]{:S(2)}) %all-to-all-start.6) | async-done | bytes 2375712 | tf_op jit(solution)/shard_map/all_to_all | solution.py:596
  564.9 11.1 %all-to-all-start.7 = ((bf16[64,21,512]{2,1,0:T(8,128)(2,1)}), bf16[64,21,512]{2,1,0:T(8,128)(2,1)S(1)}, u32[]{:S(2)}, u32[]{:S(2)}) async-start(bf16[64,21,512]{2,1,0:T(8,128)(2,1)} %broadcast_in_dim.187), calls=%async_computation.9 | async-start | bytes 3145728 | tf_op jit(solution)/shard_map/all_to_all | solution.py:596
  577.0 25.1 %all-to-all-done.7 = bf16[64,21,512]{2,1,0:T(8,128)(2,1)S(1)} async-done(((bf16[64,21,512]{2,1,0:T(8,128)(2,1)}), bf16[64,21,512]{2,1,0:T(8,128)(2,1)S(1)}, u32[]{:S(2)}, u32[]{:S(2)}) %all-to-all-start.7) | async-done | bytes 1376288 | tf_op jit(solution)/shard_map/all_to_all | solution.py:596
  630.0 8.2 %collective-permute-done.60 = bf16[32,3968]{1,0:T(8,128)(2,1)S(1)} collective-permute-done((bf16[32,3968]{1,0:T(8,128)(2,1)}, bf16[32,3968]{1,0:T(8,128)(2,1)S(1)}, u32[]{:S(2)}, u32[]{:S(2)}) %collective-permute-start.60) | collective-permute-done | bytes 253984 | tf_op jit(solution)/shard_map/ppermute | solution.py:604
  (723 shorter events, 374.3 us)
Async XLA Ops:
  7.2 88.1 %all-gather.4.cloned.1.call-start = ((), (), s32[]{:S(2)}) async-start(), calls=%async_computation.11 | async-start | bytes 8355840 | tf_op jit(solution)/shard_map/all_gather | solution.py:738
  25.0 190.5 %all-gather.6.cloned.1.call-start = ((), (), s32[]{:S(2)}) async-start(), calls=%async_computation.12 | async-start | bytes 3727360 | tf_op jit(solution)/shard_map/all_gather | solution.py:824
  28.6 16.0 %collective-permute-start.5 = (bf16[64,2048]{1,0:T(8,128)(2,1)S(1)}, bf16[64,2048]{1,0:T(8,128)(2,1)S(1)}, u32[]{:S(2)}, u32[]{:S(2)}) collective-permute-start(bf16[64,2048]{1,0:T(8,128)(2,1)S(1)} %fusion.27), channel_id=1, source_target_pairs={{6,0},{0,2},{2,4},{4,6},{7,1},{1,3},{3,5},{5,7},{14,8},{8,10},{10,... | collective-permute-start | bytes 786440 | tf_op jit(solution)/shard_map/ppermute | solution.py:513
  29.0 18.6 %collective-permute-start.4 = (bf16[64,2048]{1,0:T(8,128)(2,1)S(1)}, bf16[64,2048]{1,0:T(8,128)(2,1)S(1)}, u32[]{:S(2)}, u32[]{:S(2)}) collective-permute-start(bf16[64,2048]{1,0:T(8,128)(2,1)S(1)} %fusion.27), channel_id=1, source_target_pairs={{4,0},{6,2},{0,4},{2,6},{5,1},{7,3},{1,5},{3,7},{12,8},{14,10},{8,... | collective-permute-start | bytes 786440 | tf_op jit(solution)/shard_map/ppermute | solution.py:513
  30.8 16.8 %collective-permute-start.3 = (bf16[64,2048]{1,0:T(8,128)(2,1)S(1)}, bf16[64,2048]{1,0:T(8,128)(2,1)}, u32[]{:S(2)}, u32[]{:S(2)}) collective-permute-start(bf16[64,2048]{1,0:T(8,128)(2,1)S(1)} %fusion.27), channel_id=1, source_target_pairs={{2,0},{4,2},{6,4},{0,6},{3,1},{5,3},{7,5},{1,7},{10,8},{12,10},{14... | collective-permute-start | bytes 786440 | tf_op jit(solution)/shard_map/ppermute | solution.py:513
  31.5 22.4 %collective-permute-start = (bf16[128,1600]{0,1:T(8,128)(2,1)S(1)}, bf16[128,1600]{0,1:T(8,128)(2,1)S(1)}, u32[]{:S(2)}, u32[]{:S(2)}) collective-permute-start(bf16[128,1600]{0,1:T(8,128)(2,1)S(1)} %copy-done.80), channel_id=1, source_target_pairs={{2,0},{4,2},{6,4},{0,6},{3,1},{5,3},{7,5},{1,7},{10,8},{12,10},{14... | collective-permute-start | bytes 1228808 | tf_op jit(solution)/shard_map/ppermute | solution.py:513
  32.3 34.2 %collective-permute-start.2 = (bf16[128,1600]{0,1:T(8,128)(2,1)S(1)}, bf16[128,1600]{0,1:T(8,128)(2,1)S(1)}, u32[]{:S(2)}, u32[]{:S(2)}) collective-permute-start(bf16[128,1600]{0,1:T(8,128)(2,1)S(1)} %copy-done.80), channel_id=1, source_target_pairs={{6,0},{0,2},{2,4},{4,6},{7,1},{1,3},{3,5},{5,7},{14,8},{8,10},{10,... | collective-permute-start | bytes 1228808 | tf_op jit(solution)/shard_map/ppermute | solution.py:513
  35.9 29.7 %all-to-all-start.3 = ((bf16[4,32,2304]{2,1,0:T(8,128)(2,1)}), bf16[4,32,2304]{2,1,0:T(8,128)(2,1)S(1)}, u32[]{:S(2)}, u32[]{:S(2)}) async-start(bf16[4,32,2304]{2,1,0:T(8,128)(2,1)} %copy.138), calls=%async_computation.3 | async-start | bytes 1179648 | tf_op jit(solution)/shard_map/all_to_all | solution.py:733
  39.4 216.1 %all-gather.8.cloned.1.call-start = ((), (), s32[]{:S(2)}) async-start(), calls=%async_computation.13 | async-start | bytes 10027008 | tf_op jit(solution)/shard_map/all_gather | solution.py:738
  44.7 20.1 %collective-permute-start.1 = (bf16[128,1600]{0,1:T(8,128)(2,1)S(1)}, bf16[128,1600]{0,1:T(8,128)(2,1)S(1)}, u32[]{:S(2)}, u32[]{:S(2)}) collective-permute-start(bf16[128,1600]{0,1:T(8,128)(2,1)S(1)} %copy-done.80), channel_id=1, source_target_pairs={{4,0},{6,2},{0,4},{2,6},{5,1},{7,3},{1,5},{3,7},{12,8},{14,10},{8,... | collective-permute-start | bytes 1228808 | tf_op jit(solution)/shard_map/ppermute | solution.py:513
  49.7 30.5 %collective-permute-start.6 = (bf16[4,64,2048]{2,1,0:T(8,128)(2,1)}, bf16[4,64,2048]{2,1,0:T(8,128)(2,1)}, u32[]{:S(2)}, u32[]{:S(2)}) collective-permute-start(bf16[4,64,2048]{2,1,0:T(8,128)(2,1)} %pad_maximum_fusion.2.own_ref), channel_id=1, source_target_pairs={{0,1},{1,0},{2,3},{3,2},{4,5},{5,4},{6,7},{7,6},{8,9},{9,8},{10,11... | collective-permute-start | bytes 3145736 | tf_op jit(solution)/shard_map/ppermute | solution.py:508
  130.5 15.8 %collective-permute-start.16 = (bf16[128,1120]{1,0:T(8,128)(2,1)S(1)}, bf16[128,1120]{1,0:T(8,128)(2,1)}, u32[]{:S(2)}, u32[]{:S(2)}) collective-permute-start(bf16[128,1120]{1,0:T(8,128)(2,1)S(1)} %copy.133), channel_id=1, source_target_pairs={{0,1},{1,0},{2,3},{3,2},{4,5},{5,4},{6,7},{7,6},{8,9},{9,8},{10,11... | collective-permute-start | bytes 860168 | tf_op jit(solution)/shard_map/ppermute | solution.py:508
  138.3 30.5 %all-to-all-start.1 = ((f32[16,17,512]{2,1,0:T(8,128)}), f32[16,17,512]{2,1,0:T(8,128)}, u32[]{:S(2)}, u32[]{:S(2)}) async-start(f32[16,17,512]{2,1,0:T(8,128)} %broadcast_in_dim.167), calls=%async_computation.1 | async-start | bytes 1572864 | tf_op jit(solution)/shard_map/all_to_all | solution.py:596
  146.3 332.6 %reduce-scatter.6.cloned.1.call-start = ((), (), s32[]{:S(2)}) async-start(), calls=%async_computation.15 | async-start | bytes 2359296 | tf_op jit(solution)/shard_map/reduce_scatter | solution.py:994
  150.8 14.1 %collective-permute-start.17 = (bf16[128,320]{1,0:T(8,128)(2,1)S(1)}, bf16[128,320]{1,0:T(8,128)(2,1)S(1)}, u32[]{:S(2)}, u32[]{:S(2)}) collective-permute-start(bf16[128,320]{1,0:T(8,128)(2,1)S(1)} %constant_dynamic-slice_fusion.4), channel_id=1, source_target_pairs={{0,16},{8,24},{16,32},{24,40},{32,48},{40,56},{48,64},{56,72},{64,... | collective-permute-start | bytes 245768 | tf_op jit(solution)/shard_map/ppermute | solution.py:627
  165.8 14.9 %collective-permute-start.19 = (bf16[256,320]{1,0:T(8,128)(2,1)}, bf16[256,320]{1,0:T(8,128)(2,1)}, u32[]{:S(2)}, u32[]{:S(2)}) collective-permute-start(bf16[256,320]{1,0:T(8,128)(2,1)} %pad_maximum_fusion.13), channel_id=1, source_target_pairs={{0,6},{2,0},{4,2},{6,4},{1,7},{3,1},{5,3},{7,5},{8,14},{10,8},{12,... | collective-permute-start | bytes 491528 | tf_op jit(solution)/shard_map/ppermute | solution.py:641
  167.1 14.6 %collective-permute-start.20 = (bf16[256,320]{1,0:T(8,128)(2,1)}, bf16[256,320]{1,0:T(8,128)(2,1)}, u32[]{:S(2)}, u32[]{:S(2)}) collective-permute-start(bf16[256,320]{1,0:T(8,128)(2,1)} %pad_maximum_fusion.14), channel_id=1, source_target_pairs={{0,4},{2,6},{4,0},{6,2},{1,5},{3,7},{5,1},{7,3},{8,12},{10,14},{12... | collective-permute-start | bytes 491528 | tf_op jit(solution)/shard_map/ppermute | solution.py:641
  168.8 13.9 %collective-permute-start.21 = (bf16[256,320]{1,0:T(8,128)(2,1)}, bf16[256,320]{1,0:T(8,128)(2,1)}, u32[]{:S(2)}, u32[]{:S(2)}) collective-permute-start(bf16[256,320]{1,0:T(8,128)(2,1)} %pad_maximum_fusion.15), channel_id=1, source_target_pairs={{0,2},{2,4},{4,6},{6,0},{1,3},{3,5},{5,7},{7,1},{8,10},{10,12},{12... | collective-permute-start | bytes 491528 | tf_op jit(solution)/shard_map/ppermute | solution.py:641
  193.2 14.1 %collective-permute-start.12 = (bf16[4,64,2048]{2,1,0:T(8,128)(2,1)}, bf16[4,64,2048]{2,1,0:T(8,128)(2,1)}, u32[]{:S(2)}, u32[]{:S(2)}) collective-permute-start(bf16[4,64,2048]{2,1,0:T(8,128)(2,1)} %fusion.58), channel_id=1, source_target_pairs={{0,1},{1,0},{2,3},{3,2},{4,5},{5,4},{6,7},{7,6},{8,9},{9,8},{10,11... | collective-permute-start | bytes 3145736 | tf_op jit(solution)/shard_map/ppermute | solution.py:508
  269.0 209.9 %reduce-scatter.4.cloned.1.call-start = ((), (), s32[]{:S(2)}) async-start(), calls=%async_computation.14 | async-start | bytes 10027008 | tf_op jit(solution)/shard_map/reduce_scatter | solution.py:742
  283.7 18.5 %collective-permute-start.31 = (bf16[64,2048]{1,0:T(8,128)(2,1)}, bf16[64,2048]{1,0:T(8,128)(2,1)}, u32[]{:S(2)}, u32[]{:S(2)}) collective-permute-start(bf16[64,2048]{1,0:T(8,128)(2,1)} %get-tuple-element.211), channel_id=1, source_target_pairs={{0,4},{2,6},{4,0},{6,2},{1,5},{3,7},{5,1},{7,3},{8,12},{10,14},{12... | collective-permute-start | bytes 786440 | tf_op jit(solution)/shard_map/ppermute | solution.py:544
  358.6 23.4 %all-to-all-start.4 = ((f32[16,17,512]{2,1,0:T(8,128)}), f32[16,17,512]{2,1,0:T(8,128)}, u32[]{:S(2)}, u32[]{:S(2)}) async-start(f32[16,17,512]{2,1,0:T(8,128)} %broadcast_in_dim.180), calls=%async_computation.4 | async-start | bytes 1572864 | tf_op jit(solution)/shard_map/all_to_all | solution.py:596
  365.7 45.7 %collective-permute-start.43 = (bf16[1152,320]{0,1:T(8,128)(2,1)}, bf16[1152,320]{0,1:T(8,128)(2,1)}, u32[]{:S(2)}, u32[]{:S(2)}) collective-permute-start(bf16[1152,320]{0,1:T(8,128)(2,1)} %copy.142), channel_id=1, source_target_pairs={{0,1},{1,0},{2,3},{3,2},{4,5},{5,4},{6,7},{7,6},{8,9},{9,8},{10,11... | collective-permute-start | bytes 2211848 | tf_op jit(solution)/shard_map/ppermute | solution.py:508
  443.9 20.9 %all-to-all-start.5 = ((bf16[4,128,640]{1,2,0:T(8,128)(2,1)}), bf16[4,128,640]{1,2,0:T(8,128)(2,1)}, u32[]{:S(2)}, u32[]{:S(2)}) async-start(bf16[4,128,640]{1,2,0:T(8,128)(2,1)} %fusion.67), calls=%async_computation.5 | async-start | bytes 1310720 | tf_op jit(solution)/shard_map/all_to_all | solution.py:733
  448.0 165.8 %reduce-scatter.8.cloned.1.call-start = ((), (), s32[]{:S(2)}) async-start(), calls=%async_computation.16 | async-start | bytes 7241728 | tf_op jit(solution)/shard_map/reduce_scatter | solution.py:742
  449.6 15.1 %collective-permute-start.39 = (bf16[132,512]{1,0:T(8,128)(2,1)S(1)}, bf16[132,512]{1,0:T(8,128)(2,1)S(1)}, u32[]{:S(2)}, u32[]{:S(2)}) collective-permute-start(bf16[132,512]{1,0:T(8,128)(2,1)S(1)} %fusion.130), channel_id=1, source_target_pairs={{4,0},{6,2},{0,4},{2,6},{5,1},{7,3},{1,5},{3,7},{12,8},{14,10},{8,... | collective-permute-start | bytes 405512 | tf_op jit(solution)/shard_map/ppermute | solution.py:513
  505.9 14.6 %collective-permute-start.53 = (bf16[4,64,2048]{2,1,0:T(8,128)(2,1)}, bf16[4,64,2048]{2,1,0:T(8,128)(2,1)}, u32[]{:S(2)}, u32[]{:S(2)}) collective-permute-start(bf16[4,64,2048]{2,1,0:T(8,128)(2,1)} %fusion.60), channel_id=1, source_target_pairs={{0,1},{1,0},{2,3},{3,2},{4,5},{5,4},{6,7},{7,6},{8,9},{9,8},{10,11... | collective-permute-start | bytes 3145736 | tf_op jit(solution)/shard_map/ppermute | solution.py:508
  510.8 14.8 %collective-permute-start.50 = (bf16[64,1600]{1,0:T(8,128)(2,1)}, bf16[64,1600]{1,0:T(8,128)(2,1)}, u32[]{:S(2)}, u32[]{:S(2)}) collective-permute-start(bf16[64,1600]{1,0:T(8,128)(2,1)} %fusion.28), channel_id=1, source_target_pairs={{0,1},{1,0},{2,3},{3,2},{4,5},{5,4},{6,7},{7,6},{8,9},{9,8},{10,11... | collective-permute-start | bytes 614408 | tf_op jit(solution)/shard_map/ppermute | solution.py:508
  510.9 49.6 %all-to-all-start.6 = ((bf16[16,145,512]{2,1,0:T(8,128)(2,1)}), bf16[16,145,512]{2,1,0:T(8,128)(2,1)S(1)}, u32[]{:S(2)}, u32[]{:S(2)}) async-start(bf16[16,145,512]{2,1,0:T(8,128)(2,1)} %pad_maximum_fusion), calls=%async_computation.8 | async-start | bytes 4980736 | tf_op jit(solution)/shard_map/all_to_all | solution.py:596
  560.9 15.1 %collective-permute-start.65 = (bf16[32,512]{1,0:T(8,128)(2,1)S(1)}, bf16[32,512]{1,0:T(8,128)(2,1)S(1)}, u32[]{:S(2)}, u32[]{:S(2)}) collective-permute-start(bf16[32,512]{1,0:T(8,128)(2,1)S(1)} %get-tuple-element.291), channel_id=1, source_target_pairs={{0,2},{2,4},{4,6},{6,0},{1,3},{3,5},{5,7},{7,1},{8,10},{10,12},{12... | collective-permute-start | bytes 98312 | tf_op jit(solution)/shard_map/ppermute | solution.py:604
  561.0 15.0 %collective-permute-start.64 = (bf16[32,512]{1,0:T(8,128)(2,1)S(1)}, bf16[32,512]{1,0:T(8,128)(2,1)S(1)}, u32[]{:S(2)}, u32[]{:S(2)}) collective-permute-start(bf16[32,512]{1,0:T(8,128)(2,1)S(1)} %get-tuple-element.293), channel_id=1, source_target_pairs={{0,4},{2,6},{4,0},{6,2},{1,5},{3,7},{5,1},{7,3},{8,12},{10,14},{12... | collective-permute-start | bytes 98312 | tf_op jit(solution)/shard_map/ppermute | solution.py:604
  564.9 37.2 %all-to-all-start.7 = ((bf16[64,21,512]{2,1,0:T(8,128)(2,1)}), bf16[64,21,512]{2,1,0:T(8,128)(2,1)S(1)}, u32[]{:S(2)}, u32[]{:S(2)}) async-start(bf16[64,21,512]{2,1,0:T(8,128)(2,1)} %broadcast_in_dim.187), calls=%async_computation.9 | async-start | bytes 3145728 | tf_op jit(solution)/shard_map/all_to_all | solution.py:596
  (191 other events, 1998.2 us)
Sparse Core Ops, SparseCore 0:
  25.1 70.1 all-gather.3
  98.2 76.5 all-gather.5
  177.5 77.9 all-gather.7
  269.1 36.2 reduce-scatter.5
  308.8 102.6 reduce-scatter.3
  479.1 123.5 reduce-scatter.7
